TPU v7x, 256 devices: a whole 4x4x8 slice. The times are simulated.
256 devices in a mesh: sample: 8 (over z), space: 32 (over y, x, core).
Axes of the slice: x: 4, y: 4, z: 8, core: 2. Of those that a mesh axis runs over, the one named last changes fastest.
Arguments:
- volume: bfloat16 [256, 8, 4, 16, 128], P(('sample', 'space')), may hold values from -6 to 6
- grad_out: bfloat16 [256, 1, 2, 16, 128], P(('sample', 'space')), may hold values from -6 to 6
- filter_one: bfloat16 [3, 3, 3, 4, 32], replicated, may hold values from -0.625 to 0.625
- filter_two: bfloat16 [3, 3, 3, 32, 64], replicated, may hold values from -0.21875 to 0.21875
- filter_three: bfloat16 [3, 3, 3, 64, 128], replicated, may hold values from -0.15625 to 0.15625
Outputs:
- grad_one: float32 [3, 3, 3, 4, 32], replicated
- grad_two: float32 [3, 3, 3, 32, 64], replicated
- grad_three: float32 [3, 3, 3, 64, 128], replicated
All inputs are finite; a program needn't handle non-finite values.
Results may differ from a plain program's by a relative error of at most 0.011.
Values may be sent and summed in bfloat16 or wider, within the bound.
No kernel may reach another device: no remote copies, remote signals or barrier semaphores. Data moves between devices by JAX's collectives and lax.ppermute only.
A program may use at most 128 MiB of HBM per device.

v0:
```python
import jax
import jax.numpy as jnp
from jax import lax
from jax.sharding import PartitionSpec as P


def padded_2(shard, sides, width):
    for axis, dim in sides:
        size, length = (lax.axis_size(axis), shard.shape[dim])
        up = [(i, (i + 1) % size) for i in range(size - 1)]
        down = [(j, i) for i, j in up]
        last = lax.slice_in_dim(shard, length - width, length, axis=dim)
        initial = lax.slice_in_dim(shard, 0, width, axis=dim)
        before = lax.ppermute(last, axis, up)
        after = lax.ppermute(initial, axis, down)
        shard = jnp.concatenate([before, shard, after], axis=dim)
    return shard


def convolve(inputs, kernel, spec, padding):
    return lax.conv_general_dilated(
        inputs,
        kernel,
        (1, 1, 1),
        padding,
        dimension_numbers=(spec, "DHWIO", "NDHWC"),
        preferred_element_type=jnp.float32,
    )


def reverse_kernel(kernel):
    return jnp.transpose(kernel[::-1, ::-1, ::-1], (0, 1, 2, 4, 3))


def pooled(values):
    nb, dd, hh, ww, cc = values.shape
    return values.reshape(nb, dd // 2, 2, hh // 2, 2, ww // 2, 2, cc).mean(axis=(2, 4, 6))


def expand(values):
    values = jnp.repeat(jnp.repeat(jnp.repeat(values, 2, axis=1), 2, axis=2), 2, axis=3)
    return values * 0.125


def slope(values):
    sig = jax.nn.sigmoid(values)
    return sig * (1.0 + values * (1.0 - sig))


def filter_grad(padded, delta, form):
    depth, rows, cols = (delta.shape[1], delta.shape[2], delta.shape[3])
    blocks = []
    for off_d in range(3):
        for off_h in range(3):
            for off_w in range(3):
                if form == "last":
                    piece = padded[
                        :, off_d : off_d + depth, off_h : off_h + rows, off_w : off_w + cols, :
                    ]
                    blocks.append(
                        jnp.einsum(
                            "ndhwi,ndhwo->io", piece, delta, preferred_element_type=jnp.float32
                        )
                    )
                else:
                    piece = padded[
                        :, off_d : off_d + depth, :, off_h : off_h + rows, off_w : off_w + cols
                    ]
                    blocks.append(
                        jnp.einsum(
                            "ndihw,ndhwo->io", piece, delta, preferred_element_type=jnp.float32
                        )
                    )
    stacked = jnp.stack(blocks)
    return stacked.reshape(3, 3, 3, stacked.shape[1], stacked.shape[2])


def with_rims(values, first_block, last_block):
    extended = padded_2(values, (("space", 1),), 1)
    lower = jnp.where(first_block, jnp.zeros_like(extended[:, :1]), extended[:, :1])
    upper = jnp.where(last_block, jnp.zeros_like(extended[:, -1:]), extended[:, -1:])
    return jnp.concatenate([lower, extended[:, 1:-1], upper], axis=1)


def per_device(volume, grad_out, filter_one, filter_two, filter_three):
    devices = lax.axis_size("space")
    place = lax.axis_index("space")
    first_block = place == 0
    last_block = place == devices - 1
    inner_pad = [(0, 0), (1, 1), (1, 1)]
    vol_ext = with_rims(volume, first_block, last_block)
    z_one = convolve(vol_ext, filter_one, "NDCHW", inner_pad)
    p_one = pooled(jax.nn.silu(z_one)).astype(jnp.bfloat16)
    p_one_ext = with_rims(p_one, first_block, last_block)
    z_two = convolve(p_one_ext, filter_two, "NDHWC", inner_pad)
    p_two = pooled(jax.nn.silu(z_two)).astype(jnp.bfloat16)
    p_two_ext = with_rims(p_two, first_block, last_block)
    z_three = convolve(p_two_ext, filter_three, "NDHWC", inner_pad)
    d_three = (expand(grad_out.astype(jnp.float32)) * slope(z_three)).astype(jnp.bfloat16)
    g_three = filter_grad(
        jnp.pad(p_two_ext, ((0, 0), (0, 0), (1, 1), (1, 1), (0, 0))), d_three, "last"
    )
    d_three_ext = with_rims(d_three, first_block, last_block)
    q_two = convolve(d_three_ext, reverse_kernel(filter_three), "NDHWC", inner_pad).astype(
        jnp.bfloat16
    )
    d_two = (expand(q_two.astype(jnp.float32)) * slope(z_two)).astype(jnp.bfloat16)
    g_two = filter_grad(jnp.pad(p_one_ext, ((0, 0), (0, 0), (1, 1), (1, 1), (0, 0))), d_two, "last")
    d_two_ext = with_rims(d_two, first_block, last_block)
    q_one = convolve(d_two_ext, reverse_kernel(filter_two), "NDHWC", inner_pad)
    d_one = (expand(q_one) * slope(z_one)).astype(jnp.bfloat16)
    g_one = filter_grad(jnp.pad(vol_ext, ((0, 0), (0, 0), (0, 0), (1, 1), (1, 1))), d_one, "first")
    cells = float(
        lax.axis_size("sample") * devices * volume.shape[1] * volume.shape[3] * volume.shape[4]
    )
    totals = lax.psum((g_one, g_two, g_three), ("sample", "space"))
    return (
        totals[0] / jnp.sqrt(jnp.float32(cells)),
        totals[1] / jnp.sqrt(jnp.float32(cells / 8.0)),
        totals[2] / jnp.sqrt(jnp.float32(cells / 64.0)),
    )


def solution(mesh):
    return jax.shard_map(
        per_device,
        mesh=mesh,
        in_specs=(
            P(("sample", "space"), None, None, None, None),
            P(("sample", "space"), None, None, None, None),
            P(),
            P(),
            P(),
        ),
        out_specs=(P(), P(), P()),
        check_vma=False,
    )
```

profile of v0, /device:TPU:1, one launch (start us, length us, event | category | flops | bytes accessed | tf_op | source)
XLA Modules:
  0.0 404.8 jit_solution(2037019577987577131)
XLA Ops:
  7.2 1.0 copy.233
  8.3 4.5 %collective-permute-start = (bf16[1,1,4,16,128]{4,2,3,1,0:T(4,128)(2,1)S(1)}, bf16[1,1,4,16,128]{4,2,3,1,0:T(4,128)(2,1)S(1)}, u32[]{:S(2)}, u32[]{:S(2)}) collective-permute-start(bf16[1,1,4,16,128]{4,2,3,1,0:T(4,128)(2,1)S(1)} %get-tuple-element.19), channel_id=1, source_target_pairs={{0,1},{1,2},{2,3},{3,4},{4,5},{5,6},{6,7},{7,8},{8,9},{9,10},{10,1... | collective-permute-start | bytes 49160 | tf_op jit(solution)/shard_map/ppermute | solution.py:14
  12.8 1.9 collective-permute-start.1
  14.7 3.1 collective-permute-done.1
  18.2 1.0 reshape.711
  19.2 5.2 %copy.239 = bf16[10,4,16,1,8,17]{4,1,5,2,0,3:T(4,128)(2,1)} copy(bf16[10,4,16,1,8,17]{5,4,1,2,0,3:T(8,128)(2,1)S(1)} %reshape.711) | data formatting | bytes 348160 | tf_op jit(solution)/shard_map/conv_general_dilated | solution.py:21
  24.4 1.2 slice.384
  25.7 24.3 %add_multiply_fusion = (f32[8,16,8,17,32]{4,2,3,1,0:T(8,128)}, f32[8,16,8,17,32]{4,2,3,1,0:T(8,128)S(1)}) fusion(pred[8,17]{0,1:T(8,128)(4,1)S(1)} %copy-done.13, bf16[3,3,3,4,32]{4,3,2,1,0:T(4,128)(2,1)S(1)} %copy-done.12, bf16[10,4,16,1,7,2]{4,1,5,2,0,3:T(4,128)(2,1)S(1)} %slice.384, bf16[10,4,16,1,8,17]{4,1,5,2,0,3:T(4,128)(2,1)} %copy.239), kind=kOutput, calls=%fused_computation | convolution fusion | flops 120907776 | bytes 4655496 | tf_op jit(solution)/shard_map/conv_general_dilated | solution.py:21
  50.0 1.6 copy.240
  51.6 4.1 %slice.385 = f32[8,16,1,128,32]{4,1,3,0,2:T(8,128)} slice(f32[8,16,1,136,32]{4,1,3,0,2:T(8,128)S(1)} %bitcast.1033), slice={[0:8], [0:16], [0:1], [0:128], [0:32]} | slice | bytes 4194304 | tf_op jit(solution)/shard_map/jit(silu)/mul | solution.py:93
  55.7 9.7 %reduce_sum.18 = f32[4,8,64,32]{3,1,2,0:T(8,128)S(1)} reduce(f32[4,2,8,2,64,2,32]{6,3,2,5,4,1,0:T(2,128)} %bitcast.1035, f32[]{:T(128)} %constant.16.clone.1), dimensions={1,3,5}, to_apply=%region_0.1 | reduce | flops 458752 | bytes 2359300 | tf_op jit(solution)/shard_map/reduce_sum | solution.py:37
  65.8 1.9 collective-permute-start.2
  67.8 2.6 collective-permute-start.3
  70.4 2.9 collective-permute-done.3
  73.5 1.3 copy.426
  74.8 1.3 pad.17.clone
  76.3 3.6 add_multiply_fusion.1
  80.2 0.9 reduce_sum.19
  81.2 1.9 collective-permute-start.4
  83.2 8.7 %copy.258 = f32[8,16,8,17,32]{4,1,3,2,0:T(8,128)} copy(f32[8,16,8,17,32]{4,2,3,1,0:T(8,128)} %get-tuple-element.5) | data formatting | bytes 4456448 | tf_op jit(solution)/shard_map/mul | solution.py:47
  92.1 2.4 collective-permute-start.5
  94.6 2.8 collective-permute-done.5
  97.6 0.5 add_multiply_fusion.2
  98.3 1.9 collective-permute-start.6
  100.3 2.4 collective-permute-start.7
  108.0 0.7 fusion.19
  109.2 0.7 fusion.456
  109.9 4.5 %collective-permute-start.8 = (bf16[1,1,8,64,64]{4,2,3,1,0:T(8,128)(2,1)}, bf16[1,1,8,64,64]{4,2,3,1,0:T(8,128)(2,1)S(1)}, u32[]{:S(2)}, u32[]{:S(2)}) collective-permute-start(bf16[1,1,8,64,64]{4,2,3,1,0:T(8,128)(2,1)} %get-tuple-element.9), channel_id=1, source_target_pairs={{0,1},{1,2},{2,3},{3,4},{4,5},{5,6},{6,7},{7,8},{8,9},{9,10},{10,1... | collective-permute-start | bytes 196616 | tf_op jit(solution)/shard_map/ppermute | solution.py:14
  114.4 2.3 collective-permute-start.9
  125.5 0.8 copy-done.3
  126.9 0.6 copy-done.11
  127.5 4.6 %fusion.15 = f32[4,8,8,9,32]{4,2,3,1,0:T(8,128)S(1)} fusion(bf16[3,3,3,32,64]{4,3,2,1,0:T(8,128)(2,1)S(1)} %copy-done.11, bf16[6,8,1,7,2,64]{5,3,4,1,0,2:T(8,128)(2,1)S(1)} %slice.401, bf16[6,8,1,8,9,64]{5,3,4,1,0,2:T(8,128)(2,1)S(1)} %copy.256, pred[8,9]{0,1:T(8,128)(4,1)S(1)} %copy-done.14), kind=kOutput, calls=%fused_computation.21 | convolution fusion | flops 235339776 | bytes 933960 | tf_op jit(solution)/shard_map/conv_general_dilated | solution.py:21
  132.5 1.6 broadcast_in_dim.34
  134.2 4.0 broadcast_in_dim.35
  138.1 8.8 %fusion.4 = bf16[8,16,128,32]{3,1,2,0:T(8,128)(2,1)} fusion(f32[1,8,16,128,32]{4,2,3,1,0:T(8,128)} %bitcast.1034, f32[8,16,1,136,32]{4,1,3,0,2:T(8,128)} %bitcast.1032), kind=kLoop, calls=%fused_computation.8 | loop fusion | flops 1048576 | bytes 5242880 | tf_op jit(solution)/shard_map/reshape.9
  147.0 4.8 %copy.259 = bf16[8,16,128,32]{2,3,1,0:T(8,128)(2,1)S(1)} copy(bf16[8,16,128,32]{3,1,2,0:T(8,128)(2,1)} %fusion.4) | data formatting | bytes 2097152 | tf_op jit(solution)/shard_map/reshape.9
  153.1 0.5 fusion.97
  154.0 0.5 fusion.95
  155.3 0.5 fusion.92
  158.0 0.5 fusion.86
  159.4 0.5 fusion.83
  162.0 0.5 fusion.77
  163.4 0.5 fusion.74
  163.9 88.9 %psum.21 = f32[3,3,3,4,32]{4,3,2,1,0:T(4,128)S(1)} all-reduce(f32[3,3,3,4,32]{4,3,2,1,0:T(4,128)S(1)} %bitcast.1056), channel_id=1, replica_groups=mesh['sample'=8,'space'=32] {'sample','space'}, use_global_device_ids=true, to_apply=%region_2.3 | all-reduce | flops 3456 | bytes 27648 | tf_op jit(solution)/shard_map/psum | solution.py:116
  252.7 0.6 broadcast_multiply_fusion.2
  253.4 140.4 %all-reduce.6.cloned.1.call-done = (f32[3,3,3,32,64]{4,3,2,1,0:T(8,128)}, f32[3,3,3,64,128]{4,3,2,1,0:T(8,128)}) async-done(((f32[3,3,3,32,64]{4,3,2,1,0:T(8,128)}, f32[3,3,3,64,128]{4,3,2,1,0:T(8,128)}), (f32[3,3,3,32,64]{4,3,2,1,0:T(8,128)}, f32[3,3,3,64,128]{4,3,2,1,0:T(8,128)})) %all-reduce.6.cloned.1.call-update) | async-done | bytes 1105936 | tf_op jit(solution)/shard_map/psum | solution.py:116
  393.8 1.8 broadcast_multiply_fusion.1
  395.6 2.2 broadcast_multiply_fusion
  (167 shorter events, 26.2 us)
Async XLA Ops:
  7.2 90.5 %copy-start = (bf16[3,3,3,64,128]{4,3,2,1,0:T(8,128)(2,1)S(1)}, bf16[3,3,3,64,128]{4,3,2,1,0:T(8,128)(2,1)}, u32[]{:S(2)}) copy-start(bf16[3,3,3,64,128]{4,3,2,1,0:T(8,128)(2,1)} %param.9) | copy-start | bytes 1327108
  7.2 386.6 %all-reduce.6.cloned.1.call-start = ((), (), s32[]{:S(2)}) async-start(), calls=%async_computation | async-start | bytes 2654208 | tf_op jit(solution)/shard_map/psum | solution.py:116
  8.3 6.5 %collective-permute-start = (bf16[1,1,4,16,128]{4,2,3,1,0:T(4,128)(2,1)S(1)}, bf16[1,1,4,16,128]{4,2,3,1,0:T(4,128)(2,1)S(1)}, u32[]{:S(2)}, u32[]{:S(2)}) collective-permute-start(bf16[1,1,4,16,128]{4,2,3,1,0:T(4,128)(2,1)S(1)} %get-tuple-element.19), channel_id=1, source_target_pairs={{0,1},{1,2},{2,3},{3,4},{4,5},{5,6},{6,7},{7,8},{8,9},{9,10},{10,1... | collective-permute-start | bytes 49160 | tf_op jit(solution)/shard_map/ppermute | solution.py:14
  12.8 5.1 %collective-permute-start.1 = (bf16[1,1,4,16,128]{4,2,3,1,0:T(4,128)(2,1)S(1)}, bf16[1,1,4,16,128]{4,2,3,1,0:T(4,128)(2,1)S(1)}, u32[]{:S(2)}, u32[]{:S(2)}) collective-permute-start(bf16[1,1,4,16,128]{4,2,3,1,0:T(4,128)(2,1)S(1)} %get-tuple-element.20), channel_id=1, source_target_pairs={{1,0},{2,1},{3,2},{4,3},{5,4},{6,5},{7,6},{8,7},{9,8},{10,9},{11,1... | collective-permute-start | bytes 49160 | tf_op jit(solution)/shard_map/ppermute | solution.py:15
  19.2 6.5 %copy-start.12 = (bf16[3,3,3,4,32]{4,3,2,1,0:T(4,128)(2,1)S(1)}, bf16[3,3,3,4,32]{4,3,2,1,0:T(4,128)(2,1)}, u32[]{:S(2)}) copy-start(bf16[3,3,3,4,32]{4,3,2,1,0:T(4,128)(2,1)} %param.7) | copy-start | bytes 20740
  19.2 6.5 %copy-start.13 = (pred[8,17]{0,1:T(8,128)(4,1)S(1)}, pred[8,17]{0,1:T(8,128)(4,1)}, u32[]{:S(2)}) copy-start(pred[8,17]{0,1:T(8,128)(4,1)} %constant.74) | copy-start | bytes 412
  65.4 2.4 copy-start.9
  65.8 4.6 %collective-permute-start.2 = (bf16[1,1,8,64,32]{3,4,2,1,0:T(8,128)(2,1)S(1)}, bf16[1,1,8,64,32]{3,4,2,1,0:T(8,128)(2,1)S(1)}, u32[]{:S(2)}, u32[]{:S(2)}) collective-permute-start(bf16[1,1,8,64,32]{3,4,2,1,0:T(8,128)(2,1)S(1)} %get-tuple-element.13), channel_id=1, source_target_pairs={{0,1},{1,2},{2,3},{3,4},{4,5},{5,6},{6,7},{7,8},{8,9},{9,10},{10,1... | collective-permute-start | bytes 98312 | tf_op jit(solution)/shard_map/ppermute | solution.py:14
  67.8 5.6 %collective-permute-start.3 = (bf16[1,1,8,64,32]{3,4,2,1,0:T(8,128)(2,1)S(1)}, bf16[1,1,8,64,32]{3,4,2,1,0:T(8,128)(2,1)S(1)}, u32[]{:S(2)}, u32[]{:S(2)}) collective-permute-start(bf16[1,1,8,64,32]{3,4,2,1,0:T(8,128)(2,1)S(1)} %get-tuple-element.14), channel_id=1, source_target_pairs={{1,0},{2,1},{3,2},{4,3},{5,4},{6,5},{7,6},{8,7},{9,8},{10,9},{11,1... | collective-permute-start | bytes 98312 | tf_op jit(solution)/shard_map/ppermute | solution.py:15
  70.4 5.8 %copy-start.6 = (bf16[1,1,8,64,32]{3,4,2,1,0:T(8,128)(2,1)}, bf16[1,1,8,64,32]{3,4,2,1,0:T(8,128)(2,1)S(1)}, u32[]{:S(2)}) copy-start(bf16[1,1,8,64,32]{3,4,2,1,0:T(8,128)(2,1)S(1)} %broadcast_select_fusion.3) | copy-start | bytes 98308
  73.4 2.9 copy-start.4
  74.8 1.5 copy-start.10
  74.8 1.6 copy-start.14
  81.2 13.4 %collective-permute-start.4 = (bf16[1,1,4,32,64]{4,3,2,1,0:T(8,128)(2,1)S(1)}, bf16[1,1,4,32,64]{4,3,2,1,0:T(8,128)(2,1)S(1)}, u32[]{:S(2)}, u32[]{:S(2)}) collective-permute-start(bf16[1,1,4,32,64]{4,3,2,1,0:T(8,128)(2,1)S(1)} %get-tuple-element.23), channel_id=1, source_target_pairs={{0,1},{1,2},{2,3},{3,4},{4,5},{5,6},{6,7},{7,8},{8,9},{9,10},{10,1... | collective-permute-start | bytes 49160 | tf_op jit(solution)/shard_map/ppermute | solution.py:14
  83.2 8.7 %copy-start.1 = (f32[4,8,8,9,64]{4,2,3,1,0:T(8,128)S(1)}, f32[4,8,8,9,64]{4,2,3,1,0:T(8,128)}, u32[]{:S(2)}) copy-start(f32[4,8,8,9,64]{4,2,3,1,0:T(8,128)} %get-tuple-element.7) | copy-start | bytes 1769476
  91.9 5.7 %copy-start.15 = (pred[8,5]{0,1:T(8,128)(4,1)S(1)}, pred[8,5]{0,1:T(8,128)(4,1)}, u32[]{:S(2)}) copy-start(pred[8,5]{0,1:T(8,128)(4,1)} %constant.71) | copy-start | bytes 124
  92.1 5.2 %collective-permute-start.5 = (bf16[1,1,4,32,64]{4,3,2,1,0:T(8,128)(2,1)S(1)}, bf16[1,1,4,32,64]{4,3,2,1,0:T(8,128)(2,1)S(1)}, u32[]{:S(2)}, u32[]{:S(2)}) collective-permute-start(bf16[1,1,4,32,64]{4,3,2,1,0:T(8,128)(2,1)S(1)} %get-tuple-element.24), channel_id=1, source_target_pairs={{1,0},{2,1},{3,2},{4,3},{5,4},{6,5},{7,6},{8,7},{9,8},{10,9},{11,1... | collective-permute-start | bytes 49160 | tf_op jit(solution)/shard_map/ppermute | solution.py:15
  98.3 9.3 %collective-permute-start.6 = (bf16[1,1,4,32,128]{4,2,3,1,0:T(4,128)(2,1)S(1)}, bf16[1,1,4,32,128]{4,2,3,1,0:T(4,128)(2,1)S(1)}, u32[]{:S(2)}, u32[]{:S(2)}) collective-permute-start(bf16[1,1,4,32,128]{4,2,3,1,0:T(4,128)(2,1)S(1)} %get-tuple-element.21), channel_id=1, source_target_pairs={{0,1},{1,2},{2,3},{3,4},{4,5},{5,6},{6,7},{7,8},{8,9},{9,10},{10,1... | collective-permute-start | bytes 98312 | tf_op jit(solution)/shard_map/ppermute | solution.py:14
  100.3 7.5 %collective-permute-start.7 = (bf16[1,1,4,32,128]{4,2,3,1,0:T(4,128)(2,1)S(1)}, bf16[1,1,4,32,128]{4,2,3,1,0:T(4,128)(2,1)S(1)}, u32[]{:S(2)}, u32[]{:S(2)}) collective-permute-start(bf16[1,1,4,32,128]{4,2,3,1,0:T(4,128)(2,1)S(1)} %get-tuple-element.22), channel_id=1, source_target_pairs={{1,0},{2,1},{3,2},{4,3},{5,4},{6,5},{7,6},{8,7},{9,8},{10,9},{11,1... | collective-permute-start | bytes 98312 | tf_op jit(solution)/shard_map/ppermute | solution.py:15
  107.7 1.4 copy-start.2
  109.2 8.9 %copy-start.7 = (bf16[1,1,8,64,32]{3,4,2,1,0:T(8,128)(2,1)S(1)}, bf16[1,1,8,64,32]{3,4,2,1,0:T(8,128)(2,1)}, u32[]{:S(2)}) copy-start(bf16[1,1,8,64,32]{3,4,2,1,0:T(8,128)(2,1)} %copy-done.6) | copy-start | bytes 98308
  109.9 16.4 %collective-permute-start.8 = (bf16[1,1,8,64,64]{4,2,3,1,0:T(8,128)(2,1)}, bf16[1,1,8,64,64]{4,2,3,1,0:T(8,128)(2,1)S(1)}, u32[]{:S(2)}, u32[]{:S(2)}) collective-permute-start(bf16[1,1,8,64,64]{4,2,3,1,0:T(8,128)(2,1)} %get-tuple-element.9), channel_id=1, source_target_pairs={{0,1},{1,2},{2,3},{3,4},{4,5},{5,6},{6,7},{7,8},{8,9},{9,10},{10,1... | collective-permute-start | bytes 196616 | tf_op jit(solution)/shard_map/ppermute | solution.py:14
  114.4 11.9 %collective-permute-start.9 = (bf16[1,1,8,64,64]{4,2,3,1,0:T(8,128)(2,1)S(1)}, bf16[1,1,8,64,64]{4,2,3,1,0:T(8,128)(2,1)S(1)}, u32[]{:S(2)}, u32[]{:S(2)}) collective-permute-start(bf16[1,1,8,64,64]{4,2,3,1,0:T(8,128)(2,1)S(1)} %get-tuple-element.10), channel_id=1, source_target_pairs={{1,0},{2,1},{3,2},{4,3},{5,4},{6,5},{7,6},{8,7},{9,8},{10,9},{11,1... | collective-permute-start | bytes 196616 | tf_op jit(solution)/shard_map/ppermute | solution.py:15
  122.2 1.7 copy-start.5
  125.5 0.8 copy-start.3
  126.5 0.9 copy-start.11
  155.8 1.8 copy-start.8
Sparse Core Ops, SparseCore 0:
  126.4 267.3 all-reduce.5
where the time goes:
time: 411 us; the launch traced here: 405 us
  waiting for transfers between devices  149 us (36%)
  blocking collectives  88.9 us (22%)
  matrix products  59.3 us (14%)
  local copies, waits for them, and re-layouts  40.6 us (10%)
  starting transfers between devices  26.5 us (6%)
  other arithmetic  25.1 us (6%)
  between operations  15.2 us (4%)
    psum x1, waiting for transfers between devices, per_device(): totals = lax.psum((g_one, g_two, g_three), ('sample', 'space'))  140 us
    psum x1, blocking collectives, per_device(): totals = lax.psum((g_one, g_two, g_three), ('sample', 'space'))  88.9 us
    conv_general_dilated x5, matrix products, convolve(): lax.conv_general_dilated(inputs, kernel, (1, 1, 1), padding, dimension_nu...  33.7 us
    ppermute x5, starting transfers between devices, padded_2(): before = lax.ppermute(last, axis, up)  14.8 us
    dot_general x54, matrix products, filter_grad(): jnp.einsum('ndhwi,ndhwo->io', piece, delta, preferred_element_type=jnp.fl...  13.5 us
    dot_general x27, matrix products, filter_grad(): jnp.einsum('ndihw,ndhwo->io', piece, delta, preferred_element_type=jnp.fl...  12.1 us
    ppermute x5, starting transfers between devices, padded_2(): after = lax.ppermute(initial, axis, down)  11.7 us
    reduce_sum x2, other arithmetic, pooled(): values.reshape(nb, dd // 2, 2, hh // 2, 2, ww // 2, 2, cc)  10.6 us
  transfers between devices with their start and end apart: 11, of which 4 were waited for; matrix products, arithmetic and copies ran while one was open for 15% of the time, Pallas kernels for 0%

commit v1 on v0

v1 whole, which is shorter than its diff:
```python
import jax
import jax.numpy as jnp
import numpy as np
from jax import lax
from jax.experimental import pallas as pl
from jax.experimental.pallas import tpu as pltpu
from jax.sharding import PartitionSpec as P

BF = jnp.bfloat16
F32 = jnp.float32
SLOT = 80


def one_hot_tables():
    def table(rows, cols):
        return np.zeros((rows, cols), np.float32)

    shift = table(128, 256)
    for w in range(128):
        if w >= 1:
            shift[w - 1, w] = 1.0
        if w + 1 < 128:
            shift[w + 1, 128 + w] = 1.0
    pair = table(256, 384)
    odd = table(256, 384)
    even = table(128, 384)
    for a in range(2):
        for kw in range(3):
            for w in range(64):
                src = w + kw - 1
                if 0 <= src < 64:
                    pair[128 * a + 2 * src, 128 * kw + 64 * a + w] = 1.0
                    odd[64 + 64 * a + src, 128 * kw + 64 * a + w] = 1.0
                    even[64 * a + src, 128 * kw + 64 * a + w] = 1.0
    squeeze = table(1024, 256)
    for m in range(8):
        for w in range(32):
            squeeze[128 * m + 2 * w, 32 * m + w] = 1.0
    spread3 = table(256, 2304)
    spread_b = table(256, 1152)
    for kd in range(3):
        for kw in range(3):
            at = 3 * kd + kw
            for w in range(32):
                src = w + kw - 1
                if 0 <= src < 32:
                    for n in range(6):
                        spread3[32 * (n + kd) + src, 256 * at + 32 * n + w] = 1.0
                    for n in range(4):
                        spread_b[32 * (n + kd) + src, 128 * at + 32 * n + w] = 1.0
    grow_g = table(48, 256)
    for b in range(3):
        for d in range(2):
            for w in range(32):
                grow_g[16 * b + w // 2, 32 * (2 * b + d) + w] = 1.0 / 16
    grow2 = table(128, 512)
    for n in range(4):
        for d in range(2):
            for w in range(64):
                grow2[32 * n + w // 2, 64 * (2 * n + d) + w] = 1.0 / 16
    grow1 = table(256, 512)
    for e in range(4):
        for w in range(128):
            grow1[64 * e + w // 2, 128 * e + w] = 1.0 / 16
    return [shift, pair, odd, even, squeeze, spread3, spread_b, grow_g, grow2, grow1]


def dot(a, b):
    return jnp.dot(a, b, preferred_element_type=F32)


def inside(index, count):
    return jnp.logical_and(index >= 0, index < count)


def body(
    place,
    vol_b2,
    vol_b1,
    vol_own,
    vol_a1,
    vol_a2,
    grad_own,
    base_one,
    filter_two,
    filter_three,
    shift,
    pair,
    odd,
    even,
    squeeze,
    spread3,
    spread_b,
    grow_g,
    grow2,
    grow1,
    out,
    t1,
    t2,
    t3,
    t3r,
    t2r,
    x1,
    pp,
    x2,
    q,
    x3,
    d3c,
    d2c,
    sl1,
    sl2,
    d2,
    d1,
    d2t,
    d3t,
):
    me = place[0]
    blocks = place[1]

    lane640 = lax.broadcasted_iota(jnp.int32, (32, 640), 1) % 16
    base = base_one[...]
    for h in range(16):
        moved = pltpu.roll(base, (h - 1) % 640, 1) if h != 1 else base
        if h == 0:
            moved = jnp.where(lane640 == 15, 0.0, moved)
        if h == 15:
            moved = jnp.where(lane640 == 0, 0.0, moved)
        t1[32 * h : 32 * h + 32, :] = moved[:, :576].astype(BF)

    def build(it, carry):
        kd = it // 3
        kw = it % 3
        taps = [kd * 9 + kh * 3 + kw for kh in range(3)]
        back = [(2 - kd) * 9 + (2 - kh) * 3 + (2 - kw) for kh in range(3)]
        w2 = [filter_two[k].astype(F32).T * 0.5 for k in taps]
        zero = jnp.zeros((64, 32), F32)
        for s in range(-6, 6):
            parts = [w2[s + j] if 0 <= s + j <= 2 else zero for j in range(4)]
            if -3 <= s <= 2:
                tile = jnp.concatenate(parts, axis=1).astype(BF)
            else:
                tile = jnp.zeros((64, 128), BF)
            for m in range(2):
                h = 4 * m + 1 - s
                if 0 <= h < 8:
                    t2[64 * h : 64 * h + 64, pl.ds(pl.multiple_of(it * 256 + 128 * m, 128), 128)] = tile
        w3 = [filter_three[k].astype(F32).T * 0.5 for k in taps]
        zero = jnp.zeros((128, 64), F32)
        for s in range(-2, 4):
            parts = [w3[s + j] if 0 <= s + j <= 2 else zero for j in range(2)]
            if -1 <= s <= 2:
                tile = jnp.concatenate(parts, axis=1).astype(BF)
            else:
                tile = jnp.zeros((128, 128), BF)
            for m in range(2):
                h = 2 * m + 1 - s
                if 0 <= h < 4:
                    t3[128 * h : 128 * h + 128, pl.ds(pl.multiple_of(it * 256 + 128 * m, 128), 128)] = tile
        v3 = [filter_three[k] for k in back]
        for hp in range(4):
            for h in range(4):
                kh = h - hp + 1
                tile = v3[kh] if 0 <= kh <= 2 else jnp.zeros((64, 128), BF)
                t3r[64 * hp : 64 * hp + 64, pl.ds(pl.multiple_of(it * 512 + 128 * h, 128), 128)] = tile
        v2 = [filter_two[k].astype(F32) for k in back]
        zero = jnp.zeros((32, 64), F32)
        for s in range(-6, 8):
            parts = [v2[s + j] if 0 <= s + j <= 2 else zero for j in range(2)]
            if -1 <= s <= 2:
                tile = jnp.concatenate(parts, axis=1).astype(BF)
            else:
                tile = jnp.zeros((32, 128), BF)
            for m in range(4):
                hp = 2 * m + 1 - s
                if 0 <= hp < 8:
                    t2r[32 * hp : 32 * hp + 32, pl.ds(pl.multiple_of(it * 512 + 128 * m, 128), 128)] = tile
        return carry

    lax.fori_loop(0, 9, build, 0)

    at = 0
    for ref, count in ((vol_b2, 7), (vol_b1, 8), (vol_own, 8), (vol_a1, 8), (vol_a2, 7)):
        rows = ref[: 64 * count, :]
        moved = dot(rows, shift[...]).astype(BF)
        for p in range(count):
            lanes = slice(128 * (at + p), 128 * (at + p) + 128)
            x1[0:64, lanes] = moved[64 * p : 64 * p + 64, :128]
            x1[64:128, lanes] = rows[64 * p : 64 * p + 64, :]
            x1[128:192, lanes] = moved[64 * p : 64 * p + 64, 128:]
        at += count

    def layer_one(j, own):
        rhs = jnp.concatenate(
            [x1[:, pl.ds(pl.multiple_of((2 * j + kd) * 128, 128), 256)] for kd in range(3)], axis=0
        )
        half = dot(t1[...], rhs)
        t = jnp.tanh(half)
        if own:
            slope = (1.0 + t) + half * (1.0 - t * t)
            sl1[:, pl.ds(pl.multiple_of((j - 7) * 256, 256), 256)] = slope.astype(BF)
        act = half + half * t
        act = act[:, :128] + act[:, 128:]
        act = act.reshape(8, 2, 32, 128)
        act = (act[:, 0] + act[:, 1]).reshape(256, 128)
        act = act + pltpu.roll(act, 127, 1)
        scale = jnp.where(inside(4 * me - 7 + j, 4 * blocks), 0.125, 0.0)
        pp[:, pl.ds(pl.multiple_of(j * 128, 128), 128)] = (act * scale).astype(BF)

    def loop_one(lo, hi, own):
        def step(j, carry):
            layer_one(j, own)
            return carry

        lax.fori_loop(lo, hi, step, 0)

    loop_one(0, 7, False)
    loop_one(7, 11, True)
    loop_one(11, 18, False)

    def gather_two(m, carry):
        for kd in range(3):
            got = dot(
                pp[:, pl.ds(pl.multiple_of((2 * m + kd) * 128, 128), 256)], pair[...]
            ).astype(BF)
            for kw in range(3):
                k = 3 * kd + kw
                x2[256 * k : 256 * k + 256, pl.ds(pl.multiple_of(m * 128, 128), 128)] = got[
                    :, 128 * kw : 128 * kw + 128
                ]
        return carry

    lax.fori_loop(0, 8, gather_two, 0)

    def layer_two(c, carry):
        lanes = pl.ds(pl.multiple_of(c * 256, 256), 256)
        half = dot(t2[...], x2[:, lanes])
        t = jnp.tanh(half)
        slope = (1.0 + t) + half * (1.0 - t * t)
        sl2[:, lanes] = slope.astype(BF)
        act = (half + half * t).reshape(4, 2, 64, 256)
        act = (act[:, 0] + act[:, 1]).reshape(256, 256)
        for u in range(2):
            tile = act[:, 128 * u : 128 * u + 128]
            tile = tile + pltpu.roll(tile, 64, 1)
            tile = tile + pltpu.roll(tile, 127, 1)
            m = 2 * c + u
            scale = jnp.where(inside(2 * me - 3 + m, 2 * blocks), 0.125, 0.0)
            q[:, pl.ds(pl.multiple_of(m * 128, 128), 128)] = (tile * scale).astype(BF)
        return carry

    lax.fori_loop(0, 4, layer_two, 0)

    packed = dot(q[...], squeeze[...]).astype(BF)
    for k in range(9):
        x3[256 * k : 256 * k + 256, :] = dot(
            packed, spread3[:, 256 * k : 256 * k + 256]
        ).astype(BF)
    half = dot(t3[...], x3[...])
    t = jnp.tanh(half)
    slope = (1.0 + t) + half * (1.0 - t * t)
    grown = []
    for hh in range(2):
        rows = jnp.concatenate(
            [
                vol_b1[512 + 16 * hh : 528 + 16 * hh, :],
                grad_own[16 * hh : 16 * hh + 16, :],
                vol_a1[512 + 16 * hh : 528 + 16 * hh, :],
            ],
            axis=0,
        )
        got = dot(rows.astype(F32).T.astype(BF), grow_g[...])
        grown += [got, got]
    delta = jnp.concatenate(grown, axis=0) * slope
    lane = lax.broadcasted_iota(jnp.int32, (512, 128), 1)
    d3t[...] = jnp.where(lane >= 64, delta[:, :128], 0.0).T.astype(BF)
    delta = delta.astype(BF)
    for k in range(9):
        d3c[512 * k : 512 * k + 512, :] = dot(
            delta, spread_b[:, 128 * k : 128 * k + 128]
        ).astype(BF)
    back = dot(t3r[...], d3c[...])
    lane = lax.broadcasted_iota(jnp.int32, (256, 128), 1)
    back = jnp.where(inside(2 * me - 1 + lane // 32, 2 * blocks), back, 0.0).astype(BF)
    back = dot(back, grow2[...])
    for h in range(8):
        rows = slice(64 * h, 64 * h + 64)
        delta = back[64 * (h // 2) : 64 * (h // 2) + 64, :] * sl2[rows, 256:768].astype(F32)
        d2t[:, rows] = delta[:, 128:384].T.astype(BF)
        d2[rows, :] = delta.astype(BF)

    for start in range(1, 6):
        u = start // 2
        if start % 2:
            got = dot(d2[:, 128 * u : 128 * u + 256], odd[...])
        else:
            got = dot(d2[:, 128 * u : 128 * u + 128], even[...])
        got = got.astype(BF)
        for kd in range(3):
            for m in range(2):
                if 1 + kd + 2 * m == start:
                    for kw in range(3):
                        k = 3 * kd + kw
                        d2c[512 * k : 512 * k + 512, 128 * m : 128 * m + 128] = got[
                            :, 128 * kw : 128 * kw + 128
                        ]
    back = dot(t2r[...], d2c[...]).astype(BF)
    back = dot(back, grow1[...])
    for h in range(16):
        rows = slice(32 * h, 32 * h + 32)
        source = back[32 * (h // 2) : 32 * (h // 2) + 32, :]
        for e in range(8):
            lanes = slice(128 * e, 128 * e + 128)
            delta = source[:, 128 * (e // 2) : 128 * (e // 2) + 128] * sl1[rows, lanes].astype(F32)
            d1[rows, lanes] = delta.astype(BF)

    def grad_three(it, carry):
        kd = it // 3
        kw = it % 3
        got = dot(x3[pl.ds(pl.multiple_of(it * 256, 256), 256), 0:128], d3t[...])
        for kh in range(3):
            total = None
            for h in range(4):
                hp = h + kh - 1
                if 0 <= hp < 4:
                    part = got[64 * hp : 64 * hp + 64, 128 * h : 128 * h + 128]
                    total = part if total is None else total + part
            k = kd * 9 + kh * 3 + kw
            out[pl.ds(pl.multiple_of(k * 64, 64), 64), :] = total.astype(BF)
        return carry

    lax.fori_loop(0, 9, grad_three, 0)

    lane16 = lax.broadcasted_iota(jnp.int32, (16, 128), 1)

    def grad_two(it, carry):
        kd = it // 3
        kw = it % 3
        got = dot(x2[pl.ds(pl.multiple_of(it * 256, 256), 256), 384:640], d2t[...])
        for kh in range(3):
            totals = [None, None]
            for h in range(8):
                hp = h + kh - 1
                if 0 <= hp < 8:
                    part = got[32 * hp : 32 * hp + 32, 128 * (h // 2) : 128 * (h // 2) + 128]
                    now = totals[h % 2]
                    totals[h % 2] = part if now is None else now + part
            low = totals[0] + pltpu.roll(totals[1], 64, 1)
            high = pltpu.roll(totals[0], 64, 1) + totals[1]
            k = kd * 9 + kh * 3 + kw
            out[pl.ds(pl.multiple_of(1728 + k * 16, 16), 16), :] = jnp.where(
                lane16 < 64, low[:16], high[16:]
            ).astype(BF)
        return carry

    lax.fori_loop(0, 9, grad_two, 0)

    lhs = jnp.concatenate([x1[:, 128 * (14 + kd) : 128 * (14 + kd) + 1024] for kd in range(3)], axis=0)
    got = lax.dot_general(lhs, d1[...], (((1,), (1,)), ((), ())), preferred_element_type=F32)
    row = lax.broadcasted_iota(jnp.int32, (576, 128), 0) % 16
    col = lax.broadcasted_iota(jnp.int32, (576, 128), 1) // 32
    lane36 = lax.broadcasted_iota(jnp.int32, (36, 128), 1)
    packed = jnp.zeros((36, 128), F32)
    for kh in range(3):
        total = jnp.zeros((576, 128), F32)
        for u in range(4):
            keep = row == col + (4 * u + kh - 1)
            total = total + jnp.where(keep, got[:, 128 * u : 128 * u + 128], 0.0)
        total = total.reshape(36, 16, 128).sum(axis=1)
        total = total + pltpu.roll(total, 64, 1)
        total = total + pltpu.roll(total, 32, 1)
        packed = packed + jnp.where(lane36 // 32 == kh, total, 0.0)
    out[2160:2208, :] = jnp.concatenate([packed, jnp.zeros((12, 128), F32)], axis=0).astype(BF)
    out[2208:, :] = jnp.zeros((out.shape[0] - 2208, 128), BF)


def local_grads(place, volumes, grad_own, base_one, filter_two, filter_three, rows):
    tables = [jnp.asarray(t, BF) for t in one_hot_tables()]
    vmem = pl.BlockSpec(memory_space=pltpu.VMEM)
    args = [*volumes, grad_own, base_one, filter_two, filter_three, *tables]
    return pl.pallas_call(
        body,
        out_shape=jax.ShapeDtypeStruct((rows, 128), BF),
        in_specs=[pl.BlockSpec(memory_space=pltpu.SMEM)] + [vmem] * len(args),
        out_specs=vmem,
        scratch_shapes=[
            pltpu.VMEM((512, 576), BF),
            pltpu.VMEM((512, 2304), BF),
            pltpu.VMEM((512, 2304), BF),
            pltpu.VMEM((256, 4608), BF),
            pltpu.VMEM((256, 4608), BF),
            pltpu.VMEM((192, 38 * 128), BF),
            pltpu.VMEM((256, 18 * 128), BF),
            pltpu.VMEM((2304, 1024), BF),
            pltpu.VMEM((256, 1024), BF),
            pltpu.VMEM((2304, 256), BF),
            pltpu.VMEM((4608, 128), BF),
            pltpu.VMEM((4608, 256), BF),
            pltpu.VMEM((512, 1024), BF),
            pltpu.VMEM((512, 1024), BF),
            pltpu.VMEM((512, 512), BF),
            pltpu.VMEM((512, 1024), BF),
            pltpu.VMEM((256, 512), BF),
            pltpu.VMEM((128, 512), BF),
        ],
        compiler_params=pltpu.CompilerParams(vmem_limit_bytes=58 * 1024 * 1024),
        name="local_grads",
    )(place, *args)


def exchange(pieces, axis):
    return lax.all_to_all(pieces, axis, 0, 0, tiled=True)


def total_of(got):
    return got.astype(F32).sum(axis=0).astype(BF)


def per_device(volume, grad_out, filter_one, filter_two, filter_three):
    spaces, samples = (lax.axis_size("space"), lax.axis_size("sample"))
    place = jnp.stack([lax.axis_index("space"), jnp.int32(spaces)]).astype(jnp.int32)
    vol = volume.reshape(512, 128)
    grad = grad_out.reshape(32, 128)
    both = jnp.concatenate([vol, grad], axis=0)

    def move(values, step):
        return lax.ppermute(
            values, "space", [(i, i + step) for i in range(spaces) if 0 <= i + step < spaces]
        )

    before1, after1 = (move(both, 1), move(both, -1))
    before2, after2 = (move(vol[64:], 2), move(vol[:448], -2))
    base_one = jnp.transpose(filter_one, (4, 0, 2, 3, 1)).astype(F32) * 0.5
    base_one = jnp.pad(base_one, ((0, 0), (0, 0), (0, 0), (0, 0), (0, 13))).reshape(32, 576)
    base_one = jnp.pad(base_one, ((0, 0), (0, 64)))
    flat = local_grads(
        place,
        (before2, before1, vol, after1, after2),
        grad,
        base_one,
        filter_two.reshape(27, 32, 64),
        filter_three.reshape(27, 64, 128),
        spaces * SLOT,
    )
    part = total_of(exchange(flat.reshape(spaces, SLOT, 128), "space"))
    part = total_of(exchange(jnp.broadcast_to(part[None], (samples, SLOT, 128)), "sample"))
    flat = exchange(jnp.broadcast_to(part[None], (spaces, SLOT, 128)), "space")
    flat = flat.reshape(-1, 128).astype(F32)
    cells = float(samples * spaces * volume.shape[1] * volume.shape[3] * volume.shape[4])
    g_three = flat[:1728].reshape(3, 3, 3, 64, 128)
    g_two = flat[1728:2160].reshape(3, 3, 3, 16, 128)
    g_two = jnp.concatenate([g_two[..., :64], g_two[..., 64:]], axis=3)
    g_one = jnp.transpose(flat[2160:2196, :96].reshape(3, 3, 4, 3, 32), (0, 3, 1, 2, 4))
    return (
        g_one / jnp.sqrt(jnp.float32(cells)),
        g_two / jnp.sqrt(jnp.float32(cells / 8.0)),
        g_three / jnp.sqrt(jnp.float32(cells / 64.0)),
    )


def solution(mesh):
    return jax.shard_map(
        per_device,
        mesh=mesh,
        in_specs=(
            P(("sample", "space"), None, None, None, None),
            P(("sample", "space"), None, None, None, None),
            P(),
            P(),
            P(),
        ),
        out_specs=(P(), P(), P()),
        check_vma=False,
    )
```

time: 411 us -> 115 us (0.28); the launches traced: 405 us -> 115 us
  waiting for transfers between devices: 149 us -> 3.45 us
  matrix products: 59.3 us -> 0 us
  local copies, waits for them, and re-layouts: 40.6 us -> 3.48 us
  Pallas kernels: 0 us -> 33.5 us
  blocking collectives: 88.9 us -> 58.3 us
  other arithmetic: 25.1 us -> 4.34 us
  starting transfers between devices: 26.5 us -> 10.8 us
  between operations: 15.2 us -> 0.77 us
    psum x1 -> x0, waiting for transfers between devices: 140 us -> none  [per_device(): totals = lax.psum((g_one, g_two, g_three), ('sample', 'space'))]
    psum x1 -> x0, blocking collectives: 88.9 us -> none  [per_device(): totals = lax.psum((g_one, g_two, g_three), ('sample', 'space'))]
    all_to_all x0 -> x3, blocking collectives: none -> 58.3 us  [exchange(): return lax.all_to_all(pieces, axis, 0, 0, tiled=True)]
    conv_general_dilated x5 -> x0, matrix products: 33.7 us -> none  [convolve(): lax.conv_general_dilated(inputs, kernel, (1, 1, 1), padding, dimension_nu...]
    pallas_call x0 -> x1, Pallas kernels: none -> 33.5 us  [local_grads(): pl.pallas_call(body, out_shape=jax.ShapeDtypeStruct((rows, 128), BF), in_...]
    dot_general x81 -> x0, matrix products: 25.6 us -> none  [the longest x54 13.5 us: filter_grad(): jnp.einsum('ndhwi,ndhwo->io', piece, delta, preferred_element_type=jnp.fl...]
    ppermute x10 -> x4, starting transfers between devices: 26.5 us -> 10.8 us  [move(): lax.ppermute(values, 'space', [(i, i + step) for i in range(spaces) if 0...]
    mul x12 -> x0, local copies, waits for them, and re-layouts: 15.2 us -> none  [the longest x3 8.92 us: slope(): return sig * (1.0 + values * (1.0 - sig))]
  transfers between devices with their start and end apart: 11 -> 4, of which waited for: 4 -> 1; matrix products, arithmetic and copies ran while one was open for 15% -> 3% of each run, Pallas kernels for 0% -> 0%
where the time goes in v1:
time: 115 us
  blocking collectives  58.3 us (51%)
  Pallas kernels  33.5 us (29%)
  starting transfers between devices  10.8 us (9%)
  other arithmetic  4.34 us (4%)
  local copies, waits for them, and re-layouts  3.48 us (3%)
  waiting for transfers between devices  3.45 us (3%)
    all_to_all x3, blocking collectives, exchange(): return lax.all_to_all(pieces, axis, 0, 0, tiled=True)  58.3 us
    pallas_call x1, Pallas kernels, local_grads(): pl.pallas_call(body, out_shape=jax.ShapeDtypeStruct((rows, 128), BF), in_...  33.5 us
    ppermute x4, starting transfers between devices, move(): lax.ppermute(values, 'space', [(i, i + step) for i in range(spaces) if 0...  10.8 us
    ppermute x4, waiting for transfers between devices, move(): lax.ppermute(values, 'space', [(i, i + step) for i in range(spaces) if 0...  3.45 us
  transfers between devices with their start and end apart: 4, of which 1 were waited for; matrix products, arithmetic and copies ran while one was open for 3% of the time, Pallas kernels for 0%

profile of v1, /device:TPU:1, one launch (start us, length us, event | category | flops | bytes accessed | tf_op | source)
XLA Modules:
  0.0 114.7 jit_solution(12993568422726957076)
XLA Ops:
  0.6 0.9 pad_maximum_fusion
  1.6 5.1 %collective-permute-start.2 = (bf16[544,128]{1,0:T(8,128)(2,1)S(1)}, bf16[544,128]{1,0:T(8,128)(2,1)S(1)}, u32[]{:S(2)}, u32[]{:S(2)}) collective-permute-start(bf16[544,128]{1,0:T(8,128)(2,1)S(1)} %pad_maximum_fusion), channel_id=1, source_target_pairs={{1,0},{2,1},{3,2},{4,3},{5,4},{6,5},{7,6},{8,7},{9,8},{10,9},{11,1... | collective-permute-start | bytes 417800 | tf_op jit(solution)/shard_map/ppermute | solution.py:426
  6.7 1.9 %collective-permute-start.1 = (bf16[544,128]{1,0:T(8,128)(2,1)S(1)}, bf16[544,128]{1,0:T(8,128)(2,1)S(1)}, u32[]{:S(2)}, u32[]{:S(2)}) collective-permute-start(bf16[544,128]{1,0:T(8,128)(2,1)S(1)} %pad_maximum_fusion), channel_id=1, source_target_pairs={{0,1},{1,2},{2,3},{3,4},{4,5},{5,6},{6,7},{7,8},{8,9},{9,10},{10,1... | collective-permute-start | bytes 417800 | tf_op jit(solution)/shard_map/ppermute | solution.py:426
  8.7 1.0 fusion.1
  9.6 2.5 %collective-permute-start = (bf16[448,128]{1,0:T(8,128)(2,1)S(1)}, bf16[448,128]{1,0:T(8,128)(2,1)S(1)}, u32[]{:S(2)}, u32[]{:S(2)}) collective-permute-start(bf16[448,128]{1,0:T(8,128)(2,1)S(1)} %bitcast.27), channel_id=1, source_target_pairs={{0,2},{1,3},{2,4},{3,5},{4,6},{5,7},{6,8},{7,9},{8,10},{9,11},{10,... | collective-permute-start | bytes 344072 | tf_op jit(solution)/shard_map/ppermute | solution.py:426
  12.1 1.3 %collective-permute-start.3 = (bf16[448,128]{1,0:T(8,128)(2,1)S(1)}, bf16[448,128]{1,0:T(8,128)(2,1)S(1)}, u32[]{:S(2)}, u32[]{:S(2)}) collective-permute-start(bf16[448,128]{1,0:T(8,128)(2,1)S(1)} %bitcast.26), channel_id=1, source_target_pairs={{2,0},{3,1},{4,2},{5,3},{6,4},{7,5},{8,6},{9,7},{10,8},{11,9},{12,... | collective-permute-start | bytes 344072 | tf_op jit(solution)/shard_map/ppermute | solution.py:426
  13.4 0.8 multiply_bitcast_fusion
  14.3 0.1 copy.23
  14.4 0.6 pad.9.base_one
  15.0 0.6 pad_add_fusion.place
  15.6 0.0 collective-permute-done.vol_b2
  15.6 0.0 copy-start.2
  15.6 3.4 %collective-permute-done.3.vol_a2 = bf16[448,128]{1,0:T(8,128)(2,1)S(1)} collective-permute-done((bf16[448,128]{1,0:T(8,128)(2,1)S(1)}, bf16[448,128]{1,0:T(8,128)(2,1)S(1)}, u32[]{:S(2)}, u32[]{:S(2)}) %collective-permute-start.3) | collective-permute-done | bytes 114720 | tf_op jit(solution)/shard_map/ppermute | solution.py:426
  19.1 0.0 copy-start.3
  19.1 0.0 collective-permute-done.2.vol_a1
  19.1 0.0 copy-start
  19.1 0.0 collective-permute-done.1.vol_b1
  19.1 0.0 copy-start.1
  19.1 0.0 copy-done.2
  19.1 0.6 copy-done.3
  19.7 0.0 copy-done
  19.7 0.1 copy-done.1
  19.8 33.5 %local_grads.1 = bf16[2560,128]{1,0:T(8,128)(2,1)} custom-call(s32[2]{0:T(128)} %pad_add_fusion.place, bf16[448,128]{1,0:T(8,128)(2,1)} %copy-done.2, bf16[544,128]{1,0:T(8,128)(2,1)} %copy-done.1, bf16[512,128]{1,0:T(8,128)(2,1)} %bitcast.20, bf16[544,128]{1,0:T(8,128)(2,1)} %copy-done, bf16[448,128]{1,0:T(8,128)(2,1)} %copy-done.3, ...), custom_call_target="tpu_custom_call" | custom-call | tf_op jit(solution)/shard_map/local_grads/pallas_call | solution.py:380
  53.2 23.2 %all_to_all.15 = bf16[32,80,128]{2,1,0:T(8,128)(2,1)S(1)} all-to-all(bf16[32,80,128]{2,1,0:T(8,128)(2,1)} %bitcast.17), channel_id=1, replica_groups=mesh['sample'=8,'space'=32] {'space'}, dimensions={0} | all-to-all | bytes 1310720 | tf_op jit(solution)/shard_map/all_to_all | solution.py:411
  76.5 0.1 reduce_sum.24
  76.6 16.4 %all_to_all.16 = bf16[8,80,128]{2,1,0:T(8,128)(2,1)S(1)} all-to-all(bf16[8,80,128]{2,1,0:T(8,128)(2,1)S(1)} %broadcast_in_dim.4), channel_id=1, replica_groups=mesh['sample'=8,'space'=32] {'sample'}, dimensions={0} | all-to-all | bytes 327680 | tf_op jit(solution)/shard_map/all_to_all | solution.py:411
  93.0 0.1 broadcast_in_dim.5
  93.1 18.7 %all_to_all.17 = bf16[32,80,128]{2,1,0:T(8,128)(2,1)S(1)} all-to-all(bf16[32,80,128]{2,1,0:T(8,128)(2,1)S(1)} %broadcast_in_dim.5), channel_id=1, replica_groups=mesh['sample'=8,'space'=32] {'space'}, dimensions={0} | all-to-all | bytes 1310720 | tf_op jit(solution)/shard_map/all_to_all | solution.py:411
  111.8 0.1 bitcast_convert_fusion
  112.0 1.0 slice_multiply_fusion
  113.0 0.1 div.26
  113.1 0.6 copy.24
  113.7 0.1 fusion
  113.8 0.8 maximum_multiply_fusion
  (6 shorter events, 0.1 us)
Async XLA Ops:
  1.6 17.5 %collective-permute-start.2 = (bf16[544,128]{1,0:T(8,128)(2,1)S(1)}, bf16[544,128]{1,0:T(8,128)(2,1)S(1)}, u32[]{:S(2)}, u32[]{:S(2)}) collective-permute-start(bf16[544,128]{1,0:T(8,128)(2,1)S(1)} %pad_maximum_fusion), channel_id=1, source_target_pairs={{1,0},{2,1},{3,2},{4,3},{5,4},{6,5},{7,6},{8,7},{9,8},{10,9},{11,1... | collective-permute-start | bytes 417800 | tf_op jit(solution)/shard_map/ppermute | solution.py:426
  6.7 12.3 %collective-permute-start.1 = (bf16[544,128]{1,0:T(8,128)(2,1)S(1)}, bf16[544,128]{1,0:T(8,128)(2,1)S(1)}, u32[]{:S(2)}, u32[]{:S(2)}) collective-permute-start(bf16[544,128]{1,0:T(8,128)(2,1)S(1)} %pad_maximum_fusion), channel_id=1, source_target_pairs={{0,1},{1,2},{2,3},{3,4},{4,5},{5,6},{6,7},{7,8},{8,9},{9,10},{10,1... | collective-permute-start | bytes 417800 | tf_op jit(solution)/shard_map/ppermute | solution.py:426
  9.6 6.0 %collective-permute-start = (bf16[448,128]{1,0:T(8,128)(2,1)S(1)}, bf16[448,128]{1,0:T(8,128)(2,1)S(1)}, u32[]{:S(2)}, u32[]{:S(2)}) collective-permute-start(bf16[448,128]{1,0:T(8,128)(2,1)S(1)} %bitcast.27), channel_id=1, source_target_pairs={{0,2},{1,3},{2,4},{3,5},{4,6},{5,7},{6,8},{7,9},{8,10},{9,11},{10,... | collective-permute-start | bytes 344072 | tf_op jit(solution)/shard_map/ppermute | solution.py:426
  12.1 6.9 %collective-permute-start.3 = (bf16[448,128]{1,0:T(8,128)(2,1)S(1)}, bf16[448,128]{1,0:T(8,128)(2,1)S(1)}, u32[]{:S(2)}, u32[]{:S(2)}) collective-permute-start(bf16[448,128]{1,0:T(8,128)(2,1)S(1)} %bitcast.26), channel_id=1, source_target_pairs={{2,0},{3,1},{4,2},{5,3},{6,4},{7,5},{8,6},{9,7},{10,8},{11,9},{12,... | collective-permute-start | bytes 344072 | tf_op jit(solution)/shard_map/ppermute | solution.py:426
  15.6 3.5 %copy-start.2 = (bf16[448,128]{1,0:T(8,128)(2,1)}, bf16[448,128]{1,0:T(8,128)(2,1)S(1)}, u32[]{:S(2)}) copy-start(bf16[448,128]{1,0:T(8,128)(2,1)S(1)} %collective-permute-done.vol_b2) | copy-start | bytes 344068
  19.1 0.6 copy-start.3
  19.1 0.7 copy-start
  19.1 0.7 copy-start.1

commit v2 on v1

v2 whole, which is shorter than its diff:
```python
import jax
import jax.numpy as jnp
import numpy as np
from jax import lax
from jax.experimental import pallas as pl
from jax.experimental.pallas import tpu as pltpu
from jax.sharding import PartitionSpec as P

BF = jnp.bfloat16
F32 = jnp.float32
SLOT = 80
G_TWO = 1728
G_ONE = 2160
NT = (((1,), (1,)), ((), ()))
TN = (((0,), (0,)), ((), ()))


def table(rows, cols):
    return np.zeros((rows, cols), np.float32)


def build_tables():
    perm = table(108, 640)
    for kd in range(3):
        for kh in range(3):
            for kw in range(3):
                for c in range(4):
                    row = ((kd * 3 + kh) * 3 + kw) * 4 + c
                    perm[row, ((kd * 3 + kw) * 4 + c) * 16 + kh] = 0.5
    return [perm]


def forward_tables():
    shift = table(128, 256)
    for w in range(128):
        if w >= 1:
            shift[w - 1, w] = 1.0
        if w + 1 < 128:
            shift[w + 1, 128 + w] = 1.0
    pair = table(256, 384)
    for a in range(2):
        for kw in range(3):
            for w in range(64):
                src = w + kw - 1
                if 0 <= src < 64:
                    pair[128 * a + 2 * src, 128 * kw + 64 * a + w] = 1.0
    squeeze = table(512, 128)
    for m in range(4):
        for w in range(32):
            squeeze[128 * m + 2 * w, 32 * m + w] = 1.0
    spread = table(128, 1152)
    for kd in range(3):
        for kw in range(3):
            at = 3 * kd + kw
            for w in range(32):
                src = w + kw - 1
                if 0 <= src < 32:
                    for n in range(2):
                        spread[32 * (n + kd) + src, 128 * at + 32 * n + w] = 1.0
    grow = table(16, 128)
    for d in range(2):
        for w in range(32):
            grow[w // 2, 32 * d + w] = 1.0 / 16
    return [shift, pair, squeeze, spread, grow]


def backward_tables():
    odd = table(256, 384)
    even = table(128, 384)
    for a in range(2):
        for kw in range(3):
            for w in range(64):
                src = w + kw - 1
                if 0 <= src < 64:
                    odd[64 + 64 * a + src, 128 * kw + 64 * a + w] = 1.0
                    even[64 * a + src, 128 * kw + 64 * a + w] = 1.0
    spread = table(256, 1152)
    for kd in range(3):
        for kw in range(3):
            at = 3 * kd + kw
            for w in range(32):
                src = w + kw - 1
                if 0 <= src < 32:
                    for n in range(4):
                        spread[32 * (n + kd) + src, 128 * at + 32 * n + w] = 1.0
    grow2 = table(128, 512)
    for n in range(4):
        for d in range(2):
            for w in range(64):
                grow2[32 * n + w // 2, 64 * (2 * n + d) + w] = 1.0 / 16
    grow1 = table(256, 512)
    for e in range(4):
        for w in range(128):
            grow1[64 * e + w // 2, 128 * e + w] = 1.0 / 16
    return [odd, even, spread, grow2, grow1]


def dot(a, b):
    return jnp.dot(a, b, preferred_element_type=F32)


def inside(index, count):
    return jnp.logical_and(index >= 0, index < count)


def position():
    return lax.axis_index("space"), lax.axis_size("space")


def taps_of(it):
    kd, kw = (it // 3, it % 3)
    return [kd * 9 + kh * 3 + kw for kh in range(3)]


def taps_back(it):
    kd, kw = (2 - it // 3, 2 - it % 3)
    return [kd * 9 + (2 - kh) * 3 + kw for kh in range(3)]


def build_forward(filter_one, filter_two, filter_three, perm, t1, t2, t3, s2, s3, sems):
    for it in range(9):
        w2 = [filter_two[k].astype(F32).T * 0.5 for k in taps_of(it)]
        zero = jnp.zeros((64, 32), F32)
        for s in range(-6, 6):
            if -3 <= s <= 2:
                parts = [w2[s + j] if 0 <= s + j <= 2 else zero for j in range(4)]
                tile = jnp.concatenate(parts, axis=1).astype(BF)
            else:
                tile = jnp.zeros((64, 128), BF)
            for m in range(2):
                h = 4 * m + 1 - s
                if 0 <= h < 8:
                    s2[64 * h : 64 * h + 64, it * 256 + 128 * m : it * 256 + 128 * m + 128] = tile
    copy2 = pltpu.make_async_copy(s2, t2, sems.at[0])
    copy2.start()
    for it in range(9):
        w3 = [filter_three[k].astype(F32).T * 0.5 for k in taps_of(it)]
        zero = jnp.zeros((128, 64), F32)
        for s in range(-2, 4):
            if -1 <= s <= 2:
                parts = [w3[s + j] if 0 <= s + j <= 2 else zero for j in range(2)]
                tile = jnp.concatenate(parts, axis=1).astype(BF)
            else:
                tile = jnp.zeros((128, 128), BF)
            for m in range(2):
                h = 2 * m + 1 - s
                if 0 <= h < 4:
                    s3[128 * h : 128 * h + 128, it * 256 + 128 * m : it * 256 + 128 * m + 128] = tile
    copy3 = pltpu.make_async_copy(s3, t3, sems.at[1])
    copy3.start()
    lane = lax.broadcasted_iota(jnp.int32, (32, 640), 1) % 16
    base = lax.dot_general(filter_one[...], perm[...], TN, preferred_element_type=F32)
    for h in range(16):
        moved = pltpu.roll(base, (h - 1) % 640, 1) if h != 1 else base
        if h == 0:
            moved = jnp.where(lane == 15, 0.0, moved)
        if h == 15:
            moved = jnp.where(lane == 0, 0.0, moved)
        t1[32 * h : 32 * h + 32, :] = moved[:, :576].astype(BF)
    copy2.wait()
    copy3.wait()


def build_backward(filter_two, filter_three, t3r, t2r, s3, s2, sems):
    for it in range(9):
        v3 = [filter_three[k] for k in taps_back(it)]
        for hp in range(4):
            for h in range(4):
                kh = h - hp + 1
                tile = v3[kh] if 0 <= kh <= 2 else jnp.zeros((64, 128), BF)
                s3[64 * hp : 64 * hp + 64, it * 512 + 128 * h : it * 512 + 128 * h + 128] = tile
    copy3 = pltpu.make_async_copy(s3, t3r, sems.at[0])
    copy3.start()
    for it in range(9):
        v2 = [filter_two[k].astype(F32) for k in taps_back(it)]
        zero = jnp.zeros((32, 64), F32)
        for s in range(-6, 8):
            if -1 <= s <= 2:
                parts = [v2[s + j] if 0 <= s + j <= 2 else zero for j in range(2)]
                tile = jnp.concatenate(parts, axis=1).astype(BF)
            else:
                tile = jnp.zeros((32, 128), BF)
            for m in range(4):
                hp = 2 * m + 1 - s
                if 0 <= hp < 8:
                    s2[32 * hp : 32 * hp + 32, it * 512 + 128 * m : it * 512 + 128 * m + 128] = tile
    copy2 = pltpu.make_async_copy(s2, t2r, sems.at[1])
    copy2.start()
    copy3.wait()
    copy2.wait()


def forward(
    vol_before,
    vol_own,
    vol_after,
    grad_own,
    t1,
    t2_far,
    t3_far,
    shift,
    pair,
    squeeze,
    spread,
    grow,
    d3p,
    d3t,
    x3,
    sl1,
    sl2,
    x1_own,
    x2_own,
    t2,
    t3,
    x1,
    pp,
    x2,
    q,
    sems,
):
    me, blocks = position()
    copy2 = pltpu.make_async_copy(t2_far, t2, sems.at[0])
    copy2.start()
    copy3 = pltpu.make_async_copy(t3_far, t3, sems.at[1])
    copy3.start()

    at = 0
    for ref, first, count in ((vol_before, 1, 7), (vol_own, 0, 8), (vol_after, 0, 7)):
        rows = ref[64 * first : 64 * (first + count), :]
        moved = dot(rows, shift[...]).astype(BF)
        for p in range(count):
            lanes = slice(128 * (at + p), 128 * (at + p) + 128)
            x1[0:64, lanes] = moved[64 * p : 64 * p + 64, :128]
            x1[64:128, lanes] = rows[64 * p : 64 * p + 64, :]
            x1[128:192, lanes] = moved[64 * p : 64 * p + 64, 128:]
        at += count

    for j in range(10):
        rhs = jnp.concatenate(
            [x1[:, (2 * j + kd) * 128 : (2 * j + kd) * 128 + 256] for kd in range(3)], axis=0
        )
        half = dot(t1[...], rhs)
        t = jnp.tanh(half)
        if 3 <= j < 7:
            slope = (1.0 + t) + half * (1.0 - t * t)
            sl1[:, (j - 3) * 256 : (j - 3) * 256 + 256] = slope.astype(BF)
        act = half + half * t
        act = act[:, :128] + act[:, 128:]
        act = act.reshape(8, 2, 32, 128)
        act = (act[:, 0] + act[:, 1]).reshape(256, 128)
        act = act + pltpu.roll(act, 127, 1)
        scale = jnp.where(inside(4 * me - 3 + j, 4 * blocks), 0.125, 0.0)
        pp[:, j * 128 : j * 128 + 128] = (act * scale).astype(BF)

    for first in range(9):
        got = dot(pp[:, first * 128 : first * 128 + 256], pair[...]).astype(BF)
        for kd in range(3):
            m = (first - kd) // 2
            if (first - kd) % 2 == 0 and 0 <= m < 4:
                for kw in range(3):
                    k = 3 * kd + kw
                    x2[256 * k : 256 * k + 256, m * 128 : m * 128 + 128] = got[
                        :, 128 * kw : 128 * kw + 128
                    ]

    copy2.wait()
    for c in range(2):
        lanes = slice(c * 256, c * 256 + 256)
        half = dot(t2[...], x2[:, lanes])
        t = jnp.tanh(half)
        slope = (1.0 + t) + half * (1.0 - t * t)
        sl2[:, lanes] = slope.astype(BF)
        act = (half + half * t).reshape(4, 2, 64, 256)
        act = (act[:, 0] + act[:, 1]).reshape(256, 256)
        for u in range(2):
            tile = act[:, 128 * u : 128 * u + 128]
            tile = tile + pltpu.roll(tile, 64, 1)
            tile = tile + pltpu.roll(tile, 127, 1)
            m = 2 * c + u
            scale = jnp.where(inside(2 * me - 1 + m, 2 * blocks), 0.125, 0.0)
            q[:, m * 128 : m * 128 + 128] = (tile * scale).astype(BF)
    x1_own[...] = x1[:, 6 * 128 : 16 * 128]
    x2_own[...] = x2[:, 128:384]

    packed = dot(q[...], squeeze[...]).astype(BF)
    got = dot(packed, spread[...]).astype(BF)
    for k in range(9):
        x3[256 * k : 256 * k + 256, :] = got[:, 128 * k : 128 * k + 128]
    copy3.wait()
    half = dot(t3[...], x3[...])
    t = jnp.tanh(half)
    slope = (1.0 + t) + half * (1.0 - t * t)
    grown = []
    for hh in range(2):
        rows = grad_own[16 * hh : 16 * hh + 16, :]
        got = lax.dot_general(rows, grow[...], TN, preferred_element_type=F32)
        grown += [got, got]
    delta = jnp.concatenate(grown, axis=0) * slope
    d3t[...] = delta.T.astype(BF)
    d3p[...] = (delta[:256] + pltpu.roll(delta[256:], 64, 1)).astype(BF)


def grad_three(x3, d3t, out):
    for it in range(9):
        got = dot(x3[256 * it : 256 * it + 256, :], d3t[...])
        for kh, k in enumerate(taps_of(it)):
            total = None
            for h in range(4):
                hp = h + kh - 1
                if 0 <= hp < 4:
                    part = got[64 * hp : 64 * hp + 64, 128 * h : 128 * h + 128]
                    total = part if total is None else total + part
            out[k * 64 : k * 64 + 64, :] = total.astype(BF)


def backward(
    d3_before,
    d3_own,
    d3_after,
    g3,
    sl2,
    t3r_far,
    t2r_far,
    sl1_far,
    x2_far,
    x1_far,
    odd,
    even,
    spread,
    grow2,
    grow1,
    out,
    t3r,
    t2r,
    sl1,
    x2,
    x1,
    d3c,
    d2c,
    d2,
    d1,
    d2t,
    sems,
):
    me, blocks = position()
    copies = []
    for i, (far, near) in enumerate(
        ((t3r_far, t3r), (t2r_far, t2r), (x2_far, x2), (sl1_far, sl1), (x1_far, x1))
    ):
        copies.append(pltpu.make_async_copy(far, near, sems.at[i]))
        copies[-1].start()
    out[:G_TWO, :] = g3[...]

    before, own, after = (ref[...].astype(F32) for ref in (d3_before, d3_own, d3_after))
    low = lax.broadcasted_iota(jnp.int32, (256, 128), 1) < 64
    top = jnp.where(low, before, pltpu.roll(own, 64, 1))
    bottom = jnp.where(low, pltpu.roll(before, 64, 1), own)
    delta = jnp.concatenate(
        [
            jnp.concatenate([top, after], axis=1),
            jnp.concatenate([bottom, pltpu.roll(after, 64, 1)], axis=1),
        ],
        axis=0,
    ).astype(BF)
    got = dot(delta, spread[...]).astype(BF)
    for k in range(9):
        d3c[512 * k : 512 * k + 512, :] = got[:, 128 * k : 128 * k + 128]
    copies[0].wait()
    back = dot(t3r[...], d3c[...])
    lane = lax.broadcasted_iota(jnp.int32, (256, 128), 1)
    back = jnp.where(inside(2 * me - 1 + lane // 32, 2 * blocks), back, 0.0).astype(BF)
    back = dot(back, grow2[...])
    for h in range(8):
        rows = slice(64 * h, 64 * h + 64)
        delta = back[64 * (h // 2) : 64 * (h // 2) + 64, :] * sl2[rows, :].astype(F32)
        d2t[:, rows] = delta[:, 128:384].T.astype(BF)
        d2[rows, :] = delta.astype(BF)

    for start in range(1, 6):
        u = start // 2
        if start % 2:
            got = dot(d2[:, 128 * u : 128 * u + 256], odd[...])
        else:
            got = dot(d2[:, 128 * u : 128 * u + 128], even[...])
        got = got.astype(BF)
        for kd in range(3):
            for m in range(2):
                if 1 + kd + 2 * m == start:
                    for kw in range(3):
                        k = 3 * kd + kw
                        d2c[512 * k : 512 * k + 512, 128 * m : 128 * m + 128] = got[
                            :, 128 * kw : 128 * kw + 128
                        ]
    copies[1].wait()
    back = dot(t2r[...], d2c[...]).astype(BF)

    copies[2].wait()
    lane16 = lax.broadcasted_iota(jnp.int32, (16, 128), 1)
    for it in range(9):
        got = dot(x2[256 * it : 256 * it + 256, :], d2t[...])
        for kh, k in enumerate(taps_of(it)):
            totals = [None, None]
            for h in range(8):
                hp = h + kh - 1
                if 0 <= hp < 8:
                    part = got[32 * hp : 32 * hp + 32, 128 * (h // 2) : 128 * (h // 2) + 128]
                    now = totals[h % 2]
                    totals[h % 2] = part if now is None else now + part
            low = totals[0] + pltpu.roll(totals[1], 64, 1)
            high = pltpu.roll(totals[0], 64, 1) + totals[1]
            out[G_TWO + k * 16 : G_TWO + k * 16 + 16, :] = jnp.where(
                lane16 < 64, low[:16], high[16:]
            ).astype(BF)

    copies[3].wait()
    back = dot(back, grow1[...])
    for h in range(16):
        rows = slice(32 * h, 32 * h + 32)
        source = back[32 * (h // 2) : 32 * (h // 2) + 32, :]
        for e in range(8):
            lanes = slice(128 * e, 128 * e + 128)
            delta = source[:, 128 * (e // 2) : 128 * (e // 2) + 128] * sl1[rows, lanes].astype(F32)
            d1[rows, lanes] = delta.astype(BF)

    copies[4].wait()
    lhs = jnp.concatenate([x1[:, 128 * kd : 128 * kd + 1024] for kd in range(3)], axis=0)
    got = lax.dot_general(lhs, d1[...], NT, preferred_element_type=F32)
    row = lax.broadcasted_iota(jnp.int32, (576, 128), 0) % 16
    col = lax.broadcasted_iota(jnp.int32, (576, 128), 1) // 32
    lane36 = lax.broadcasted_iota(jnp.int32, (36, 128), 1)
    packed = jnp.zeros((36, 128), F32)
    for kh in range(3):
        total = jnp.zeros((576, 128), F32)
        for u in range(4):
            keep = row == col + (4 * u + kh - 1)
            total = total + jnp.where(keep, got[:, 128 * u : 128 * u + 128], 0.0)
        total = total.reshape(36, 16, 128).sum(axis=1)
        total = total + pltpu.roll(total, 64, 1)
        total = total + pltpu.roll(total, 32, 1)
        packed = packed + jnp.where(lane36 // 32 == kh, total, 0.0)
    out[G_ONE : G_ONE + 48, :] = jnp.concatenate(
        [packed, jnp.zeros((12, 128), F32)], axis=0
    ).astype(BF)
    out[G_ONE + 48 :, :] = jnp.zeros((out.shape[0] - G_ONE - 48, 128), BF)


def finish(scales, flat, one, two, three):
    for k in range(27):
        three[k] = flat[64 * k : 64 * k + 64, :].astype(F32) * scales[2]
        got = flat[G_TWO + 16 * k : G_TWO + 16 * k + 16, :].astype(F32) * scales[1]
        two[k, 0:16, :] = got[:, :64]
        two[k, 16:32, :] = got[:, 64:]
    got = flat[G_ONE : G_ONE + 48, :].astype(F32) * scales[0]
    for it in range(9):
        for kh, k in enumerate(taps_of(it)):
            one[k] = got[4 * it : 4 * it + 4, 32 * kh : 32 * kh + 32]


VMEM = pl.BlockSpec(memory_space=pltpu.VMEM)
FAR = pl.BlockSpec(memory_space=pl.ANY)


def call(kernel, name, args, far, outs, far_outs, scratch, flops):
    shapes = [jax.ShapeDtypeStruct(shape, kind) for shape, kind in outs]
    moved = sum(a.size * a.dtype.itemsize for a in list(args) + shapes)
    return pl.pallas_call(
        kernel,
        out_shape=shapes,
        in_specs=[FAR if i in far else VMEM for i in range(len(args))],
        out_specs=[FAR if i in far_outs else VMEM for i in range(len(outs))],
        scratch_shapes=scratch,
        compiler_params=pltpu.CompilerParams(vmem_limit_bytes=58 * 1024 * 1024),
        cost_estimate=pl.CostEstimate(flops=flops, bytes_accessed=moved, transcendentals=0),
        name=name,
    )(*args)


def near(*shape):
    return pltpu.VMEM(shape, BF)


def constants(tables):
    return [jnp.asarray(t, BF) for t in tables]


def run_build_forward(filter_one, filter_two, filter_three):
    return call(
        build_forward,
        "build_forward",
        [filter_one, filter_two, filter_three, *constants(build_tables())],
        (),
        [((512, 576), BF), ((512, 2304), BF), ((512, 2304), BF)],
        (1, 2),
        [near(512, 2304), near(512, 2304), pltpu.SemaphoreType.DMA((2,))],
        10**9,
    )


def run_build_backward(filter_two, filter_three):
    return call(
        build_backward,
        "build_backward",
        [filter_two, filter_three],
        (),
        [((256, 4608), BF), ((256, 4608), BF)],
        (0, 1),
        [near(256, 4608), near(256, 4608), pltpu.SemaphoreType.DMA((2,))],
        10**9,
    )


def run_forward(volumes, grad_own, t1, t2, t3):
    args = [*volumes, grad_own, t1, t2, t3, *constants(forward_tables())]
    return call(
        forward,
        "forward",
        args,
        (5, 6),
        [
            ((256, 128), BF),
            ((128, 512), BF),
            ((2304, 128), BF),
            ((512, 1024), BF),
            ((512, 512), BF),
            ((192, 1280), BF),
            ((2304, 256), BF),
        ],
        (),
        [
            near(512, 2304),
            near(512, 2304),
            near(192, 22 * 128),
            near(256, 10 * 128),
            near(2304, 512),
            near(256, 512),
            pltpu.SemaphoreType.DMA((2,)),
        ],
        7 * 10**9,
    )


def run_grad_three(x3, d3t):
    return call(grad_three, "grad_three", [x3, d3t], (), [((G_TWO, 128), BF)], (), [], 10**9)[0]


def run_backward(deltas, g3, sl2, t3r, t2r, sl1, x2, x1, rows):
    args = [*deltas, g3, sl2, t3r, t2r, sl1, x2, x1, *constants(backward_tables())]
    return call(
        backward,
        "backward",
        args,
        (5, 6, 7, 8, 9),
        [((rows, 128), BF)],
        (),
        [
            near(256, 4608),
            near(256, 4608),
            near(512, 1024),
            near(2304, 256),
            near(192, 1280),
            near(4608, 128),
            near(4608, 256),
            near(512, 512),
            near(512, 1024),
            near(256, 512),
            pltpu.SemaphoreType.DMA((5,)),
        ],
        4 * 10**9,
    )[0]


def run_finish(flat, cells):
    scales = 1.0 / jnp.sqrt(jnp.array([cells, cells / 8.0, cells / 64.0], F32))
    shapes = [(27, 4, 32), (27, 32, 64), (27, 64, 128)]
    outs = pl.pallas_call(
        finish,
        out_shape=[jax.ShapeDtypeStruct(shape, F32) for shape in shapes],
        in_specs=[pl.BlockSpec(memory_space=pltpu.SMEM), VMEM],
        out_specs=[VMEM] * 3,
        name="finish",
    )(scales, flat)
    return tuple(o.reshape(3, 3, 3, *o.shape[1:]) for o in outs)


def exchange(pieces, axis):
    return lax.all_to_all(pieces, axis, 0, 0, tiled=True)


def total_of(got):
    return got.astype(F32).sum(axis=0).astype(BF)


def move(values, step):
    size = lax.axis_size("space")
    pairs = [(i, i + step) for i in range(size) if 0 <= i + step < size]
    return lax.ppermute(values, "space", pairs)


def per_device(volume, grad_out, filter_one, filter_two, filter_three):
    spaces, samples = (lax.axis_size("space"), lax.axis_size("sample"))
    own = volume.reshape(512, 128)
    f1 = filter_one.reshape(108, 32)
    f2 = filter_two.reshape(27, 32, 64)
    f3 = filter_three.reshape(27, 64, 128)

    before = move(own, 1)
    t1, t2, t3 = run_build_forward(f1, f2, f3)
    sent, t1 = lax.optimization_barrier((own, t1))
    after = move(sent, -1)
    d3p, d3t, x3, sl1, sl2, x1, x2 = run_forward(
        (before, own, after), grad_out.reshape(32, 128), t1, t2, t3
    )
    d3_before = move(d3p, 1)
    g3 = run_grad_three(x3, d3t)
    t3r, t2r = run_build_backward(*lax.optimization_barrier((f2, f3, d3t))[:2])
    sent, g3, t2r = lax.optimization_barrier((d3p, g3, t2r))
    d3_after = move(sent, -1)
    flat = run_backward(
        (d3_before, d3p, d3_after), g3, sl2, t3r, t2r, sl1, x2, x1, spaces * SLOT
    )
    part = total_of(exchange(flat.reshape(spaces, SLOT, 128), "space"))
    part = total_of(exchange(jnp.broadcast_to(part[None], (samples, SLOT, 128)), "sample"))
    flat = exchange(jnp.broadcast_to(part[None], (spaces, SLOT, 128)), "space")
    cells = float(samples * spaces * volume.shape[1] * volume.shape[3] * volume.shape[4])
    return run_finish(flat.reshape(-1, 128), cells)


def solution(mesh):
    return jax.shard_map(
        per_device,
        mesh=mesh,
        in_specs=(
            P(("sample", "space"), None, None, None, None),
            P(("sample", "space"), None, None, None, None),
            P(),
            P(),
            P(),
        ),
        out_specs=(P(), P(), P()),
        check_vma=False,
    )
```

time: 115 us -> 116 us (level)
  other arithmetic: 4.34 us -> 0.13 us
  waiting for transfers between devices: 3.45 us -> 7.3 us
    ppermute x4, waiting for transfers between devices: 3.45 us -> 7.3 us  [move(): return lax.ppermute(values, 'space', pairs)]
    div x3 -> x0, other arithmetic: 1.81 us -> none  [the longest x1 0.97 us: per_device(): g_three / jnp.sqrt(jnp.float32(cells / 64.0))]
    reshape x1, local copies, waits for them, and re-layouts: 0.13 us -> 1.38 us  [per_device(): f1 = filter_one.reshape(108, 32)]
    pallas_call x1 -> x6, Pallas kernels: 33.5 us -> 34.4 us  [the longest x5 32.2 us: call(): pl.pallas_call(kernel, out_shape=shapes, in_specs=[FAR if i in far else V...]
  transfers between devices with their start and end apart: 4 -> 4, of which waited for: 1 -> 2; matrix products, arithmetic and copies ran while one was open for 3% -> 1% of each run, Pallas kernels for 0% -> 8%
where the time goes in v2:
time: 116 us; the launch traced here: 115 us
  blocking collectives  59 us (51%)
  Pallas kernels  34.4 us (30%)
  starting transfers between devices  11.1 us (10%)
  waiting for transfers between devices  7.3 us (6%)
  local copies, waits for them, and re-layouts  2.78 us (2%)
    all_to_all x3, blocking collectives, exchange(): return lax.all_to_all(pieces, axis, 0, 0, tiled=True)  59 us
    pallas_call x5, Pallas kernels, call(): pl.pallas_call(kernel, out_shape=shapes, in_specs=[FAR if i in far else V...  32.2 us
    ppermute x4, starting transfers between devices, move(): return lax.ppermute(values, 'space', pairs)  11.1 us
    ppermute x4, waiting for transfers between devices, move(): return lax.ppermute(values, 'space', pairs)  7.3 us
  transfers between devices with their start and end apart: 4, of which 2 were waited for; matrix products, arithmetic and copies ran while one was open for 1% of the time, Pallas kernels for 8%

profile of v2, /device:TPU:1, one launch (start us, length us, event | category | flops | bytes accessed | tf_op | source)
XLA Modules:
  0.0 115.4 jit_solution(10943216657718533270)
XLA Ops:
  0.6 0.0 copy-start
  0.6 4.6 %collective-permute-start = (bf16[512,128]{1,0:T(8,128)(2,1)}, bf16[512,128]{1,0:T(8,128)(2,1)S(1)}, u32[]{:S(2)}, u32[]{:S(2)}) collective-permute-start(bf16[512,128]{1,0:T(8,128)(2,1)} %bitcast.17), channel_id=1, source_target_pairs={{0,1},{1,2},{2,3},{3,4},{4,5},{5,6},{6,7},{7,8},{8,9},{9,10},{10,1... | collective-permute-start | bytes 393224 | tf_op jit(solution)/shard_map/ppermute | solution.py:596
  5.3 1.4 %reshape.39.filter_one = bf16[108,32]{1,0:T(8,128)(2,1)} reshape(bf16[3,3,3,4,32]{4,3,2,1,0:T(4,128)(2,1)} %param.19) | data formatting | bytes 13824 | tf_op jit(solution)/shard_map/reshape | solution.py:602
  6.7 5.2 %build_forward.1 = (bf16[512,576]{1,0:T(8,128)(2,1)}, bf16[512,2304]{1,0:T(8,128)(2,1)}, bf16[512,2304]{1,0:T(8,128)(2,1)}) custom-call(bf16[108,32]{1,0:T(8,128)(2,1)} %reshape.39.filter_one, bf16[27,32,64]{2,1,0:T(8,128)(2,1)} %bitcast.15, bf16[27,64,128]{2,1,0:T(8,128)(2,1)} %bitcast.12, bf16[108,640]{1,0:T(8,128)(2,1)} %constant.29.clone.perm), custom_call_target="tpu_custom_call" | custom-call | flops 1000000000 | bytes 6006528 | tf_op jit(solution)/shard_map/build_forward/pallas_call | solution.py:466
  11.9 0.0 copy-done
  11.9 1.9 %collective-permute-start.1 = (bf16[512,128]{1,0:T(8,128)(2,1)S(1)}, bf16[512,128]{1,0:T(8,128)(2,1)S(1)}, u32[]{:S(2)}, u32[]{:S(2)}) collective-permute-start(bf16[512,128]{1,0:T(8,128)(2,1)S(1)} %bitcast.19), channel_id=1, source_target_pairs={{1,0},{2,1},{3,2},{4,3},{5,4},{6,5},{7,6},{8,7},{9,8},{10,9},{11,1... | collective-permute-start | bytes 393224 | tf_op jit(solution)/shard_map/ppermute | solution.py:596
  13.9 0.0 collective-permute-done.vol_before
  13.9 0.0 copy-start.1
  13.9 4.3 %collective-permute-done.1.vol_after = bf16[512,128]{1,0:T(8,128)(2,1)S(1)} collective-permute-done((bf16[512,128]{1,0:T(8,128)(2,1)S(1)}, bf16[512,128]{1,0:T(8,128)(2,1)S(1)}, u32[]{:S(2)}, u32[]{:S(2)}) %collective-permute-start.1) | collective-permute-done | bytes 131104 | tf_op jit(solution)/shard_map/ppermute | solution.py:596
  18.2 0.0 copy-start.2
  18.2 0.0 copy-done.1
  18.2 0.6 copy-done.2
  18.9 10.0 %forward.1 = (bf16[256,128]{1,0:T(8,128)(2,1)}, bf16[128,512]{1,0:T(8,128)(2,1)}, bf16[2304,128]{1,0:T(8,128)(2,1)}, bf16[512,1024]{1,0:T(8,128)(2,1)}, bf16[512...) custom-call(bf16[512,128]{1,0:T(8,128)(2,1)} %copy-done.1, bf16[512,128]{1,0:T(8,128)(2,1)} %bitcast.18, ...), custom_call_target="tpu_custom_call" | custom-call | flops 7000000000 | bytes 10432512 | tf_op jit(solution)/shard_map/forward/pallas_call | solution.py:466
  28.8 0.0 copy-start.3
  28.9 2.6 %grad_three.1.g3 = bf16[1728,128]{1,0:T(8,128)(2,1)} custom-call(bf16[2304,128]{1,0:T(8,128)(2,1)} %get-tuple-element.31.x3, bf16[128,512]{1,0:T(8,128)(2,1)} %get-tuple-element.32.d3t), custom_call_target="tpu_custom_call" | custom-call | flops 1000000000 | bytes 1163264 | tf_op jit(solution)/shard_map/grad_three/pallas_call | solution.py:466
  31.5 0.0 copy-done.3
  31.5 1.9 %collective-permute-start.2 = (bf16[256,128]{1,0:T(8,128)(2,1)S(1)}, bf16[256,128]{1,0:T(8,128)(2,1)S(1)}, u32[]{:S(2)}, u32[]{:S(2)}) collective-permute-start(bf16[256,128]{1,0:T(8,128)(2,1)S(1)} %copy-done.3), channel_id=1, source_target_pairs={{0,1},{1,2},{2,3},{3,4},{4,5},{5,6},{6,7},{7,8},{8,9},{9,10},{10,1... | collective-permute-start | bytes 196616 | tf_op jit(solution)/shard_map/ppermute | solution.py:596
  33.4 3.8 %build_backward.1 = (bf16[256,4608]{1,0:T(8,128)(2,1)}, bf16[256,4608]{1,0:T(8,128)(2,1)}) custom-call(bf16[27,32,64]{2,1,0:T(8,128)(2,1)} %bitcast.16, bf16[27,64,128]{2,1,0:T(8,128)(2,1)} %bitcast.13), custom_call_target="tpu_custom_call" | custom-call | flops 1000000000 | bytes 5271552 | tf_op jit(solution)/shard_map/build_backward/pallas_call | solution.py:466
  37.3 2.6 %collective-permute-start.3 = (bf16[256,128]{1,0:T(8,128)(2,1)S(1)}, bf16[256,128]{1,0:T(8,128)(2,1)S(1)}, u32[]{:S(2)}, u32[]{:S(2)}) collective-permute-start(bf16[256,128]{1,0:T(8,128)(2,1)S(1)} %copy-done.3), channel_id=1, source_target_pairs={{1,0},{2,1},{3,2},{4,3},{5,4},{6,5},{7,6},{8,7},{9,8},{10,9},{11,1... | collective-permute-start | bytes 196616 | tf_op jit(solution)/shard_map/ppermute | solution.py:596
  39.9 0.0 collective-permute-done.2.d3_before
  39.9 0.0 copy-start.4
  39.9 3.0 %collective-permute-done.3.d3_after = bf16[256,128]{1,0:T(8,128)(2,1)S(1)} collective-permute-done((bf16[256,128]{1,0:T(8,128)(2,1)S(1)}, bf16[256,128]{1,0:T(8,128)(2,1)S(1)}, u32[]{:S(2)}, u32[]{:S(2)}) %collective-permute-start.3) | collective-permute-done | bytes 65568 | tf_op jit(solution)/shard_map/ppermute | solution.py:596
  42.9 0.0 copy-start.5
  42.9 0.0 copy-done.4
  42.9 0.6 copy-done.5
  43.5 10.5 %backward.1 = bf16[2560,128]{1,0:T(8,128)(2,1)} custom-call(bf16[256,128]{1,0:T(8,128)(2,1)} %copy-done.4, bf16[256,128]{1,0:T(8,128)(2,1)} %get-tuple-element.36.d3_own, bf16[256,128]{1,0:T(8,128)(2,1)} %copy-done.5, bf16[1728,128]{1,0:T(8,128)(2,1)} %grad_three.1.g3, bf16[512,512]{1,0:T(8,128)(2,1)} %get-tuple-element.38.sl2, ...), custom_call_target="tpu_custom_call" | custom-call | flops 4000000000 | bytes 10534912 | tf_op jit(solution)/shard_map/backward/pallas_call | solution.py:466
  54.0 23.8 %all_to_all.15 = bf16[32,80,128]{2,1,0:T(8,128)(2,1)S(1)} all-to-all(bf16[32,80,128]{2,1,0:T(8,128)(2,1)} %bitcast.10), channel_id=1, replica_groups=mesh['sample'=8,'space'=32] {'space'}, dimensions={0} | all-to-all | bytes 1310720 | tf_op jit(solution)/shard_map/all_to_all | solution.py:586
  77.7 0.1 reduce_sum.24
  77.9 16.3 %all_to_all.16 = bf16[8,80,128]{2,1,0:T(8,128)(2,1)S(1)} all-to-all(bf16[8,80,128]{2,1,0:T(8,128)(2,1)S(1)} %broadcast_in_dim.4), channel_id=1, replica_groups=mesh['sample'=8,'space'=32] {'sample'}, dimensions={0} | all-to-all | bytes 327680 | tf_op jit(solution)/shard_map/all_to_all | solution.py:586
  94.2 0.1 broadcast_in_dim.5
  94.3 18.8 %all_to_all.17 = bf16[32,80,128]{2,1,0:T(8,128)(2,1)} all-to-all(bf16[32,80,128]{2,1,0:T(8,128)(2,1)S(1)} %broadcast_in_dim.5), channel_id=1, replica_groups=mesh['sample'=8,'space'=32] {'space'}, dimensions={0} | all-to-all | bytes 1310720 | tf_op jit(solution)/shard_map/all_to_all | solution.py:586
  113.2 2.3 %finish.1 = (f32[27,4,32]{2,1,0:T(4,128)}, f32[27,32,64]{2,1,0:T(8,128)}, f32[27,64,128]{2,1,0:T(8,128)}) custom-call(f32[3]{0:T(128)} %constant.43.scales, bf16[2560,128]{1,0:T(8,128)(2,1)} %bitcast.9), custom_call_target="tpu_custom_call" | custom-call | tf_op jit(solution)/shard_map/finish/pallas_call | solution.py:575
  (2 shorter events, 0.1 us)
Async XLA Ops:
  0.6 11.3 %copy-start = (bf16[1,8,4,16,128]{4,3,2,1,0:T(8,128)(2,1)S(1)}, bf16[1,8,4,16,128]{4,3,2,1,0:T(8,128)(2,1)}, u32[]{:S(2)}) copy-start(bf16[1,8,4,16,128]{4,3,2,1,0:T(8,128)(2,1)} %param.17) | copy-start | bytes 393220
  0.6 13.2 %collective-permute-start = (bf16[512,128]{1,0:T(8,128)(2,1)}, bf16[512,128]{1,0:T(8,128)(2,1)S(1)}, u32[]{:S(2)}, u32[]{:S(2)}) collective-permute-start(bf16[512,128]{1,0:T(8,128)(2,1)} %bitcast.17), channel_id=1, source_target_pairs={{0,1},{1,2},{2,3},{3,4},{4,5},{5,6},{6,7},{7,8},{8,9},{9,10},{10,1... | collective-permute-start | bytes 393224 | tf_op jit(solution)/shard_map/ppermute | solution.py:596
  11.9 6.3 %collective-permute-start.1 = (bf16[512,128]{1,0:T(8,128)(2,1)S(1)}, bf16[512,128]{1,0:T(8,128)(2,1)S(1)}, u32[]{:S(2)}, u32[]{:S(2)}) collective-permute-start(bf16[512,128]{1,0:T(8,128)(2,1)S(1)} %bitcast.19), channel_id=1, source_target_pairs={{1,0},{2,1},{3,2},{4,3},{5,4},{6,5},{7,6},{8,7},{9,8},{10,9},{11,1... | collective-permute-start | bytes 393224 | tf_op jit(solution)/shard_map/ppermute | solution.py:596
  13.9 4.3 %copy-start.1 = (bf16[512,128]{1,0:T(8,128)(2,1)}, bf16[512,128]{1,0:T(8,128)(2,1)S(1)}, u32[]{:S(2)}) copy-start(bf16[512,128]{1,0:T(8,128)(2,1)S(1)} %collective-permute-done.vol_before) | copy-start | bytes 393220
  18.2 0.7 copy-start.2
  28.8 2.6 %copy-start.3 = (bf16[256,128]{1,0:T(8,128)(2,1)S(1)}, bf16[256,128]{1,0:T(8,128)(2,1)}, u32[]{:S(2)}) copy-start(bf16[256,128]{1,0:T(8,128)(2,1)} %get-tuple-element.36.d3_own) | copy-start | bytes 196612
  31.5 8.4 %collective-permute-start.2 = (bf16[256,128]{1,0:T(8,128)(2,1)S(1)}, bf16[256,128]{1,0:T(8,128)(2,1)S(1)}, u32[]{:S(2)}, u32[]{:S(2)}) collective-permute-start(bf16[256,128]{1,0:T(8,128)(2,1)S(1)} %copy-done.3), channel_id=1, source_target_pairs={{0,1},{1,2},{2,3},{3,4},{4,5},{5,6},{6,7},{7,8},{8,9},{9,10},{10,1... | collective-permute-start | bytes 196616 | tf_op jit(solution)/shard_map/ppermute | solution.py:596
  37.3 5.6 %collective-permute-start.3 = (bf16[256,128]{1,0:T(8,128)(2,1)S(1)}, bf16[256,128]{1,0:T(8,128)(2,1)S(1)}, u32[]{:S(2)}, u32[]{:S(2)}) collective-permute-start(bf16[256,128]{1,0:T(8,128)(2,1)S(1)} %copy-done.3), channel_id=1, source_target_pairs={{1,0},{2,1},{3,2},{4,3},{5,4},{6,5},{7,6},{8,7},{9,8},{10,9},{11,1... | collective-permute-start | bytes 196616 | tf_op jit(solution)/shard_map/ppermute | solution.py:596
  39.9 3.0 %copy-start.4 = (bf16[256,128]{1,0:T(8,128)(2,1)}, bf16[256,128]{1,0:T(8,128)(2,1)S(1)}, u32[]{:S(2)}) copy-start(bf16[256,128]{1,0:T(8,128)(2,1)S(1)} %collective-permute-done.2.d3_before) | copy-start | bytes 196612
  42.9 0.6 copy-start.5

commit v3 on v1

v3 whole, which is shorter than its diff:
```python
import jax
import jax.numpy as jnp
import numpy as np
from jax import lax
from jax.experimental import pallas as pl
from jax.experimental.pallas import tpu as pltpu
from jax.sharding import PartitionSpec as P

BF = jnp.bfloat16
F32 = jnp.float32
SLOT = 80
G_TWO = 1728
G_ONE = 2160
NT = (((1,), (1,)), ((), ()))
TN = (((0,), (0,)), ((), ()))


def table(rows, cols):
    return np.zeros((rows, cols), np.float32)


def one_hot_tables():
    perm = table(108, 640)
    for kd in range(3):
        for kh in range(3):
            for kw in range(3):
                for c in range(4):
                    row = ((kd * 3 + kh) * 3 + kw) * 4 + c
                    perm[row, ((kd * 3 + kw) * 4 + c) * 16 + kh] = 0.5
    shift = table(128, 256)
    for w in range(128):
        if w >= 1:
            shift[w - 1, w] = 1.0
        if w + 1 < 128:
            shift[w + 1, 128 + w] = 1.0
    pair = table(256, 384)
    odd = table(256, 384)
    even = table(128, 384)
    for a in range(2):
        for kw in range(3):
            for w in range(64):
                src = w + kw - 1
                if 0 <= src < 64:
                    pair[128 * a + 2 * src, 128 * kw + 64 * a + w] = 1.0
                    odd[64 + 64 * a + src, 128 * kw + 64 * a + w] = 1.0
                    even[64 * a + src, 128 * kw + 64 * a + w] = 1.0
    squeeze = table(512, 128)
    spread = table(128, 1152)
    grow_g = table(96, 768)
    grow2 = table(128, 512)
    for h in range(4):
        for w in range(32):
            squeeze[128 * h + 2 * w, 32 * h + w] = 1.0
            for kh in range(3):
                for kw in range(3):
                    if 0 <= h + kh - 1 < 4 and 0 <= w + kw - 1 < 32:
                        src = 32 * (h + kh - 1) + w + kw - 1
                        spread[src, 128 * (3 * kh + kw) + 32 * h + w] = 1.0
            for n in range(6):
                src = 32 * (n // 2) + 16 * (h // 2) + w // 2
                grow_g[src, 128 * n + 32 * h + w] = 1.0 / 16
            for d in range(2):
                for u in range(2):
                    grow2[32 * h + w, 128 * h + 64 * d + 2 * w + u] = 1.0 / 16
    grow1 = table(256, 512)
    for e in range(4):
        for w in range(128):
            grow1[64 * e + w // 2, 128 * e + w] = 1.0 / 16
    return [perm, shift, pair, odd, even, squeeze, spread, grow_g, grow2, grow1]


def dot(a, b):
    return jnp.dot(a, b, preferred_element_type=F32)


def inside(index, count):
    return jnp.logical_and(index >= 0, index < count)


def position():
    return lax.axis_index("space"), lax.axis_size("space")


def taps_of(it):
    kd, kw = (it // 3, it % 3)
    return [kd * 9 + kh * 3 + kw for kh in range(3)]


def taps_back(it):
    kd, kw = (2 - it // 3, 2 - it % 3)
    return [kd * 9 + (2 - kh) * 3 + kw for kh in range(3)]


def body(
    vol_own,
    grad_own,
    swap_core,
    swap_chip,
    swap_chip2,
    swap_core2,
    filter_one,
    filter_two,
    filter_three,
    perm,
    shift,
    pair,
    odd,
    even,
    squeeze,
    spread,
    grow_g,
    grow2,
    grow1,
    out,
    t1,
    t2,
    t2r,
    w3t,
    x1,
    pp,
    x2,
    q,
    x3,
    d2c,
    sl1,
    sl2,
    d2,
    d1,
):
    me, blocks = position()
    first_core = me % 2 == 0

    lane = lax.broadcasted_iota(jnp.int32, (32, 640), 1) % 16
    base = lax.dot_general(filter_one[...], perm[...], TN, preferred_element_type=F32)
    for h in range(16):
        moved = pltpu.roll(base, (h - 1) % 640, 1) if h != 1 else base
        if h == 0:
            moved = jnp.where(lane == 15, 0.0, moved)
        if h == 15:
            moved = jnp.where(lane == 0, 0.0, moved)
        t1[32 * h : 32 * h + 32, :] = moved[:, :576].astype(BF)
    for it in range(9):
        w2 = [filter_two[k].astype(F32).T * 0.5 for k in taps_of(it)]
        zero = jnp.zeros((64, 32), F32)
        for s in range(-6, 6):
            if -3 <= s <= 2:
                parts = [w2[s + j] if 0 <= s + j <= 2 else zero for j in range(4)]
                tile = jnp.concatenate(parts, axis=1).astype(BF)
            else:
                tile = jnp.zeros((64, 128), BF)
            for m in range(2):
                h = 4 * m + 1 - s
                if 0 <= h < 8:
                    t2[64 * h : 64 * h + 64, it * 256 + 128 * m : it * 256 + 128 * m + 128] = tile
    for it in range(9):
        v2 = [filter_two[k].astype(F32) for k in taps_back(it)]
        zero = jnp.zeros((32, 64), F32)
        for s in range(-6, 8):
            if -1 <= s <= 2:
                parts = [v2[s + j] if 0 <= s + j <= 2 else zero for j in range(2)]
                tile = jnp.concatenate(parts, axis=1).astype(BF)
            else:
                tile = jnp.zeros((32, 128), BF)
            for m in range(4):
                hp = 2 * m + 1 - s
                if 0 <= hp < 8:
                    t2r[32 * hp : 32 * hp + 32, it * 512 + 128 * m : it * 512 + 128 * m + 128] = tile
    w3t[...] = (filter_three[...].astype(F32).T * 0.5).astype(BF)

    def either(a, b, lo, hi):
        return jnp.where(first_core, a[lo:hi, :], b[lo:hi, :])

    at = 0
    for rows in (
        either(swap_chip2, swap_core2, 64, 512),
        either(swap_chip, swap_core, 0, 512),
        vol_own[...],
        either(swap_core, swap_chip, 0, 512),
        either(swap_core2, swap_chip2, 0, 448),
    ):
        moved = dot(rows, shift[...]).astype(BF)
        count = rows.shape[0] // 64
        for p in range(count):
            lanes = slice(128 * (at + p), 128 * (at + p) + 128)
            x1[0:64, lanes] = moved[64 * p : 64 * p + 64, :128]
            x1[64:128, lanes] = rows[64 * p : 64 * p + 64, :]
            x1[128:192, lanes] = moved[64 * p : 64 * p + 64, 128:]
        at += count

    for j in range(18):
        rhs = jnp.concatenate(
            [x1[:, (2 * j + kd) * 128 : (2 * j + kd) * 128 + 256] for kd in range(3)], axis=0
        )
        half = dot(t1[...], rhs)
        t = jnp.tanh(half)
        if 7 <= j < 11:
            slope = (1.0 + t) + half * (1.0 - t * t)
            sl1[:, (j - 7) * 256 : (j - 7) * 256 + 256] = slope.astype(BF)
        act = half + half * t
        act = act[:, :128] + act[:, 128:]
        act = act.reshape(8, 2, 32, 128)
        act = (act[:, 0] + act[:, 1]).reshape(256, 128)
        act = act + pltpu.roll(act, 127, 1)
        scale = jnp.where(inside(4 * me - 7 + j, 4 * blocks), 0.125, 0.0)
        pp[:, j * 128 : j * 128 + 128] = (act * scale).astype(BF)

    for first in range(17):
        got = dot(pp[:, first * 128 : first * 128 + 256], pair[...]).astype(BF)
        for kd in range(3):
            m = (first - kd) // 2
            if (first - kd) % 2 == 0 and 0 <= m < 8:
                for kw in range(3):
                    k = 3 * kd + kw
                    x2[256 * k : 256 * k + 256, m * 128 : m * 128 + 128] = got[
                        :, 128 * kw : 128 * kw + 128
                    ]

    for c in range(4):
        lanes = slice(c * 256, c * 256 + 256)
        half = dot(t2[...], x2[:, lanes])
        t = jnp.tanh(half)
        if 1 <= c < 3:
            slope = (1.0 + t) + half * (1.0 - t * t)
            sl2[:, c * 256 - 256 : c * 256] = slope.astype(BF)
        act = (half + half * t).reshape(4, 2, 64, 256)
        act = (act[:, 0] + act[:, 1]).reshape(256, 256)
        for u in range(2):
            tile = act[:, 128 * u : 128 * u + 128]
            tile = tile + pltpu.roll(tile, 64, 1)
            tile = tile + pltpu.roll(tile, 127, 1)
            m = 2 * c + u
            scale = jnp.where(inside(2 * me - 3 + m, 2 * blocks), 0.125, 0.0)
            tile = (tile * scale).astype(BF)
            for h in range(4):
                q[64 * m : 64 * m + 64, 128 * h : 128 * h + 128] = tile[64 * h : 64 * h + 64, :]

    packed = dot(q[...], squeeze[...]).astype(BF)
    got = dot(packed, spread[...]).astype(BF)
    for kd in range(3):
        for s in range(9):
            k = 9 * kd + s
            for n in range(6):
                x3[64 * k : 64 * k + 64, 128 * n : 128 * n + 128] = got[
                    64 * (n + kd) : 64 * (n + kd) + 64, 128 * s : 128 * s + 128
                ]
    rows = jnp.concatenate(
        [
            either(swap_chip, swap_core, 512, 544),
            grad_own[...],
            either(swap_core, swap_chip, 512, 544),
        ],
        axis=0,
    )
    grown = dot(rows.astype(F32).T.astype(BF), grow_g[...])
    half = dot(w3t[...], x3[...])
    t = jnp.tanh(half)
    d3 = (grown * ((1.0 + t) + half * (1.0 - t * t))).astype(BF)

    out[:G_TWO, :] = lax.dot_general(
        x3[:, 256:512], d3[:, 256:512], NT, preferred_element_type=F32
    ).astype(BF)

    lane = lax.broadcasted_iota(jnp.int32, (64, 128), 1)
    col, line = (lane % 32, lane // 32)
    masks = []
    for b in range(3):
        for c in range(3):
            keep = inside(col + 1 - c, 32)
            masks.append(jnp.logical_and(keep, inside(line + 1 - b, 4)))
    grown = []
    for n in range(4):
        total = None
        for b in range(3):
            for c in range(3):
                part = None
                for a in range(3):
                    k = 9 * a + 3 * b + c
                    plane = n + 2 - a
                    got = dot(
                        filter_three[64 * k : 64 * k + 64, :], d3[:, 128 * plane : 128 * plane + 128]
                    )
                    part = got if part is None else part + got
                move_by = -(32 * (1 - b) + 1 - c) % 128
                if move_by:
                    part = jnp.where(masks[3 * b + c], pltpu.roll(part, move_by, 1), 0.0)
                total = part if total is None else total + part
        scale = jnp.where(inside(2 * me - 1 + n, 2 * blocks), 1.0, 0.0)
        grown.append((total * scale).astype(BF))
    back = dot(jnp.concatenate(grown, axis=0), grow2[...])
    for h in range(8):
        rows = slice(64 * h, 64 * h + 64)
        for n in range(4):
            lanes = slice(128 * n, 128 * n + 128)
            source = back[64 * n : 64 * n + 64, 128 * (h // 2) : 128 * (h // 2) + 128]
            d2[rows, lanes] = (source * sl2[rows, lanes].astype(F32)).astype(BF)

    for start in range(1, 6):
        u = start // 2
        if start % 2:
            got = dot(d2[:, 128 * u : 128 * u + 256], odd[...])
        else:
            got = dot(d2[:, 128 * u : 128 * u + 128], even[...])
        got = got.astype(BF)
        for kd in range(3):
            for m in range(2):
                if 1 + kd + 2 * m == start:
                    for kw in range(3):
                        k = 3 * kd + kw
                        d2c[512 * k : 512 * k + 512, 128 * m : 128 * m + 128] = got[
                            :, 128 * kw : 128 * kw + 128
                        ]
    back = dot(t2r[...], d2c[...]).astype(BF)
    back = dot(back, grow1[...])
    for h in range(16):
        rows = slice(32 * h, 32 * h + 32)
        source = back[32 * (h // 2) : 32 * (h // 2) + 32, :]
        for e in range(8):
            lanes = slice(128 * e, 128 * e + 128)
            delta = source[:, 128 * (e // 2) : 128 * (e // 2) + 128] * sl1[rows, lanes].astype(F32)
            d1[rows, lanes] = delta.astype(BF)

    lane16 = lax.broadcasted_iota(jnp.int32, (16, 128), 1)
    all_two = lax.dot_general(
        x2[:, 384:640], d2[:, 128:384], NT, preferred_element_type=F32
    )
    for it in range(9):
        got = all_two[256 * it : 256 * it + 256, :]
        for kh, k in enumerate(taps_of(it)):
            totals = [None, None]
            for h in range(8):
                hp = h + kh - 1
                if 0 <= hp < 8:
                    part = got[32 * hp : 32 * hp + 32, 128 * (h // 2) : 128 * (h // 2) + 128]
                    now = totals[h % 2]
                    totals[h % 2] = part if now is None else now + part
            low = totals[0] + pltpu.roll(totals[1], 64, 1)
            high = pltpu.roll(totals[0], 64, 1) + totals[1]
            out[G_TWO + k * 16 : G_TWO + k * 16 + 16, :] = jnp.where(
                lane16 < 64, low[:16], high[16:]
            ).astype(BF)

    lhs = jnp.concatenate([x1[:, 128 * (14 + kd) : 128 * (14 + kd) + 1024] for kd in range(3)], axis=0)
    got = lax.dot_general(lhs, d1[...], NT, preferred_element_type=F32)
    row = lax.broadcasted_iota(jnp.int32, (576, 128), 0) % 16
    col = lax.broadcasted_iota(jnp.int32, (576, 128), 1) // 32
    lane36 = lax.broadcasted_iota(jnp.int32, (36, 128), 1)
    packed = jnp.zeros((36, 128), F32)
    for kh in range(3):
        total = jnp.zeros((576, 128), F32)
        for u in range(4):
            keep = row == col + (4 * u + kh - 1)
            total = total + jnp.where(keep, got[:, 128 * u : 128 * u + 128], 0.0)
        total = total.reshape(36, 16, 128).sum(axis=1)
        total = total + pltpu.roll(total, 64, 1)
        total = total + pltpu.roll(total, 32, 1)
        packed = packed + jnp.where(lane36 // 32 == kh, total, 0.0)
    out[G_ONE : G_ONE + 48, :] = jnp.concatenate(
        [packed, jnp.zeros((12, 128), F32)], axis=0
    ).astype(BF)
    out[G_ONE + 48 :, :] = jnp.zeros((out.shape[0] - G_ONE - 48, 128), BF)


def finish(scales, flat, one, two, three):
    for k in range(27):
        three[k] = flat[64 * k : 64 * k + 64, :].astype(F32) * scales[2]
        got = flat[G_TWO + 16 * k : G_TWO + 16 * k + 16, :].astype(F32) * scales[1]
        two[k, 0:16, :] = got[:, :64]
        two[k, 16:32, :] = got[:, 64:]
    got = flat[G_ONE : G_ONE + 48, :].astype(F32) * scales[0]
    for it in range(9):
        for kh, k in enumerate(taps_of(it)):
            one[k] = got[4 * it : 4 * it + 4, 32 * kh : 32 * kh + 32]


VMEM = pl.BlockSpec(memory_space=pltpu.VMEM)


def near(*shape):
    return pltpu.VMEM(shape, BF)


def local_grads(volume, grad, swaps, filter_one, filter_two, filter_three, rows):
    tables = [jnp.asarray(t, BF) for t in one_hot_tables()]
    args = [volume, grad, *swaps, filter_one, filter_two, filter_three, *tables]
    return pl.pallas_call(
        body,
        out_shape=jax.ShapeDtypeStruct((rows, 128), BF),
        in_specs=[VMEM] * len(args),
        out_specs=VMEM,
        scratch_shapes=[
            near(512, 576),
            near(512, 2304),
            near(256, 4608),
            near(128, 1728),
            near(192, 38 * 128),
            near(256, 18 * 128),
            near(2304, 1024),
            near(512, 512),
            near(1728, 768),
            near(4608, 256),
            near(512, 1024),
            near(512, 512),
            near(512, 512),
            near(512, 1024),
        ],
        compiler_params=pltpu.CompilerParams(vmem_limit_bytes=58 * 1024 * 1024),
        name="local_grads",
    )(*args)


def run_finish(flat, cells):
    scales = 1.0 / jnp.sqrt(jnp.array([cells, cells / 8.0, cells / 64.0], F32))
    shapes = [(27, 4, 32), (27, 32, 64), (27, 64, 128)]
    outs = pl.pallas_call(
        finish,
        out_shape=[jax.ShapeDtypeStruct(shape, F32) for shape in shapes],
        in_specs=[pl.BlockSpec(memory_space=pltpu.SMEM), VMEM],
        out_specs=[VMEM] * 3,
        name="finish",
    )(scales, flat)
    return tuple(o.reshape(3, 3, 3, *o.shape[1:]) for o in outs)


def exchange(pieces, axis):
    return lax.all_to_all(pieces, axis, 0, 0, tiled=True)


def total_of(got):
    return got.astype(F32).sum(axis=0).astype(BF)


def swap(values, first):
    size = lax.axis_size("space")
    pairs = [(i, i + 1) for i in range(first, size - 1, 2)]
    return lax.ppermute(values, "space", pairs + [(j, i) for i, j in pairs])


def per_device(volume, grad_out, filter_one, filter_two, filter_three):
    spaces, samples = (lax.axis_size("space"), lax.axis_size("sample"))
    own = volume.reshape(512, 128)
    grad = grad_out.reshape(32, 128)
    both = jnp.concatenate([own, grad], axis=0)
    swap_core = swap(both, 0)
    swap_chip = swap(both, 1)
    swap_chip2 = swap(swap_core, 1)
    swap_core2 = swap(swap_chip, 0)
    flat = local_grads(
        own,
        grad,
        (swap_core, swap_chip, swap_chip2, swap_core2),
        filter_one.reshape(108, 32),
        filter_two.reshape(27, 32, 64),
        filter_three.reshape(1728, 128),
        spaces * SLOT,
    )
    part = total_of(exchange(flat.reshape(spaces, SLOT, 128), "space"))
    part = total_of(exchange(jnp.broadcast_to(part[None], (samples, SLOT, 128)), "sample"))
    flat = exchange(jnp.broadcast_to(part[None], (spaces, SLOT, 128)), "space")
    cells = float(samples * spaces * volume.shape[1] * volume.shape[3] * volume.shape[4])
    return run_finish(flat.reshape(-1, 128), cells)


def solution(mesh):
    return jax.shard_map(
        per_device,
        mesh=mesh,
        in_specs=(
            P(("sample", "space"), None, None, None, None),
            P(("sample", "space"), None, None, None, None),
            P(),
            P(),
            P(),
        ),
        out_specs=(P(), P(), P()),
        check_vma=False,
    )
```

time: 115 us -> 96.3 us (0.84)
  Pallas kernels: 33.5 us -> 20.6 us
  other arithmetic: 4.34 us -> 1.07 us
  starting transfers between devices: 10.8 us -> 8.34 us
  local copies, waits for them, and re-layouts: 3.48 us -> 1.4 us
  waiting for transfers between devices: 3.45 us -> 4.7 us
    pallas_call x1, Pallas kernels: 33.5 us -> 18.3 us  [local_grads(): pl.pallas_call(body, out_shape=jax.ShapeDtypeStruct((rows, 128), BF), in_...]
    ppermute x4, starting transfers between devices: 10.8 us -> 8.34 us  [swap(): return lax.ppermute(values, 'space', pairs + [(j, i) for i, j in pairs])]
    pallas_call x0 -> x1, Pallas kernels: none -> 2.29 us  [run_finish(): pl.pallas_call(finish, out_shape=[jax.ShapeDtypeStruct(shape, F32) for sh...]
    div x3 -> x0, other arithmetic: 1.81 us -> none  [the longest x1 0.97 us: per_device(): g_three / jnp.sqrt(jnp.float32(cells / 64.0))]
    ppermute x4, waiting for transfers between devices: 3.45 us -> 4.7 us  [swap(): return lax.ppermute(values, 'space', pairs + [(j, i) for i, j in pairs])]
  transfers between devices with their start and end apart: 4 -> 4, of which waited for: 1 -> 2; matrix products, arithmetic and copies ran while one was open for 3% -> 1% of each run, Pallas kernels for 0% -> 0%
where the time goes in v3:
time: 96.3 us; the launch traced here: 95.9 us
  blocking collectives  59.1 us (61%)
  Pallas kernels  20.6 us (21%)
  starting transfers between devices  8.34 us (9%)
  waiting for transfers between devices  4.7 us (5%)
  local copies, waits for them, and re-layouts  1.4 us (1%)
  other arithmetic  1.07 us (1%)
    all_to_all x3, blocking collectives, exchange(): return lax.all_to_all(pieces, axis, 0, 0, tiled=True)  59.1 us
    pallas_call x1, Pallas kernels, local_grads(): pl.pallas_call(body, out_shape=jax.ShapeDtypeStruct((rows, 128), BF), in_...  18.3 us
    ppermute x4, starting transfers between devices, swap(): return lax.ppermute(values, 'space', pairs + [(j, i) for i, j in pairs])  8.34 us
    ppermute x4, waiting for transfers between devices, swap(): return lax.ppermute(values, 'space', pairs + [(j, i) for i, j in pairs])  4.7 us
    pallas_call x1, Pallas kernels, run_finish(): pl.pallas_call(finish, out_shape=[jax.ShapeDtypeStruct(shape, F32) for sh...  2.29 us
  transfers between devices with their start and end apart: 4, of which 2 were waited for; matrix products, arithmetic and copies ran while one was open for 1% of the time, Pallas kernels for 0%

profile of v3, /device:TPU:1, one launch (start us, length us, event | category | flops | bytes accessed | tf_op | source)
XLA Modules:
  0.0 95.9 jit_solution(6638964332561842675)
XLA Ops:
  0.6 0.0 copy-start.4
  0.6 0.9 pad_maximum_fusion
  1.6 4.5 %collective-permute-start.1 = (bf16[544,128]{1,0:T(8,128)(2,1)S(1)}, bf16[544,128]{1,0:T(8,128)(2,1)S(1)}, u32[]{:S(2)}, u32[]{:S(2)}) collective-permute-start(bf16[544,128]{1,0:T(8,128)(2,1)S(1)} %pad_maximum_fusion), channel_id=1, source_target_pairs={{1,2},{3,4},{5,6},{7,8},{9,10},{11,12},{13,14},{15,16},{17,18},{19... | collective-permute-start | bytes 417800 | tf_op jit(solution)/shard_map/ppermute | solution.py:435
  6.1 0.1 collective-permute-start
  6.2 2.6 %collective-permute-done.1.swap_chip = bf16[544,128]{1,0:T(8,128)(2,1)S(1)} collective-permute-done((bf16[544,128]{1,0:T(8,128)(2,1)S(1)}, bf16[544,128]{1,0:T(8,128)(2,1)S(1)}, u32[]{:S(2)}, u32[]{:S(2)}) %collective-permute-start.1) | collective-permute-done | bytes 139296 | tf_op jit(solution)/shard_map/ppermute | solution.py:435
  8.8 0.0 copy-start
  8.8 0.0 collective-permute-start.3
  8.8 0.0 collective-permute-done.swap_core
  8.8 0.0 copy-start.1
  8.8 3.7 %collective-permute-start.2 = (bf16[544,128]{1,0:T(8,128)(2,1)S(1)}, bf16[544,128]{1,0:T(8,128)(2,1)S(1)}, u32[]{:S(2)}, u32[]{:S(2)}) collective-permute-start(bf16[544,128]{1,0:T(8,128)(2,1)S(1)} %collective-permute-done.swap_core), channel_id=1, source_target_pairs={{1,2},{3,4},{5,6},{7,8},{9,10},{11,12},{13,14},{15,16},{17,18},{19... | collective-permute-start | bytes 417800 | tf_op jit(solution)/shard_map/ppermute | solution.py:435
  12.6 0.0 copy-done.4
  12.6 0.6 reshape.40.filter_one
  13.2 0.0 collective-permute-done.3.swap_core2
  13.2 0.0 copy-start.2
  13.2 2.1 %collective-permute-done.2.swap_chip2 = bf16[544,128]{1,0:T(8,128)(2,1)S(1)} collective-permute-done((bf16[544,128]{1,0:T(8,128)(2,1)S(1)}, bf16[544,128]{1,0:T(8,128)(2,1)S(1)}, u32[]{:S(2)}, u32[]{:S(2)}) %collective-permute-start.2) | collective-permute-done | bytes 139296 | tf_op jit(solution)/shard_map/ppermute | solution.py:435
  15.3 0.0 copy-start.3
  15.3 0.0 copy-done
  15.3 0.0 copy-done.1
  15.3 0.0 copy-done.2
  15.3 0.6 copy-done.3
  16.0 18.3 %local_grads.1 = bf16[2560,128]{1,0:T(8,128)(2,1)} custom-call(bf16[512,128]{1,0:T(8,128)(2,1)} %bitcast.12, bf16[32,128]{1,0:T(8,128)(2,1)} %bitcast.16, bf16[544,128]{1,0:T(8,128)(2,1)} %copy-done.1, bf16[544,128]{1,0:T(8,128)(2,1)} %copy-done, bf16[544,128]{1,0:T(8,128)(2,1)} %copy-done.3, bf16[544,128]{1,0:T(8,128)(2,1)} %copy-done.2, ...), custom_call_target="tpu_custom_call" | custom-call | tf_op jit(solution)/shard_map/local_grads/pallas_call | solution.py:385
  34.3 23.9 %all_to_all.15 = bf16[32,80,128]{2,1,0:T(8,128)(2,1)S(1)} all-to-all(bf16[32,80,128]{2,1,0:T(8,128)(2,1)} %bitcast.9), channel_id=1, replica_groups=mesh['sample'=8,'space'=32] {'space'}, dimensions={0} | all-to-all | bytes 1310720 | tf_op jit(solution)/shard_map/all_to_all | solution.py:425
  58.2 0.1 reduce_sum.24
  58.4 16.4 %all_to_all.16 = bf16[8,80,128]{2,1,0:T(8,128)(2,1)S(1)} all-to-all(bf16[8,80,128]{2,1,0:T(8,128)(2,1)S(1)} %broadcast_in_dim.4), channel_id=1, replica_groups=mesh['sample'=8,'space'=32] {'sample'}, dimensions={0} | all-to-all | bytes 327680 | tf_op jit(solution)/shard_map/all_to_all | solution.py:425
  74.7 0.1 broadcast_in_dim.5
  74.8 18.8 %all_to_all.17 = bf16[32,80,128]{2,1,0:T(8,128)(2,1)} all-to-all(bf16[32,80,128]{2,1,0:T(8,128)(2,1)S(1)} %broadcast_in_dim.5), channel_id=1, replica_groups=mesh['sample'=8,'space'=32] {'space'}, dimensions={0} | all-to-all | bytes 1310720 | tf_op jit(solution)/shard_map/all_to_all | solution.py:425
  93.7 2.3 %finish.1 = (f32[27,4,32]{2,1,0:T(4,128)}, f32[27,32,64]{2,1,0:T(8,128)}, f32[27,64,128]{2,1,0:T(8,128)}) custom-call(f32[3]{0:T(128)} %constant.40.scales, bf16[2560,128]{1,0:T(8,128)(2,1)} %bitcast.10), custom_call_target="tpu_custom_call" | custom-call | tf_op jit(solution)/shard_map/finish/pallas_call | solution.py:414
  (2 shorter events, 0.1 us)
Async XLA Ops:
  0.6 12.0 %copy-start.4 = (bf16[3,3,3,4,32]{4,3,2,1,0:T(4,128)(2,1)S(1)}, bf16[3,3,3,4,32]{4,3,2,1,0:T(4,128)(2,1)}, u32[]{:S(2)}) copy-start(bf16[3,3,3,4,32]{4,3,2,1,0:T(4,128)(2,1)} %param.18) | copy-start | bytes 20740
  1.6 7.2 %collective-permute-start.1 = (bf16[544,128]{1,0:T(8,128)(2,1)S(1)}, bf16[544,128]{1,0:T(8,128)(2,1)S(1)}, u32[]{:S(2)}, u32[]{:S(2)}) collective-permute-start(bf16[544,128]{1,0:T(8,128)(2,1)S(1)} %pad_maximum_fusion), channel_id=1, source_target_pairs={{1,2},{3,4},{5,6},{7,8},{9,10},{11,12},{13,14},{15,16},{17,18},{19... | collective-permute-start | bytes 417800 | tf_op jit(solution)/shard_map/ppermute | solution.py:435
  6.1 2.7 %collective-permute-start = (bf16[544,128]{1,0:T(8,128)(2,1)S(1)}, bf16[544,128]{1,0:T(8,128)(2,1)S(1)}, u32[]{:S(2)}, u32[]{:S(2)}) collective-permute-start(bf16[544,128]{1,0:T(8,128)(2,1)S(1)} %pad_maximum_fusion), channel_id=1, source_target_pairs={{0,1},{2,3},{4,5},{6,7},{8,9},{10,11},{12,13},{14,15},{16,17},{18,... | collective-permute-start | bytes 417800 | tf_op jit(solution)/shard_map/ppermute | solution.py:435
  8.8 6.5 %copy-start = (bf16[544,128]{1,0:T(8,128)(2,1)}, bf16[544,128]{1,0:T(8,128)(2,1)S(1)}, u32[]{:S(2)}) copy-start(bf16[544,128]{1,0:T(8,128)(2,1)S(1)} %collective-permute-done.1.swap_chip) | copy-start | bytes 417796
  8.8 4.4 %collective-permute-start.3 = (bf16[544,128]{1,0:T(8,128)(2,1)S(1)}, bf16[544,128]{1,0:T(8,128)(2,1)S(1)}, u32[]{:S(2)}, u32[]{:S(2)}) collective-permute-start(bf16[544,128]{1,0:T(8,128)(2,1)S(1)} %collective-permute-done.1.swap_chip), channel_id=1, source_target_pairs={{0,1},{2,3},{4,5},{6,7},{8,9},{10,11},{12,13},{14,15},{16,17},{18,... | collective-permute-start | bytes 417800 | tf_op jit(solution)/shard_map/ppermute | solution.py:435
  8.8 6.5 %copy-start.1 = (bf16[544,128]{1,0:T(8,128)(2,1)}, bf16[544,128]{1,0:T(8,128)(2,1)S(1)}, u32[]{:S(2)}) copy-start(bf16[544,128]{1,0:T(8,128)(2,1)S(1)} %collective-permute-done.swap_core) | copy-start | bytes 417796
  8.8 6.5 %collective-permute-start.2 = (bf16[544,128]{1,0:T(8,128)(2,1)S(1)}, bf16[544,128]{1,0:T(8,128)(2,1)S(1)}, u32[]{:S(2)}, u32[]{:S(2)}) collective-permute-start(bf16[544,128]{1,0:T(8,128)(2,1)S(1)} %collective-permute-done.swap_core), channel_id=1, source_target_pairs={{1,2},{3,4},{5,6},{7,8},{9,10},{11,12},{13,14},{15,16},{17,18},{19... | collective-permute-start | bytes 417800 | tf_op jit(solution)/shard_map/ppermute | solution.py:435
  13.2 2.1 %copy-start.2 = (bf16[544,128]{1,0:T(8,128)(2,1)}, bf16[544,128]{1,0:T(8,128)(2,1)S(1)}, u32[]{:S(2)}) copy-start(bf16[544,128]{1,0:T(8,128)(2,1)S(1)} %collective-permute-done.3.swap_core2) | copy-start | bytes 417796
  15.3 0.7 copy-start.3

commit v4 on v3

--- a/solution.py
+++ b/solution.py
@@ -9,6 +9,7 @@
 BF = jnp.bfloat16
 F32 = jnp.float32
 SLOT = 80
+LIMIT = 44
 G_TWO = 1728
 G_ONE = 2160
 NT = (((1,), (1,)), ((), ()))
@@ -91,6 +92,50 @@
     return [kd * 9 + (2 - kh) * 3 + kw for kh in range(3)]
 
 
+def build(filter_one, filter_two, filter_three, perm, t1, t2, w3t, t2r, s1, s2, s3, s2r, sems):
+    copies = [
+        pltpu.make_async_copy(near_ref, far_ref, sems.at[i])
+        for i, (near_ref, far_ref) in enumerate(((s1, t1), (s2, t2), (s3, w3t), (s2r, t2r)))
+    ]
+    for it in range(9):
+        v2 = [filter_two[k].astype(F32) for k in taps_back(it)]
+        zero = jnp.zeros((32, 64), F32)
+        for s in range(-6, 8):
+            if -1 <= s <= 2:
+                parts = [v2[s + j] if 0 <= s + j <= 2 else zero for j in range(2)]
+                tile = jnp.concatenate(parts, axis=1).astype(BF)
+            else:
+                tile = jnp.zeros((32, 128), BF)
+            for m in range(4):
+                hp = 2 * m + 1 - s
+                if 0 <= hp < 8:
+                    s2r[32 * hp : 32 * hp + 32, it * 512 + 128 * m : it * 512 + 128 * m + 128] = tile
+    copies[3].start()
+    taps = []
+    for kh in range(3):
+        rows = jnp.concatenate([filter_two[taps_of(it)[kh]] for it in range(9)], axis=0)
+        taps.append(rows.astype(F32).T * 0.5)
+    zero = jnp.zeros((64, 288), F32)
+    for s in range(5):
+        parts = [taps[p - s + 1] if 0 <= p - s + 1 < 3 else zero for p in range(5)]
+        s2[64 * s : 64 * s + 64, :] = jnp.concatenate(parts, axis=1).astype(BF)
+    copies[1].start()
+    s3[...] = (filter_three[...].astype(F32).T * 0.5).astype(BF)
+    copies[2].start()
+    lane = lax.broadcasted_iota(jnp.int32, (32, 640), 1) % 16
+    base = lax.dot_general(filter_one[...], perm[...], TN, preferred_element_type=F32)
+    for h in range(16):
+        moved = pltpu.roll(base, (h - 1) % 640, 1) if h != 1 else base
+        if h == 0:
+            moved = jnp.where(lane == 15, 0.0, moved)
+        if h == 15:
+            moved = jnp.where(lane == 0, 0.0, moved)
+        s1[32 * h : 32 * h + 32, :] = moved[:, :576].astype(BF)
+    copies[0].start()
+    for copy in copies:
+        copy.wait()
+
+
 def body(
     vol_own,
     grad_own,
@@ -98,10 +143,11 @@
     swap_chip,
     swap_chip2,
     swap_core2,
-    filter_one,
-    filter_two,
     filter_three,
-    perm,
+    t1_far,
+    t2_far,
+    w3t_far,
+    t2r_far,
     shift,
     pair,
     odd,
@@ -114,8 +160,8 @@
     out,
     t1,
     t2,
+    w3t,
     t2r,
-    w3t,
     x1,
     pp,
     x2,
@@ -126,53 +172,23 @@
     sl2,
     d2,
     d1,
+    sems,
 ):
     me, blocks = position()
     first_core = me % 2 == 0
-
-    lane = lax.broadcasted_iota(jnp.int32, (32, 640), 1) % 16
-    base = lax.dot_general(filter_one[...], perm[...], TN, preferred_element_type=F32)
-    for h in range(16):
-        moved = pltpu.roll(base, (h - 1) % 640, 1) if h != 1 else base
-        if h == 0:
-            moved = jnp.where(lane == 15, 0.0, moved)
-        if h == 15:
-            moved = jnp.where(lane == 0, 0.0, moved)
-        t1[32 * h : 32 * h + 32, :] = moved[:, :576].astype(BF)
-    for it in range(9):
-        w2 = [filter_two[k].astype(F32).T * 0.5 for k in taps_of(it)]
-        zero = jnp.zeros((64, 32), F32)
-        for s in range(-6, 6):
-            if -3 <= s <= 2:
-                parts = [w2[s + j] if 0 <= s + j <= 2 else zero for j in range(4)]
-                tile = jnp.concatenate(parts, axis=1).astype(BF)
-            else:
-                tile = jnp.zeros((64, 128), BF)
-            for m in range(2):
-                h = 4 * m + 1 - s
-                if 0 <= h < 8:
-                    t2[64 * h : 64 * h + 64, it * 256 + 128 * m : it * 256 + 128 * m + 128] = tile
-    for it in range(9):
-        v2 = [filter_two[k].astype(F32) for k in taps_back(it)]
-        zero = jnp.zeros((32, 64), F32)
-        for s in range(-6, 8):
-            if -1 <= s <= 2:
-                parts = [v2[s + j] if 0 <= s + j <= 2 else zero for j in range(2)]
-                tile = jnp.concatenate(parts, axis=1).astype(BF)
-            else:
-                tile = jnp.zeros((32, 128), BF)
-            for m in range(4):
-                hp = 2 * m + 1 - s
-                if 0 <= hp < 8:
-                    t2r[32 * hp : 32 * hp + 32, it * 512 + 128 * m : it * 512 + 128 * m + 128] = tile
-    w3t[...] = (filter_three[...].astype(F32).T * 0.5).astype(BF)
+    copies = []
+    for i, (far_ref, near_ref) in enumerate(
+        ((t1_far, t1), (t2_far, t2), (w3t_far, w3t), (t2r_far, t2r))
+    ):
+        copies.append(pltpu.make_async_copy(far_ref, near_ref, sems.at[i]))
+        copies[-1].start()
 
     def either(a, b, lo, hi):
         return jnp.where(first_core, a[lo:hi, :], b[lo:hi, :])
 
     at = 0
     for rows in (
-        either(swap_chip2, swap_core2, 64, 512),
+        either(swap_chip2, swap_core2, 0, 448),
         either(swap_chip, swap_core, 0, 512),
         vol_own[...],
         either(swap_core, swap_chip, 0, 512),
@@ -187,6 +203,7 @@
             x1[128:192, lanes] = moved[64 * p : 64 * p + 64, 128:]
         at += count
 
+    copies[0].wait()
     for j in range(18):
         rhs = jnp.concatenate(
             [x1[:, (2 * j + kd) * 128 : (2 * j + kd) * 128 + 256] for kd in range(3)], axis=0
@@ -215,24 +232,35 @@
                         :, 128 * kw : 128 * kw + 128
                     ]
 
+    copies[1].wait()
     for c in range(4):
         lanes = slice(c * 256, c * 256 + 256)
-        half = dot(t2[...], x2[:, lanes])
-        t = jnp.tanh(half)
-        if 1 <= c < 3:
-            slope = (1.0 + t) + half * (1.0 - t * t)
-            sl2[:, c * 256 - 256 : c * 256] = slope.astype(BF)
-        act = (half + half * t).reshape(4, 2, 64, 256)
-        act = (act[:, 0] + act[:, 1]).reshape(256, 256)
-        for u in range(2):
-            tile = act[:, 128 * u : 128 * u + 128]
-            tile = tile + pltpu.roll(tile, 64, 1)
-            tile = tile + pltpu.roll(tile, 127, 1)
-            m = 2 * c + u
-            scale = jnp.where(inside(2 * me - 3 + m, 2 * blocks), 0.125, 0.0)
-            tile = (tile * scale).astype(BF)
-            for h in range(4):
-                q[64 * m : 64 * m + 64, 128 * h : 128 * h + 128] = tile[64 * h : 64 * h + 64, :]
+        for g in range(2):
+            rhs = jnp.concatenate(
+                [
+                    x2[256 * it + 32 * p : 256 * it + 32 * p + 32, lanes]
+                    for p in range(3 * g, 3 * g + 5)
+                    for it in range(9)
+                ],
+                axis=0,
+            )
+            half = dot(t2[64 * g : 64 * g + 256, :], rhs)
+            t = jnp.tanh(half)
+            if 1 <= c < 3:
+                slope = (1.0 + t) + half * (1.0 - t * t)
+                sl2[256 * g : 256 * g + 256, c * 256 - 256 : c * 256] = slope.astype(BF)
+            act = (half + half * t).reshape(2, 2, 64, 256)
+            act = (act[:, 0] + act[:, 1]).reshape(128, 256)
+            for u in range(2):
+                tile = act[:, 128 * u : 128 * u + 128]
+                tile = tile + pltpu.roll(tile, 64, 1)
+                tile = tile + pltpu.roll(tile, 127, 1)
+                m = 2 * c + u
+                scale = jnp.where(inside(2 * me - 3 + m, 2 * blocks), 0.125, 0.0)
+                tile = (tile * scale).astype(BF)
+                for h in range(2):
+                    lo = 128 * (2 * g + h)
+                    q[64 * m : 64 * m + 64, lo : lo + 128] = tile[64 * h : 64 * h + 64, :]
 
     packed = dot(q[...], squeeze[...]).astype(BF)
     got = dot(packed, spread[...]).astype(BF)
@@ -245,13 +273,14 @@
                 ]
     rows = jnp.concatenate(
         [
-            either(swap_chip, swap_core, 512, 544),
+            either(swap_chip2, swap_core2, 448, 480),
             grad_own[...],
-            either(swap_core, swap_chip, 512, 544),
+            either(swap_core2, swap_chip2, 448, 480),
         ],
         axis=0,
     )
     grown = dot(rows.astype(F32).T.astype(BF), grow_g[...])
+    copies[2].wait()
     half = dot(w3t[...], x3[...])
     t = jnp.tanh(half)
     d3 = (grown * ((1.0 + t) + half * (1.0 - t * t))).astype(BF)
@@ -267,25 +296,30 @@
         for c in range(3):
             keep = inside(col + 1 - c, 32)
             masks.append(jnp.logical_and(keep, inside(line + 1 - b, 4)))
+    lhs = jnp.concatenate([filter_three[576 * a : 576 * a + 576, :] for a in range(3)], axis=1)
     grown = []
-    for n in range(4):
-        total = None
-        for b in range(3):
-            for c in range(3):
-                part = None
-                for a in range(3):
-                    k = 9 * a + 3 * b + c
-                    plane = n + 2 - a
-                    got = dot(
-                        filter_three[64 * k : 64 * k + 64, :], d3[:, 128 * plane : 128 * plane + 128]
-                    )
-                    part = got if part is None else part + got
-                move_by = -(32 * (1 - b) + 1 - c) % 128
-                if move_by:
-                    part = jnp.where(masks[3 * b + c], pltpu.roll(part, move_by, 1), 0.0)
-                total = part if total is None else total + part
-        scale = jnp.where(inside(2 * me - 1 + n, 2 * blocks), 1.0, 0.0)
-        grown.append((total * scale).astype(BF))
+    for pair_at in range(2):
+        rhs = jnp.concatenate(
+            [
+                d3[:, 128 * (2 * pair_at + 2 - a) : 128 * (2 * pair_at + 2 - a) + 256]
+                for a in range(3)
+            ],
+            axis=0,
+        )
+        got = dot(lhs, rhs)
+        for u in range(2):
+            total = None
+            for b in range(3):
+                for c in range(3):
+                    s = 3 * b + c
+                    part = got[64 * s : 64 * s + 64, 128 * u : 128 * u + 128]
+                    move_by = -(32 * (1 - b) + 1 - c) % 128
+                    if move_by:
+                        part = jnp.where(masks[s], pltpu.roll(part, move_by, 1), 0.0)
+                    total = part if total is None else total + part
+            n = 2 * pair_at + u
+            scale = jnp.where(inside(2 * me - 1 + n, 2 * blocks), 1.0, 0.0)
+            grown.append((total * scale).astype(BF))
     back = dot(jnp.concatenate(grown, axis=0), grow2[...])
     for h in range(8):
         rows = slice(64 * h, 64 * h + 64)
@@ -309,6 +343,7 @@
                         d2c[512 * k : 512 * k + 512, 128 * m : 128 * m + 128] = got[
                             :, 128 * kw : 128 * kw + 128
                         ]
+    copies[3].wait()
     back = dot(t2r[...], d2c[...]).astype(BF)
     back = dot(back, grow1[...])
     for h in range(16):
@@ -379,19 +414,35 @@
     return pltpu.VMEM(shape, BF)
 
 
-def local_grads(volume, grad, swaps, filter_one, filter_two, filter_three, rows):
-    tables = [jnp.asarray(t, BF) for t in one_hot_tables()]
-    args = [volume, grad, *swaps, filter_one, filter_two, filter_three, *tables]
+FAR = pl.BlockSpec(memory_space=pl.ANY)
+BANDED = ((512, 576), (320, 1440), (128, 1728), (256, 4608))
+
+
+def run_build(filter_one, filter_two, filter_three):
+    args = [filter_one, filter_two, filter_three, jnp.asarray(one_hot_tables()[0], BF)]
+    return pl.pallas_call(
+        build,
+        out_shape=[jax.ShapeDtypeStruct(shape, BF) for shape in BANDED],
+        in_specs=[VMEM] * len(args),
+        out_specs=[FAR] * 4,
+        scratch_shapes=[near(*shape) for shape in BANDED] + [pltpu.SemaphoreType.DMA((4,))],
+        compiler_params=pltpu.CompilerParams(vmem_limit_bytes=24 * 1024 * 1024),
+        cost_estimate=pl.CostEstimate(flops=10**9, bytes_accessed=6 * 10**6, transcendentals=0),
+        name="build",
+    )(*args)
+
+
+def local_grads(volume, grad, swaps, filter_three, banded, rows):
+    tables = [jnp.asarray(t, BF) for t in one_hot_tables()[1:]]
+    args = [volume, grad, *swaps, filter_three, *banded, *tables]
+    far = range(7, 11)
     return pl.pallas_call(
         body,
         out_shape=jax.ShapeDtypeStruct((rows, 128), BF),
-        in_specs=[VMEM] * len(args),
+        in_specs=[FAR if i in far else VMEM for i in range(len(args))],
         out_specs=VMEM,
-        scratch_shapes=[
-            near(512, 576),
-            near(512, 2304),
-            near(256, 4608),
-            near(128, 1728),
+        scratch_shapes=[near(*shape) for shape in BANDED]
+        + [
             near(192, 38 * 128),
             near(256, 18 * 128),
             near(2304, 1024),
@@ -402,8 +453,10 @@
             near(512, 512),
             near(512, 512),
             near(512, 1024),
+            pltpu.SemaphoreType.DMA((4,)),
         ],
-        compiler_params=pltpu.CompilerParams(vmem_limit_bytes=58 * 1024 * 1024),
+        compiler_params=pltpu.CompilerParams(vmem_limit_bytes=LIMIT * 1024 * 1024),
+        cost_estimate=pl.CostEstimate(flops=10**10, bytes_accessed=10**7, transcendentals=0),
         name="local_grads",
     )(*args)
 
@@ -439,18 +492,29 @@
     spaces, samples = (lax.axis_size("space"), lax.axis_size("sample"))
     own = volume.reshape(512, 128)
     grad = grad_out.reshape(32, 128)
-    both = jnp.concatenate([own, grad], axis=0)
-    swap_core = swap(both, 0)
-    swap_chip = swap(both, 1)
-    swap_chip2 = swap(swap_core, 1)
-    swap_core2 = swap(swap_chip, 0)
+    f1 = filter_one.reshape(108, 32)
+    f2 = filter_two.reshape(27, 32, 64)
+    f3 = filter_three.reshape(1728, 128)
+    core = lax.axis_index("space") % 2
+
+    def second(block, flip=0):
+        planes = lax.dynamic_slice(block, (64 * (core ^ flip), 0), (448, 128))
+        return jnp.concatenate([planes, grad], axis=0)
+
+    swap_core = swap(own, 0)
+    swap_chip = swap(own, 1)
+    relay = second(swap_core)
+    swap_chip2 = swap(relay, 1)
+    f2_later = lax.optimization_barrier((f2, relay))[0]
+    banded = run_build(f1, f2_later, f3)
+    swap_chip, *banded = lax.optimization_barrier((swap_chip, *banded))
+    swap_core2 = swap(second(swap_chip, 1), 0)
     flat = local_grads(
         own,
         grad,
         (swap_core, swap_chip, swap_chip2, swap_core2),
-        filter_one.reshape(108, 32),
-        filter_two.reshape(27, 32, 64),
-        filter_three.reshape(1728, 128),
+        f3,
+        banded,
         spaces * SLOT,
     )
     part = total_of(exchange(flat.reshape(spaces, SLOT, 128), "space"))

time: 96.3 us -> 92.4 us (0.960)
  blocking collectives: 59.1 us -> 55.2 us
  waiting for transfers between devices: 4.7 us -> 1.32 us
  local copies, waits for them, and re-layouts: 1.4 us -> 3.89 us
    all_to_all x3, blocking collectives: 59.1 us -> 55.2 us  [exchange(): return lax.all_to_all(pieces, axis, 0, 0, tiled=True)]
    ppermute x4, waiting for transfers between devices: 4.7 us -> 1.32 us  [swap(): return lax.ppermute(values, 'space', pairs + [(j, i) for i, j in pairs])]
    pallas_call x0 -> x1, Pallas kernels: none -> 2.33 us  [run_build(): pl.pallas_call(build, out_shape=[jax.ShapeDtypeStruct(shape, BF) for shap...]
    unnamed x10 -> x30, local copies, waits for them, and re-layouts: 0.66 us -> 2.92 us
    pallas_call x1, Pallas kernels: 18.3 us -> 16.2 us  [local_grads(): pl.pallas_call(body, out_shape=jax.ShapeDtypeStruct((rows, 128), BF), in_...]
  transfers between devices with their start and end apart: 4 -> 4, of which waited for: 2 -> 1; matrix products, arithmetic and copies ran while one was open for 1% -> 2% of each run, Pallas kernels for 0% -> 3%
where the time goes in v4:
time: 92.4 us; the launch traced here: 92 us
  blocking collectives  55.2 us (60%)
  Pallas kernels  20.8 us (23%)
  starting transfers between devices  8.97 us (10%)
  local copies, waits for them, and re-layouts  3.89 us (4%)
  waiting for transfers between devices  1.32 us (1%)
    all_to_all x3, blocking collectives, exchange(): return lax.all_to_all(pieces, axis, 0, 0, tiled=True)  55.2 us
    pallas_call x1, Pallas kernels, local_grads(): pl.pallas_call(body, out_shape=jax.ShapeDtypeStruct((rows, 128), BF), in_...  16.2 us
    ppermute x4, starting transfers between devices, swap(): return lax.ppermute(values, 'space', pairs + [(j, i) for i, j in pairs])  8.97 us
    unnamed x30, local copies, waits for them, and re-layouts  2.92 us
    pallas_call x1, Pallas kernels, run_build(): pl.pallas_call(build, out_shape=[jax.ShapeDtypeStruct(shape, BF) for shap...  2.33 us
    pallas_call x1, Pallas kernels, run_finish(): pl.pallas_call(finish, out_shape=[jax.ShapeDtypeStruct(shape, F32) for sh...  2.29 us
  transfers between devices with their start and end apart: 4, of which 1 were waited for; matrix products, arithmetic and copies ran while one was open for 2% of the time, Pallas kernels for 3%

profile of v4, /device:TPU:1, one launch (start us, length us, event | category | flops | bytes accessed | tf_op | source)
XLA Modules:
  0.0 92.0 jit_solution(17809390476109503343)
XLA Ops:
  0.6 0.0 copy-start
  0.6 3.3 %collective-permute-start = (bf16[512,128]{1,0:T(8,128)(2,1)}, bf16[512,128]{1,0:T(8,128)(2,1)S(1)}, u32[]{:S(2)}, u32[]{:S(2)}) collective-permute-start(bf16[512,128]{1,0:T(8,128)(2,1)} %bitcast.16), channel_id=1, source_target_pairs={{0,1},{2,3},{4,5},{6,7},{8,9},{10,11},{12,13},{14,15},{16,17},{18,... | collective-permute-start | bytes 393224 | tf_op jit(solution)/shard_map/ppermute | solution.py:488
  4.0 1.9 %collective-permute-start.1 = (bf16[512,128]{1,0:T(8,128)(2,1)}, bf16[512,128]{1,0:T(8,128)(2,1)S(1)}, u32[]{:S(2)}, u32[]{:S(2)}) collective-permute-start(bf16[512,128]{1,0:T(8,128)(2,1)} %bitcast.17), channel_id=1, source_target_pairs={{1,2},{3,4},{5,6},{7,8},{9,10},{11,12},{13,14},{15,16},{17,18},{19... | collective-permute-start | bytes 393224 | tf_op jit(solution)/shard_map/ppermute | solution.py:488
  5.9 0.0 copy-start.2
  5.9 0.0 copy-start.13
  5.9 0.8 reshape.40.filter_one
  6.8 0.0 collective-permute-done.swap_core
  6.8 0.7 pad_maximum_fusion.1
  7.5 3.6 %collective-permute-start.2 = (bf16[480,128]{1,0:T(8,128)(2,1)S(1)}, bf16[480,128]{1,0:T(8,128)(2,1)S(1)}, u32[]{:S(2)}, u32[]{:S(2)}) collective-permute-start(bf16[480,128]{1,0:T(8,128)(2,1)S(1)} %pad_maximum_fusion.1), channel_id=1, source_target_pairs={{1,2},{3,4},{5,6},{7,8},{9,10},{11,12},{13,14},{15,16},{17,18},{19... | collective-permute-start | bytes 368648 | tf_op jit(solution)/shard_map/ppermute | solution.py:488
  11.2 0.0 copy-start.1
  11.2 1.0 %copy-done.1 = bf16[3,3,3,64,128]{4,3,2,1,0:T(8,128)(2,1)S(1)} copy-done((bf16[3,3,3,64,128]{4,3,2,1,0:T(8,128)(2,1)S(1)}, bf16[3,3,3,64,128]{4,3,2,1,0:T(8,128)(2,1)}, u32[]{:S(2)}) %copy-start.1) | copy-done | bytes 442392
  12.2 0.0 copy-start.3
  12.2 0.9 %copy-done.3 = bf16[3,3,3,32,64]{4,3,2,1,0:T(8,128)(2,1)S(1)} copy-done((bf16[3,3,3,32,64]{4,3,2,1,0:T(8,128)(2,1)S(1)}, bf16[3,3,3,32,64]{4,3,2,1,0:T(8,128)(2,1)}, u32[]{:S(2)}) %copy-start.3) | copy-done | bytes 110616
  13.1 0.0 copy-start.10
  13.1 0.9 copy-done.10
  14.0 0.0 copy-start.4
  14.0 0.0 copy-start.5
  14.0 0.0 copy-start.6
  14.0 0.0 copy-start.7
  14.0 0.0 copy-start.8
  14.0 0.0 copy-start.9
  14.1 0.0 copy-start.11
  14.1 0.0 copy-start.12
  14.1 0.0 copy-start.14
  14.1 2.3 %build.1 = (bf16[512,576]{1,0:T(8,128)(2,1)S(1)}, bf16[320,1440]{1,0:T(8,128)(2,1)S(1)}, bf16[128,1728]{1,0:T(8,128)(2,1)S(1)}, bf16[256,4608]{1,0:T(8,128)(2,1)S(1)}) custom-call(bf16[108,32]{1,0:T(8,128)(2,1)S(1)} %reshape.40.filter_one, bf16[27,32,64]{2,1,0:T(8,128)(2,1)S(1)} %bitcast.15, bf16[1728,128]{1,0:T(8,128)(2,1)S(1)} %bitcast.13, ...), custom_call_target="tpu_custom_call" | custom-call | flops 1000000000 | bytes 6000000 | tf_op jit(solution)/shard_map/build/pallas_call | solution.py:423
  16.4 0.0 collective-permute-done.1.swap_chip
  16.5 0.0 copy-done
  16.5 0.1 collective-permute-start.3
  16.6 0.0 collective-permute-done.2.swap_chip2
  16.6 1.3 %collective-permute-done.3.swap_core2 = bf16[480,128]{1,0:T(8,128)(2,1)S(1)} collective-permute-done((bf16[480,128]{1,0:T(8,128)(2,1)S(1)}, bf16[480,128]{1,0:T(8,128)(2,1)S(1)}, u32[]{:S(2)}, u32[]{:S(2)}) %collective-permute-start.3) | collective-permute-done | bytes 122912 | tf_op jit(solution)/shard_map/ppermute | solution.py:488
  17.9 0.0 copy-done.2
  17.9 0.0 copy-done.13
  17.9 0.0 copy-done.4
  17.9 0.0 copy-done.5
  17.9 0.0 copy-done.6
  17.9 0.0 copy-done.7
  18.0 0.0 copy-done.8
  18.0 0.0 copy-done.9
  18.0 0.0 copy-done.11
  18.0 0.0 copy-done.12
  18.0 0.0 copy-done.14
  18.0 16.2 %local_grads.1 = bf16[2560,128]{1,0:T(8,128)(2,1)S(1)} custom-call(bf16[512,128]{1,0:T(8,128)(2,1)S(1)} %bitcast.18, bf16[32,128]{1,0:T(8,128)(2,1)S(1)} %bitcast.12, bf16[512,128]{1,0:T(8,128)(2,1)S(1)} %collective-permute-done.swap_core, bf16[512,128]{1,0:T(8,128)(2,1)S(1)} %collective-permute-done.1.swap_chip, ...), custom_call_target="tpu_custom_call" | custom-call | flops 10000000000 | bytes 10000000 | tf_op jit(solution)/shard_map/local_grads/pallas_call | solution.py:439
  34.2 20.0 %all_to_all.15 = bf16[32,80,128]{2,1,0:T(8,128)(2,1)S(1)} all-to-all(bf16[32,80,128]{2,1,0:T(8,128)(2,1)S(1)} %bitcast.9), channel_id=1, replica_groups=mesh['sample'=8,'space'=32] {'space'}, dimensions={0} | all-to-all | bytes 1310720 | tf_op jit(solution)/shard_map/all_to_all | solution.py:478
  54.3 0.1 reduce_sum.24
  54.4 16.3 %all_to_all.16 = bf16[8,80,128]{2,1,0:T(8,128)(2,1)S(1)} all-to-all(bf16[8,80,128]{2,1,0:T(8,128)(2,1)S(1)} %broadcast_in_dim.4), channel_id=1, replica_groups=mesh['sample'=8,'space'=32] {'sample'}, dimensions={0} | all-to-all | bytes 327680 | tf_op jit(solution)/shard_map/all_to_all | solution.py:478
  70.8 0.1 broadcast_in_dim.5
  70.9 18.8 %all_to_all.17 = bf16[32,80,128]{2,1,0:T(8,128)(2,1)} all-to-all(bf16[32,80,128]{2,1,0:T(8,128)(2,1)S(1)} %broadcast_in_dim.5), channel_id=1, replica_groups=mesh['sample'=8,'space'=32] {'space'}, dimensions={0} | all-to-all | bytes 1310720 | tf_op jit(solution)/shard_map/all_to_all | solution.py:478
  89.7 2.3 %finish.1 = (f32[27,4,32]{2,1,0:T(4,128)}, f32[27,32,64]{2,1,0:T(8,128)}, f32[27,64,128]{2,1,0:T(8,128)}) custom-call(f32[3]{0:T(128)} %constant.63.scales, bf16[2560,128]{1,0:T(8,128)(2,1)} %bitcast.19), custom_call_target="tpu_custom_call" | custom-call | tf_op jit(solution)/shard_map/finish/pallas_call | solution.py:467
  (5 shorter events, 0.1 us)
Async XLA Ops:
  0.6 15.8 %copy-start = (bf16[1,1,2,16,128]{4,3,2,1,0:T(8,128)(2,1)S(1)}, bf16[1,1,2,16,128]{4,3,2,1,0:T(8,128)(2,1)}, u32[]{:S(2)}) copy-start(bf16[1,1,2,16,128]{4,3,2,1,0:T(8,128)(2,1)} %param.17) | copy-start | bytes 24580
  0.6 6.1 %collective-permute-start = (bf16[512,128]{1,0:T(8,128)(2,1)}, bf16[512,128]{1,0:T(8,128)(2,1)S(1)}, u32[]{:S(2)}, u32[]{:S(2)}) collective-permute-start(bf16[512,128]{1,0:T(8,128)(2,1)} %bitcast.16), channel_id=1, source_target_pairs={{0,1},{2,3},{4,5},{6,7},{8,9},{10,11},{12,13},{14,15},{16,17},{18,... | collective-permute-start | bytes 393224 | tf_op jit(solution)/shard_map/ppermute | solution.py:488
  4.0 12.5 %collective-permute-start.1 = (bf16[512,128]{1,0:T(8,128)(2,1)}, bf16[512,128]{1,0:T(8,128)(2,1)S(1)}, u32[]{:S(2)}, u32[]{:S(2)}) collective-permute-start(bf16[512,128]{1,0:T(8,128)(2,1)} %bitcast.17), channel_id=1, source_target_pairs={{1,2},{3,4},{5,6},{7,8},{9,10},{11,12},{13,14},{15,16},{17,18},{19... | collective-permute-start | bytes 393224 | tf_op jit(solution)/shard_map/ppermute | solution.py:488
  5.9 12.0 %copy-start.2 = (bf16[3,3,3,64,128]{4,3,2,1,0:T(8,128)(2,1)S(1)}, bf16[3,3,3,64,128]{4,3,2,1,0:T(8,128)(2,1)}, u32[]{:S(2)}) copy-start(bf16[3,3,3,64,128]{4,3,2,1,0:T(8,128)(2,1)} %param.20) | copy-start | bytes 1327108
  5.9 12.0 %copy-start.13 = (bf16[128,384]{1,0:T(8,128)(2,1)S(1)}, bf16[128,384]{1,0:T(8,128)(2,1)}, u32[]{:S(2)}) copy-start(bf16[128,384]{1,0:T(8,128)(2,1)} %constant.54.clone.even) | copy-start | bytes 294916
  7.5 9.1 %collective-permute-start.2 = (bf16[480,128]{1,0:T(8,128)(2,1)S(1)}, bf16[480,128]{1,0:T(8,128)(2,1)S(1)}, u32[]{:S(2)}, u32[]{:S(2)}) collective-permute-start(bf16[480,128]{1,0:T(8,128)(2,1)S(1)} %pad_maximum_fusion.1), channel_id=1, source_target_pairs={{1,2},{3,4},{5,6},{7,8},{9,10},{11,12},{13,14},{15,16},{17,18},{19... | collective-permute-start | bytes 368648 | tf_op jit(solution)/shard_map/ppermute | solution.py:488
  11.2 1.0 %copy-start.1 = (bf16[3,3,3,64,128]{4,3,2,1,0:T(8,128)(2,1)S(1)}, bf16[3,3,3,64,128]{4,3,2,1,0:T(8,128)(2,1)}, u32[]{:S(2)}) copy-start(bf16[3,3,3,64,128]{4,3,2,1,0:T(8,128)(2,1)} %param.20) | copy-start | bytes 1327108
  12.2 0.9 %copy-start.3 = (bf16[3,3,3,32,64]{4,3,2,1,0:T(8,128)(2,1)S(1)}, bf16[3,3,3,32,64]{4,3,2,1,0:T(8,128)(2,1)}, u32[]{:S(2)}) copy-start(bf16[3,3,3,32,64]{4,3,2,1,0:T(8,128)(2,1)} %param.19) | copy-start | bytes 331780
  13.1 0.9 copy-start.10
  14.0 3.9 %copy-start.4 = (bf16[1,8,4,16,128]{4,3,2,1,0:T(8,128)(2,1)S(1)}, bf16[1,8,4,16,128]{4,3,2,1,0:T(8,128)(2,1)}, u32[]{:S(2)}) copy-start(bf16[1,8,4,16,128]{4,3,2,1,0:T(8,128)(2,1)} %param.16) | copy-start | bytes 393220
  14.0 3.9 %copy-start.5 = (bf16[128,1152]{1,0:T(8,128)(2,1)S(1)}, bf16[128,1152]{1,0:T(8,128)(2,1)}, u32[]{:S(2)}) copy-start(bf16[128,1152]{1,0:T(8,128)(2,1)} %constant.56.clone.spread) | copy-start | bytes 884740
  14.0 3.9 %copy-start.6 = (bf16[256,512]{1,0:T(8,128)(2,1)S(1)}, bf16[256,512]{1,0:T(8,128)(2,1)}, u32[]{:S(2)}) copy-start(bf16[256,512]{1,0:T(8,128)(2,1)} %constant.59.clone.grow1) | copy-start | bytes 786436
  14.0 3.9 %copy-start.7 = (bf16[256,384]{1,0:T(8,128)(2,1)S(1)}, bf16[256,384]{1,0:T(8,128)(2,1)}, u32[]{:S(2)}) copy-start(bf16[256,384]{1,0:T(8,128)(2,1)} %constant.53.clone.odd) | copy-start | bytes 589828
  14.0 3.9 %copy-start.8 = (bf16[256,384]{1,0:T(8,128)(2,1)S(1)}, bf16[256,384]{1,0:T(8,128)(2,1)}, u32[]{:S(2)}) copy-start(bf16[256,384]{1,0:T(8,128)(2,1)} %constant.52.clone.pair) | copy-start | bytes 589828
  14.0 3.9 %copy-start.9 = (bf16[96,768]{1,0:T(8,128)(2,1)S(1)}, bf16[96,768]{1,0:T(8,128)(2,1)}, u32[]{:S(2)}) copy-start(bf16[96,768]{1,0:T(8,128)(2,1)} %constant.57.clone.grow_g) | copy-start | bytes 442372
  14.1 3.9 %copy-start.11 = (bf16[128,512]{1,0:T(8,128)(2,1)S(1)}, bf16[128,512]{1,0:T(8,128)(2,1)}, u32[]{:S(2)}) copy-start(bf16[128,512]{1,0:T(8,128)(2,1)} %constant.58.clone.grow2) | copy-start | bytes 393220
  14.1 3.9 %copy-start.12 = (bf16[512,128]{1,0:T(8,128)(2,1)S(1)}, bf16[512,128]{1,0:T(8,128)(2,1)}, u32[]{:S(2)}) copy-start(bf16[512,128]{1,0:T(8,128)(2,1)} %constant.55.clone.squeeze) | copy-start | bytes 393220
  14.1 3.9 %copy-start.14 = (bf16[128,256]{1,0:T(8,128)(2,1)S(1)}, bf16[128,256]{1,0:T(8,128)(2,1)}, u32[]{:S(2)}) copy-start(bf16[128,256]{1,0:T(8,128)(2,1)} %constant.51.clone.shift) | copy-start | bytes 196612
  16.5 1.4 %collective-permute-start.3 = (bf16[480,128]{1,0:T(8,128)(2,1)S(1)}, bf16[480,128]{1,0:T(8,128)(2,1)S(1)}, u32[]{:S(2)}, u32[]{:S(2)}) collective-permute-start(bf16[480,128]{1,0:T(8,128)(2,1)S(1)} %pad_maximum_fusion), channel_id=1, source_target_pairs={{0,1},{2,3},{4,5},{6,7},{8,9},{10,11},{12,13},{14,15},{16,17},{18,... | collective-permute-start | bytes 368648 | tf_op jit(solution)/shard_map/ppermute | solution.py:488

commit v5 on v4

--- a/solution.py
+++ b/solution.py
@@ -92,11 +92,9 @@
     return [kd * 9 + (2 - kh) * 3 + kw for kh in range(3)]
 
 
-def build(filter_one, filter_two, filter_three, perm, t1, t2, w3t, t2r, s1, s2, s3, s2r, sems):
-    copies = [
-        pltpu.make_async_copy(near_ref, far_ref, sems.at[i])
-        for i, (near_ref, far_ref) in enumerate(((s1, t1), (s2, t2), (s3, w3t), (s2r, t2r)))
-    ]
+def build(filter_two, t2, t2r, s2, s2r, sems):
+    copy2r = pltpu.make_async_copy(s2r, t2r, sems.at[0])
+    copy2 = pltpu.make_async_copy(s2, t2, sems.at[1])
     for it in range(9):
         v2 = [filter_two[k].astype(F32) for k in taps_back(it)]
         zero = jnp.zeros((32, 64), F32)
@@ -110,7 +108,7 @@
                 hp = 2 * m + 1 - s
                 if 0 <= hp < 8:
                     s2r[32 * hp : 32 * hp + 32, it * 512 + 128 * m : it * 512 + 128 * m + 128] = tile
-    copies[3].start()
+    copy2r.start()
     taps = []
     for kh in range(3):
         rows = jnp.concatenate([filter_two[taps_of(it)[kh]] for it in range(9)], axis=0)
@@ -119,21 +117,9 @@
     for s in range(5):
         parts = [taps[p - s + 1] if 0 <= p - s + 1 < 3 else zero for p in range(5)]
         s2[64 * s : 64 * s + 64, :] = jnp.concatenate(parts, axis=1).astype(BF)
-    copies[1].start()
-    s3[...] = (filter_three[...].astype(F32).T * 0.5).astype(BF)
-    copies[2].start()
-    lane = lax.broadcasted_iota(jnp.int32, (32, 640), 1) % 16
-    base = lax.dot_general(filter_one[...], perm[...], TN, preferred_element_type=F32)
-    for h in range(16):
-        moved = pltpu.roll(base, (h - 1) % 640, 1) if h != 1 else base
-        if h == 0:
-            moved = jnp.where(lane == 15, 0.0, moved)
-        if h == 15:
-            moved = jnp.where(lane == 0, 0.0, moved)
-        s1[32 * h : 32 * h + 32, :] = moved[:, :576].astype(BF)
-    copies[0].start()
-    for copy in copies:
-        copy.wait()
+    copy2.start()
+    copy2r.wait()
+    copy2.wait()
 
 
 def body(
@@ -143,11 +129,11 @@
     swap_chip,
     swap_chip2,
     swap_core2,
+    filter_one,
     filter_three,
-    t1_far,
     t2_far,
-    w3t_far,
     t2r_far,
+    perm,
     shift,
     pair,
     odd,
@@ -157,7 +143,8 @@
     grow_g,
     grow2,
     grow1,
-    out,
+    kept,
+    sent,
     t1,
     t2,
     w3t,
@@ -172,16 +159,29 @@
     sl2,
     d2,
     d1,
+    out,
     sems,
 ):
     me, blocks = position()
     first_core = me % 2 == 0
-    copies = []
-    for i, (far_ref, near_ref) in enumerate(
-        ((t1_far, t1), (t2_far, t2), (w3t_far, w3t), (t2r_far, t2r))
-    ):
-        copies.append(pltpu.make_async_copy(far_ref, near_ref, sems.at[i]))
-        copies[-1].start()
+    copies = [
+        pltpu.make_async_copy(far_ref, near_ref, sems.at[i])
+        for i, (far_ref, near_ref) in enumerate(((t2_far, t2), (t2r_far, t2r)))
+    ]
+    for copy in copies:
+        copy.start()
+
+    lane = lax.broadcasted_iota(jnp.int32, (32, 640), 1) % 16
+    rows = filter_one[...].astype(F32).reshape(108, 32).astype(BF)
+    base = lax.dot_general(rows, perm[...], TN, preferred_element_type=F32)
+    for h in range(16):
+        moved = pltpu.roll(base, (h - 1) % 640, 1) if h != 1 else base
+        if h == 0:
+            moved = jnp.where(lane == 15, 0.0, moved)
+        if h == 15:
+            moved = jnp.where(lane == 0, 0.0, moved)
+        t1[32 * h : 32 * h + 32, :] = moved[:, :576].astype(BF)
+    w3t[...] = (filter_three[...].astype(F32).T * 0.5).astype(BF)
 
     def either(a, b, lo, hi):
         return jnp.where(first_core, a[lo:hi, :], b[lo:hi, :])
@@ -203,7 +203,6 @@
             x1[128:192, lanes] = moved[64 * p : 64 * p + 64, 128:]
         at += count
 
-    copies[0].wait()
     for j in range(18):
         rhs = jnp.concatenate(
             [x1[:, (2 * j + kd) * 128 : (2 * j + kd) * 128 + 256] for kd in range(3)], axis=0
@@ -232,7 +231,7 @@
                         :, 128 * kw : 128 * kw + 128
                     ]
 
-    copies[1].wait()
+    copies[0].wait()
     for c in range(4):
         lanes = slice(c * 256, c * 256 + 256)
         for g in range(2):
@@ -280,7 +279,6 @@
         axis=0,
     )
     grown = dot(rows.astype(F32).T.astype(BF), grow_g[...])
-    copies[2].wait()
     half = dot(w3t[...], x3[...])
     t = jnp.tanh(half)
     d3 = (grown * ((1.0 + t) + half * (1.0 - t * t))).astype(BF)
@@ -343,7 +341,7 @@
                         d2c[512 * k : 512 * k + 512, 128 * m : 128 * m + 128] = got[
                             :, 128 * kw : 128 * kw + 128
                         ]
-    copies[3].wait()
+    copies[1].wait()
     back = dot(t2r[...], d2c[...]).astype(BF)
     back = dot(back, grow1[...])
     for h in range(16):
@@ -393,15 +391,32 @@
         [packed, jnp.zeros((12, 128), F32)], axis=0
     ).astype(BF)
     out[G_ONE + 48 :, :] = jnp.zeros((out.shape[0] - G_ONE - 48, 128), BF)
-
-
-def finish(scales, flat, one, two, three):
+    half_rows = kept.shape[0]
+    mine = pl.multiple_of(me % 2 * half_rows, half_rows)
+    kept[...] = out[pl.ds(mine, half_rows), :]
+    sent[...] = out[pl.ds(half_rows - mine, half_rows), :]
+
+
+def finish(scales, mine, other, one, two, three):
+    first_core = position()[0] % 2 == 0
+
+    def rows(at, count):
+        half_rows = mine.shape[0]
+        parts = []
+        while count:
+            use = min(count, half_rows - at % half_rows)
+            here = slice(at % half_rows, at % half_rows + use)
+            flag = first_core if at < half_rows else jnp.logical_not(first_core)
+            parts.append(jnp.where(flag, mine[here, :], other[here, :]).astype(F32))
+            at, count = (at + use, count - use)
+        return parts[0] if len(parts) == 1 else jnp.concatenate(parts, axis=0)
+
     for k in range(27):
-        three[k] = flat[64 * k : 64 * k + 64, :].astype(F32) * scales[2]
-        got = flat[G_TWO + 16 * k : G_TWO + 16 * k + 16, :].astype(F32) * scales[1]
+        three[k] = rows(64 * k, 64) * scales[2]
+        got = rows(G_TWO + 16 * k, 16) * scales[1]
         two[k, 0:16, :] = got[:, :64]
         two[k, 16:32, :] = got[:, 64:]
-    got = flat[G_ONE : G_ONE + 48, :].astype(F32) * scales[0]
+    got = rows(G_ONE, 48) * scales[0]
     for it in range(9):
         for kh, k in enumerate(taps_of(it)):
             one[k] = got[4 * it : 4 * it + 4, 32 * kh : 32 * kh + 32]
@@ -415,34 +430,36 @@
 
 
 FAR = pl.BlockSpec(memory_space=pl.ANY)
-BANDED = ((512, 576), (320, 1440), (128, 1728), (256, 4608))
-
-
-def run_build(filter_one, filter_two, filter_three):
-    args = [filter_one, filter_two, filter_three, jnp.asarray(one_hot_tables()[0], BF)]
+BANDED = ((320, 1440), (256, 4608))
+
+
+def run_build(filter_two):
     return pl.pallas_call(
         build,
         out_shape=[jax.ShapeDtypeStruct(shape, BF) for shape in BANDED],
-        in_specs=[VMEM] * len(args),
-        out_specs=[FAR] * 4,
-        scratch_shapes=[near(*shape) for shape in BANDED] + [pltpu.SemaphoreType.DMA((4,))],
-        compiler_params=pltpu.CompilerParams(vmem_limit_bytes=24 * 1024 * 1024),
+        in_specs=[VMEM],
+        out_specs=[FAR] * 2,
+        scratch_shapes=[near(*shape) for shape in BANDED] + [pltpu.SemaphoreType.DMA((2,))],
+        compiler_params=pltpu.CompilerParams(vmem_limit_bytes=16 * 1024 * 1024),
         cost_estimate=pl.CostEstimate(flops=10**9, bytes_accessed=6 * 10**6, transcendentals=0),
         name="build",
-    )(*args)
-
-
-def local_grads(volume, grad, swaps, filter_three, banded, rows):
-    tables = [jnp.asarray(t, BF) for t in one_hot_tables()[1:]]
-    args = [volume, grad, *swaps, filter_three, *banded, *tables]
-    far = range(7, 11)
+    )(filter_two)
+
+
+def local_grads(volume, grad, swaps, filter_one, filter_three, banded, rows):
+    tables = [jnp.asarray(t, BF) for t in one_hot_tables()]
+    args = [volume, grad, *swaps, filter_one, filter_three, *banded, *tables]
+    far = (8, 9)
     return pl.pallas_call(
         body,
-        out_shape=jax.ShapeDtypeStruct((rows, 128), BF),
+        out_shape=[jax.ShapeDtypeStruct((rows // 2, 128), BF)] * 2,
         in_specs=[FAR if i in far else VMEM for i in range(len(args))],
-        out_specs=VMEM,
-        scratch_shapes=[near(*shape) for shape in BANDED]
-        + [
+        out_specs=[VMEM] * 2,
+        scratch_shapes=[
+            near(512, 576),
+            near(320, 1440),
+            near(128, 1728),
+            near(256, 4608),
             near(192, 38 * 128),
             near(256, 18 * 128),
             near(2304, 1024),
@@ -453,7 +470,8 @@
             near(512, 512),
             near(512, 512),
             near(512, 1024),
-            pltpu.SemaphoreType.DMA((4,)),
+            near(rows, 128),
+            pltpu.SemaphoreType.DMA((2,)),
         ],
         compiler_params=pltpu.CompilerParams(vmem_limit_bytes=LIMIT * 1024 * 1024),
         cost_estimate=pl.CostEstimate(flops=10**10, bytes_accessed=10**7, transcendentals=0),
@@ -461,21 +479,27 @@
     )(*args)
 
 
-def run_finish(flat, cells):
+def run_finish(mine, other, cells):
     scales = 1.0 / jnp.sqrt(jnp.array([cells, cells / 8.0, cells / 64.0], F32))
     shapes = [(27, 4, 32), (27, 32, 64), (27, 64, 128)]
     outs = pl.pallas_call(
         finish,
         out_shape=[jax.ShapeDtypeStruct(shape, F32) for shape in shapes],
-        in_specs=[pl.BlockSpec(memory_space=pltpu.SMEM), VMEM],
+        in_specs=[pl.BlockSpec(memory_space=pltpu.SMEM), VMEM, VMEM],
         out_specs=[VMEM] * 3,
         name="finish",
-    )(scales, flat)
+    )(scales, mine, other)
     return tuple(o.reshape(3, 3, 3, *o.shape[1:]) for o in outs)
 
 
-def exchange(pieces, axis):
-    return lax.all_to_all(pieces, axis, 0, 0, tiled=True)
+def over_sample(pieces):
+    return lax.all_to_all(pieces, "sample", 0, 0, tiled=True)
+
+
+def over_chips(pieces):
+    size = lax.axis_size("space")
+    groups = [list(range(core, size, 2)) for core in range(2)]
+    return lax.all_to_all(pieces, "space", 0, 0, axis_index_groups=groups, tiled=True)
 
 
 def total_of(got):
@@ -492,7 +516,7 @@
     spaces, samples = (lax.axis_size("space"), lax.axis_size("sample"))
     own = volume.reshape(512, 128)
     grad = grad_out.reshape(32, 128)
-    f1 = filter_one.reshape(108, 32)
+    f1 = filter_one.reshape(27, 4, 32)
     f2 = filter_two.reshape(27, 32, 64)
     f3 = filter_three.reshape(1728, 128)
     core = lax.axis_index("space") % 2
@@ -506,22 +530,25 @@
     relay = second(swap_core)
     swap_chip2 = swap(relay, 1)
     f2_later = lax.optimization_barrier((f2, relay))[0]
-    banded = run_build(f1, f2_later, f3)
+    banded = run_build(f2_later)
     swap_chip, *banded = lax.optimization_barrier((swap_chip, *banded))
     swap_core2 = swap(second(swap_chip, 1), 0)
-    flat = local_grads(
+    chips = spaces // 2
+    keep, send = local_grads(
         own,
         grad,
         (swap_core, swap_chip, swap_chip2, swap_core2),
+        f1,
         f3,
         banded,
         spaces * SLOT,
     )
-    part = total_of(exchange(flat.reshape(spaces, SLOT, 128), "space"))
-    part = total_of(exchange(jnp.broadcast_to(part[None], (samples, SLOT, 128)), "sample"))
-    flat = exchange(jnp.broadcast_to(part[None], (spaces, SLOT, 128)), "space")
+    half = (keep.astype(F32) + swap(send, 0).astype(F32)).astype(BF)
+    part = total_of(over_chips(half.reshape(chips, SLOT, 128)))
+    part = total_of(over_sample(jnp.broadcast_to(part[None], (samples, SLOT, 128))))
+    mine = over_chips(jnp.broadcast_to(part[None], (chips, SLOT, 128))).reshape(-1, 128)
     cells = float(samples * spaces * volume.shape[1] * volume.shape[3] * volume.shape[4])
-    return run_finish(flat.reshape(-1, 128), cells)
+    return run_finish(mine, swap(mine, 0), cells)
 
 
 def solution(mesh):

time: 92.4 us -> 82.8 us (0.90)
  blocking collectives: 55.2 us -> 42.7 us
  starting transfers between devices: 8.97 us -> 13.1 us
  waiting for transfers between devices: 1.32 us -> 4.07 us
  local copies, waits for them, and re-layouts: 3.89 us -> 1.84 us
  Pallas kernels: 20.8 us -> 18.9 us
    all_to_all x3, blocking collectives: 55.2 us -> 42.7 us  [the longest x2 26.3 us: over_chips(): lax.all_to_all(pieces, 'space', 0, 0, axis_index_groups=groups, tiled=True)]
    ppermute x4 -> x6, starting transfers between devices: 8.97 us -> 13.1 us  [swap(): return lax.ppermute(values, 'space', pairs + [(j, i) for i, j in pairs])]
    ppermute x4 -> x6, waiting for transfers between devices: 1.32 us -> 4.07 us  [swap(): return lax.ppermute(values, 'space', pairs + [(j, i) for i, j in pairs])]
    unnamed x30 -> x34, local copies, waits for them, and re-layouts: 2.92 us -> 1.74 us
    pallas_call x1, Pallas kernels: 2.33 us -> 1.17 us  [run_build(): pl.pallas_call(build, out_shape=[jax.ShapeDtypeStruct(shape, BF) for shap...]
  transfers between devices with their start and end apart: 4 -> 6, of which waited for: 1 -> 4; matrix products, arithmetic and copies ran while one was open for 2% -> 1% of each run, Pallas kernels for 3% -> 1%
where the time goes in v5:
time: 82.8 us; the launch traced here: 82.4 us
  blocking collectives  42.7 us (52%)
  Pallas kernels  18.9 us (23%)
  starting transfers between devices  13.1 us (16%)
  waiting for transfers between devices  4.07 us (5%)
  local copies, waits for them, and re-layouts  1.84 us (2%)
  between operations  0.94 us (1%)
  other arithmetic  0.89 us (1%)
    all_to_all x2, blocking collectives, over_chips(): lax.all_to_all(pieces, 'space', 0, 0, axis_index_groups=groups, tiled=True)  26.3 us
    all_to_all x1, blocking collectives, over_sample(): return lax.all_to_all(pieces, 'sample', 0, 0, tiled=True)  16.4 us
    pallas_call x1, Pallas kernels, local_grads(): pl.pallas_call(body, out_shape=[jax.ShapeDtypeStruct((rows // 2, 128), BF...  15.4 us
    ppermute x6, starting transfers between devices, swap(): return lax.ppermute(values, 'space', pairs + [(j, i) for i, j in pairs])  13.1 us
    ppermute x6, waiting for transfers between devices, swap(): return lax.ppermute(values, 'space', pairs + [(j, i) for i, j in pairs])  4.07 us
    pallas_call x1, Pallas kernels, run_finish(): pl.pallas_call(finish, out_shape=[jax.ShapeDtypeStruct(shape, F32) for sh...  2.29 us
    unnamed x34, local copies, waits for them, and re-layouts  1.74 us
  transfers between devices with their start and end apart: 6, of which 4 were waited for; matrix products, arithmetic and copies ran while one was open for 1% of the time, Pallas kernels for 1%

profile of v5, /device:TPU:1, one launch (start us, length us, event | category | flops | bytes accessed | tf_op | source)
XLA Modules:
  0.0 82.4 jit_solution(16394244317103409791)
XLA Ops:
  0.6 0.0 copy-start
  0.6 0.0 copy-start.1
  0.7 0.0 copy-start.4
  0.7 3.3 %collective-permute-start = (bf16[512,128]{1,0:T(8,128)(2,1)}, bf16[512,128]{1,0:T(8,128)(2,1)S(1)}, u32[]{:S(2)}, u32[]{:S(2)}) collective-permute-start(bf16[512,128]{1,0:T(8,128)(2,1)} %bitcast.15), channel_id=1, source_target_pairs={{0,1},{2,3},{4,5},{6,7},{8,9},{10,11},{12,13},{14,15},{16,17},{18,... | collective-permute-start | bytes 393224 | tf_op jit(solution)/shard_map/ppermute | solution.py:512
  4.0 1.9 %collective-permute-start.1 = (bf16[512,128]{1,0:T(8,128)(2,1)}, bf16[512,128]{1,0:T(8,128)(2,1)S(1)}, u32[]{:S(2)}, u32[]{:S(2)}) collective-permute-start(bf16[512,128]{1,0:T(8,128)(2,1)} %bitcast.16), channel_id=1, source_target_pairs={{1,2},{3,4},{5,6},{7,8},{9,10},{11,12},{13,14},{15,16},{17,18},{19... | collective-permute-start | bytes 393224 | tf_op jit(solution)/shard_map/ppermute | solution.py:512
  5.9 0.0 collective-permute-done.swap_core
  6.0 0.7 pad_maximum_fusion.1
  6.7 3.6 %collective-permute-start.2 = (bf16[480,128]{1,0:T(8,128)(2,1)S(1)}, bf16[480,128]{1,0:T(8,128)(2,1)S(1)}, u32[]{:S(2)}, u32[]{:S(2)}) collective-permute-start(bf16[480,128]{1,0:T(8,128)(2,1)S(1)} %pad_maximum_fusion.1), channel_id=1, source_target_pairs={{1,2},{3,4},{5,6},{7,8},{9,10},{11,12},{13,14},{15,16},{17,18},{19... | collective-permute-start | bytes 368648 | tf_op jit(solution)/shard_map/ppermute | solution.py:512
  10.3 0.0 copy-start.2
  10.3 0.9 %copy-done.2 = bf16[3,3,3,32,64]{4,3,2,1,0:T(8,128)(2,1)S(1)} copy-done((bf16[3,3,3,32,64]{4,3,2,1,0:T(8,128)(2,1)S(1)}, bf16[3,3,3,32,64]{4,3,2,1,0:T(8,128)(2,1)}, u32[]{:S(2)}) %copy-start.2) | copy-done | bytes 110616
  11.3 0.0 copy-start.8
  11.3 0.0 copy-start.9
  11.3 0.0 copy-start.10
  11.3 0.0 copy-start.11
  11.3 0.0 copy-start.12
  11.3 0.0 copy-start.13
  11.3 0.0 copy-start.14
  11.4 1.2 %build.1 = (bf16[320,1440]{1,0:T(8,128)(2,1)S(1)}, bf16[256,4608]{1,0:T(8,128)(2,1)S(1)}) custom-call(bf16[27,32,64]{2,1,0:T(8,128)(2,1)S(1)} %bitcast.14), custom_call_target="tpu_custom_call" | custom-call | flops 1000000000 | bytes 6000000 | tf_op jit(solution)/shard_map/build/pallas_call | solution.py:437
  12.5 0.0 collective-permute-done.1.swap_chip
  12.6 0.0 copy-done
  12.6 0.1 collective-permute-start.3
  12.7 0.2 collective-permute-done.2.swap_chip2
  12.9 1.2 %collective-permute-done.3.swap_core2 = bf16[480,128]{1,0:T(8,128)(2,1)S(1)} collective-permute-done((bf16[480,128]{1,0:T(8,128)(2,1)S(1)}, bf16[480,128]{1,0:T(8,128)(2,1)S(1)}, u32[]{:S(2)}, u32[]{:S(2)}) %collective-permute-start.3) | collective-permute-done | bytes 122912 | tf_op jit(solution)/shard_map/ppermute | solution.py:512
  14.0 0.0 copy-done.1
  14.0 0.0 copy-done.4
  14.0 0.0 copy-done.5
  14.0 0.0 copy-done.6
  14.1 0.0 copy-done.7
  14.1 0.0 copy-done.8
  14.1 0.0 copy-done.9
  14.1 0.0 copy-done.10
  14.1 0.0 copy-done.11
  14.1 0.0 copy-done.12
  14.1 0.0 copy-done.13
  14.1 0.0 copy-done.14
  14.1 15.4 %local_grads.1 = (bf16[1280,128]{1,0:T(8,128)(2,1)S(1)}, bf16[1280,128]{1,0:T(8,128)(2,1)S(1)}) custom-call(bf16[512,128]{1,0:T(8,128)(2,1)S(1)} %bitcast.17, bf16[32,128]{1,0:T(8,128)(2,1)S(1)} %bitcast.12, bf16[512,128]{1,0:T(8,128)(2,1)S(1)} %collective-permute-done.swap_core, bf16[512,128]{1,0:T(8,128)(2,1)S(1)} %collective-permute-done.1.swap_chip, ...), custom_call_target="tpu_custom_call" | custom-call | flops 10000000000 | bytes 10000000 | tf_op jit(solution)/shard_map/local_grads/pallas_call | solution.py:453
  29.6 0.2 collective-permute-start.4
  29.8 1.5 %collective-permute-done.4 = bf16[1280,128]{1,0:T(8,128)(2,1)S(1)} collective-permute-done((bf16[1280,128]{1,0:T(8,128)(2,1)S(1)}, bf16[1280,128]{1,0:T(8,128)(2,1)S(1)}, u32[]{:S(2)}, u32[]{:S(2)}) %collective-permute-start.4) | collective-permute-done | bytes 327712 | tf_op jit(solution)/shard_map/ppermute | solution.py:512
  31.3 0.1 add_convert_fusion
  31.4 15.7 %all_to_all.15 = bf16[16,80,128]{2,1,0:T(8,128)(2,1)S(1)} all-to-all(bf16[16,80,128]{2,1,0:T(8,128)(2,1)S(1)} %bitcast.21), channel_id=1, replica_groups={{0,2,4,6,8,10,12,14,16,18,20,22,24,26,28,30},{1,3,5,7,9,11,13,15,17,19,..., dimensions={0} | all-to-all | bytes 655360 | tf_op jit(solution)/shard_map/all_to_all | solution.py:502
  47.1 0.1 reduce_sum.24
  47.2 16.4 %all_to_all.16 = bf16[8,80,128]{2,1,0:T(8,128)(2,1)S(1)} all-to-all(bf16[8,80,128]{2,1,0:T(8,128)(2,1)S(1)} %broadcast_in_dim.4), channel_id=1, replica_groups=mesh['sample'=8,'space'=32] {'sample'}, dimensions={0} | all-to-all | bytes 327680 | tf_op jit(solution)/shard_map/all_to_all | solution.py:496
  63.6 10.6 %all_to_all.17 = bf16[16,80,128]{2,1,0:T(8,128)(2,1)S(1)} all-to-all(bf16[16,80,128]{2,1,0:T(8,128)(2,1)S(1)} %broadcast_in_dim.5), channel_id=1, replica_groups={{0,2,4,6,8,10,12,14,16,18,20,22,24,26,28,30},{1,3,5,7,9,11,13,15,17,19,..., dimensions={0} | all-to-all | bytes 655360 | tf_op jit(solution)/shard_map/all_to_all | solution.py:502
  74.2 3.9 %collective-permute-start.5 = (bf16[1280,128]{1,0:T(8,128)(2,1)S(1)}, bf16[1280,128]{1,0:T(8,128)(2,1)S(1)}, u32[]{:S(2)}, u32[]{:S(2)}) collective-permute-start(bf16[1280,128]{1,0:T(8,128)(2,1)S(1)} %bitcast.19), channel_id=1, source_target_pairs={{0,1},{2,3},{4,5},{6,7},{8,9},{10,11},{12,13},{14,15},{16,17},{18,... | collective-permute-start | bytes 983048 | tf_op jit(solution)/shard_map/ppermute | solution.py:512
  78.1 1.3 %collective-permute-done.5.other = bf16[1280,128]{1,0:T(8,128)(2,1)S(1)} collective-permute-done((bf16[1280,128]{1,0:T(8,128)(2,1)S(1)}, bf16[1280,128]{1,0:T(8,128)(2,1)S(1)}, u32[]{:S(2)}, u32[]{:S(2)}) %collective-permute-start.5) | collective-permute-done | bytes 327712 | tf_op jit(solution)/shard_map/ppermute | solution.py:512
  79.4 0.0 copy-done.15
  79.4 0.7 copy-done.16
  80.1 2.3 %finish.1 = (f32[27,4,32]{2,1,0:T(4,128)}, f32[27,32,64]{2,1,0:T(8,128)}, f32[27,64,128]{2,1,0:T(8,128)}) custom-call(f32[3]{0:T(128)} %constant.63.scales, bf16[1280,128]{1,0:T(8,128)(2,1)} %bitcast.20, bf16[1280,128]{1,0:T(8,128)(2,1)} %copy-done.16), custom_call_target="tpu_custom_call" | custom-call | tf_op jit(solution)/shard_map/finish/pallas_call | solution.py:485
  (13 shorter events, 0.1 us)
Async XLA Ops:
  0.6 11.9 %copy-start = (bf16[1,1,2,16,128]{4,3,2,1,0:T(8,128)(2,1)S(1)}, bf16[1,1,2,16,128]{4,3,2,1,0:T(8,128)(2,1)}, u32[]{:S(2)}) copy-start(bf16[1,1,2,16,128]{4,3,2,1,0:T(8,128)(2,1)} %param.17) | copy-start | bytes 24580
  0.6 13.4 %copy-start.1 = (bf16[3,3,3,64,128]{4,3,2,1,0:T(8,128)(2,1)S(1)}, bf16[3,3,3,64,128]{4,3,2,1,0:T(8,128)(2,1)}, u32[]{:S(2)}) copy-start(bf16[3,3,3,64,128]{4,3,2,1,0:T(8,128)(2,1)} %param.20) | copy-start | bytes 1327108
  0.7 13.4 %copy-start.4 = (bf16[3,3,3,4,32]{4,3,2,1,0:T(4,128)(2,1)S(1)}, bf16[3,3,3,4,32]{4,3,2,1,0:T(4,128)(2,1)}, u32[]{:S(2)}) copy-start(bf16[3,3,3,4,32]{4,3,2,1,0:T(4,128)(2,1)} %param.18) | copy-start | bytes 20740
  0.7 5.3 %collective-permute-start = (bf16[512,128]{1,0:T(8,128)(2,1)}, bf16[512,128]{1,0:T(8,128)(2,1)S(1)}, u32[]{:S(2)}, u32[]{:S(2)}) collective-permute-start(bf16[512,128]{1,0:T(8,128)(2,1)} %bitcast.15), channel_id=1, source_target_pairs={{0,1},{2,3},{4,5},{6,7},{8,9},{10,11},{12,13},{14,15},{16,17},{18,... | collective-permute-start | bytes 393224 | tf_op jit(solution)/shard_map/ppermute | solution.py:512
  4.0 8.5 %collective-permute-start.1 = (bf16[512,128]{1,0:T(8,128)(2,1)}, bf16[512,128]{1,0:T(8,128)(2,1)S(1)}, u32[]{:S(2)}, u32[]{:S(2)}) collective-permute-start(bf16[512,128]{1,0:T(8,128)(2,1)} %bitcast.16), channel_id=1, source_target_pairs={{1,2},{3,4},{5,6},{7,8},{9,10},{11,12},{13,14},{15,16},{17,18},{19... | collective-permute-start | bytes 393224 | tf_op jit(solution)/shard_map/ppermute | solution.py:512
  6.7 6.2 %collective-permute-start.2 = (bf16[480,128]{1,0:T(8,128)(2,1)S(1)}, bf16[480,128]{1,0:T(8,128)(2,1)S(1)}, u32[]{:S(2)}, u32[]{:S(2)}) collective-permute-start(bf16[480,128]{1,0:T(8,128)(2,1)S(1)} %pad_maximum_fusion.1), channel_id=1, source_target_pairs={{1,2},{3,4},{5,6},{7,8},{9,10},{11,12},{13,14},{15,16},{17,18},{19... | collective-permute-start | bytes 368648 | tf_op jit(solution)/shard_map/ppermute | solution.py:512
  10.3 0.9 %copy-start.2 = (bf16[3,3,3,32,64]{4,3,2,1,0:T(8,128)(2,1)S(1)}, bf16[3,3,3,32,64]{4,3,2,1,0:T(8,128)(2,1)}, u32[]{:S(2)}) copy-start(bf16[3,3,3,32,64]{4,3,2,1,0:T(8,128)(2,1)} %param.19) | copy-start | bytes 331780
  11.3 2.8 %copy-start.3 = (bf16[1,8,4,16,128]{4,3,2,1,0:T(8,128)(2,1)S(1)}, bf16[1,8,4,16,128]{4,3,2,1,0:T(8,128)(2,1)}, u32[]{:S(2)}) copy-start(bf16[1,8,4,16,128]{4,3,2,1,0:T(8,128)(2,1)} %param.16) | copy-start | bytes 393220
  11.3 2.8 %copy-start.5 = (bf16[128,1152]{1,0:T(8,128)(2,1)S(1)}, bf16[128,1152]{1,0:T(8,128)(2,1)}, u32[]{:S(2)}) copy-start(bf16[128,1152]{1,0:T(8,128)(2,1)} %constant.56.clone.spread) | copy-start | bytes 884740
  11.3 2.8 %copy-start.6 = (bf16[256,512]{1,0:T(8,128)(2,1)S(1)}, bf16[256,512]{1,0:T(8,128)(2,1)}, u32[]{:S(2)}) copy-start(bf16[256,512]{1,0:T(8,128)(2,1)} %constant.59.clone.grow1) | copy-start | bytes 786436
  11.3 2.8 %copy-start.7 = (bf16[256,384]{1,0:T(8,128)(2,1)S(1)}, bf16[256,384]{1,0:T(8,128)(2,1)}, u32[]{:S(2)}) copy-start(bf16[256,384]{1,0:T(8,128)(2,1)} %constant.53.clone.odd) | copy-start | bytes 589828
  11.3 2.8 %copy-start.8 = (bf16[256,384]{1,0:T(8,128)(2,1)S(1)}, bf16[256,384]{1,0:T(8,128)(2,1)}, u32[]{:S(2)}) copy-start(bf16[256,384]{1,0:T(8,128)(2,1)} %constant.52.clone.pair) | copy-start | bytes 589828
  11.3 2.8 %copy-start.9 = (bf16[96,768]{1,0:T(8,128)(2,1)S(1)}, bf16[96,768]{1,0:T(8,128)(2,1)}, u32[]{:S(2)}) copy-start(bf16[96,768]{1,0:T(8,128)(2,1)} %constant.57.clone.grow_g) | copy-start | bytes 442372
  11.3 2.8 %copy-start.10 = (bf16[108,640]{1,0:T(8,128)(2,1)S(1)}, bf16[108,640]{1,0:T(8,128)(2,1)}, u32[]{:S(2)}) copy-start(bf16[108,640]{1,0:T(8,128)(2,1)} %constant.50.clone.perm) | copy-start | bytes 414724
  11.3 2.8 %copy-start.11 = (bf16[128,512]{1,0:T(8,128)(2,1)S(1)}, bf16[128,512]{1,0:T(8,128)(2,1)}, u32[]{:S(2)}) copy-start(bf16[128,512]{1,0:T(8,128)(2,1)} %constant.58.clone.grow2) | copy-start | bytes 393220
  11.3 2.8 %copy-start.12 = (bf16[512,128]{1,0:T(8,128)(2,1)S(1)}, bf16[512,128]{1,0:T(8,128)(2,1)}, u32[]{:S(2)}) copy-start(bf16[512,128]{1,0:T(8,128)(2,1)} %constant.55.clone.squeeze) | copy-start | bytes 393220
  11.3 2.8 %copy-start.13 = (bf16[128,384]{1,0:T(8,128)(2,1)S(1)}, bf16[128,384]{1,0:T(8,128)(2,1)}, u32[]{:S(2)}) copy-start(bf16[128,384]{1,0:T(8,128)(2,1)} %constant.54.clone.even) | copy-start | bytes 294916
  11.3 2.8 %copy-start.14 = (bf16[128,256]{1,0:T(8,128)(2,1)S(1)}, bf16[128,256]{1,0:T(8,128)(2,1)}, u32[]{:S(2)}) copy-start(bf16[128,256]{1,0:T(8,128)(2,1)} %constant.51.clone.shift) | copy-start | bytes 196612
  12.6 1.4 %collective-permute-start.3 = (bf16[480,128]{1,0:T(8,128)(2,1)S(1)}, bf16[480,128]{1,0:T(8,128)(2,1)S(1)}, u32[]{:S(2)}, u32[]{:S(2)}) collective-permute-start(bf16[480,128]{1,0:T(8,128)(2,1)S(1)} %pad_maximum_fusion), channel_id=1, source_target_pairs={{0,1},{2,3},{4,5},{6,7},{8,9},{10,11},{12,13},{14,15},{16,17},{18,... | collective-permute-start | bytes 368648 | tf_op jit(solution)/shard_map/ppermute | solution.py:512
  29.6 1.7 %collective-permute-start.4 = (bf16[1280,128]{1,0:T(8,128)(2,1)S(1)}, bf16[1280,128]{1,0:T(8,128)(2,1)S(1)}, u32[]{:S(2)}, u32[]{:S(2)}) collective-permute-start(bf16[1280,128]{1,0:T(8,128)(2,1)S(1)} %get-tuple-element.21), channel_id=1, source_target_pairs={{0,1},{2,3},{4,5},{6,7},{8,9},{10,11},{12,13},{14,15},{16,17},{18,... | collective-permute-start | bytes 983048 | tf_op jit(solution)/shard_map/ppermute | solution.py:512
  74.2 5.2 %copy-start.15 = (bf16[16,80,128]{2,1,0:T(8,128)(2,1)}, bf16[16,80,128]{2,1,0:T(8,128)(2,1)S(1)}, u32[]{:S(2)}) copy-start(bf16[16,80,128]{2,1,0:T(8,128)(2,1)S(1)} %all_to_all.17) | copy-start | bytes 983044
  74.2 5.2 %collective-permute-start.5 = (bf16[1280,128]{1,0:T(8,128)(2,1)S(1)}, bf16[1280,128]{1,0:T(8,128)(2,1)S(1)}, u32[]{:S(2)}, u32[]{:S(2)}) collective-permute-start(bf16[1280,128]{1,0:T(8,128)(2,1)S(1)} %bitcast.19), channel_id=1, source_target_pairs={{0,1},{2,3},{4,5},{6,7},{8,9},{10,11},{12,13},{14,15},{16,17},{18,... | collective-permute-start | bytes 983048 | tf_op jit(solution)/shard_map/ppermute | solution.py:512
  79.4 0.7 copy-start.16

commit v6 on v5

--- a/solution.py
+++ b/solution.py
@@ -1,3 +1,5 @@
+import functools
+
 import jax
 import jax.numpy as jnp
 import numpy as np
@@ -92,9 +94,31 @@
     return [kd * 9 + (2 - kh) * 3 + kw for kh in range(3)]
 
 
-def build(filter_two, t2, t2r, s2, s2r, sems):
-    copy2r = pltpu.make_async_copy(s2r, t2r, sems.at[0])
-    copy2 = pltpu.make_async_copy(s2, t2, sems.at[1])
+def band_one(filter_one, perm, t1):
+    lane = lax.broadcasted_iota(jnp.int32, (32, 640), 1) % 16
+    rows = filter_one[...].astype(F32).reshape(108, 32).astype(BF)
+    base = lax.dot_general(rows, perm[...], TN, preferred_element_type=F32)
+    for h in range(16):
+        moved = pltpu.roll(base, (h - 1) % 640, 1) if h != 1 else base
+        if h == 0:
+            moved = jnp.where(lane == 15, 0.0, moved)
+        if h == 15:
+            moved = jnp.where(lane == 0, 0.0, moved)
+        t1[32 * h : 32 * h + 32, :] = moved[:, :576].astype(BF)
+
+
+def band_two(filter_two, t2):
+    taps = []
+    for kh in range(3):
+        rows = jnp.concatenate([filter_two[taps_of(it)[kh]] for it in range(9)], axis=0)
+        taps.append(rows.astype(F32).T * 0.5)
+    zero = jnp.zeros((64, 288), F32)
+    for s in range(5):
+        parts = [taps[p - s + 1] if 0 <= p - s + 1 < 3 else zero for p in range(5)]
+        t2[64 * s : 64 * s + 64, :] = jnp.concatenate(parts, axis=1).astype(BF)
+
+
+def band_two_back(filter_two, t2r):
     for it in range(9):
         v2 = [filter_two[k].astype(F32) for k in taps_back(it)]
         zero = jnp.zeros((32, 64), F32)
@@ -107,33 +131,113 @@
             for m in range(4):
                 hp = 2 * m + 1 - s
                 if 0 <= hp < 8:
-                    s2r[32 * hp : 32 * hp + 32, it * 512 + 128 * m : it * 512 + 128 * m + 128] = tile
-    copy2r.start()
-    taps = []
-    for kh in range(3):
-        rows = jnp.concatenate([filter_two[taps_of(it)[kh]] for it in range(9)], axis=0)
-        taps.append(rows.astype(F32).T * 0.5)
-    zero = jnp.zeros((64, 288), F32)
-    for s in range(5):
-        parts = [taps[p - s + 1] if 0 <= p - s + 1 < 3 else zero for p in range(5)]
-        s2[64 * s : 64 * s + 64, :] = jnp.concatenate(parts, axis=1).astype(BF)
-    copy2.start()
-    copy2r.wait()
-    copy2.wait()
+                    t2r[32 * hp : 32 * hp + 32, it * 512 + 128 * m : it * 512 + 128 * m + 128] = tile
+
+
+def with_column_shifts(rows, shift, x1, at):
+    moved = dot(rows, shift[...]).astype(BF)
+    for p in range(rows.shape[0] // 64):
+        lanes = slice(128 * (at + p), 128 * (at + p) + 128)
+        x1[0:64, lanes] = moved[64 * p : 64 * p + 64, :128]
+        x1[64:128, lanes] = rows[64 * p : 64 * p + 64, :]
+        x1[128:192, lanes] = moved[64 * p : 64 * p + 64, 128:]
+    return at + rows.shape[0] // 64
+
+
+def layer_one(t1, x1, at, scale):
+    rhs = jnp.concatenate(
+        [x1[:, 128 * (at + kd) : 128 * (at + kd) + 256] for kd in range(3)], axis=0
+    )
+    half = dot(t1[...], rhs)
+    t = jnp.tanh(half)
+    act = half + half * t
+    act = act[:, :128] + act[:, 128:]
+    act = act.reshape(8, 2, 32, 128)
+    act = (act[:, 0] + act[:, 1]).reshape(256, 128)
+    act = act + pltpu.roll(act, 127, 1)
+    return half, t, (act * scale).astype(BF)
+
+
+def either_of(first_core):
+    def either(a, b, lo, hi):
+        return jnp.where(first_core, a[lo:hi, :], b[lo:hi, :])
+
+    return either
+
+
+def near_part(
+    vol_own,
+    swap_core,
+    swap_chip,
+    filter_one,
+    filter_two,
+    filter_three,
+    perm,
+    shift,
+    t1_far,
+    t2_far,
+    w3t_far,
+    t2r_far,
+    x1_far,
+    pp_far,
+    sl1_far,
+    t1,
+    t2,
+    w3t,
+    t2r,
+    pp,
+    sl1,
+    x1,
+    sems,
+):
+    me, blocks = position()
+    either = either_of(me % 2 == 0)
+    copies = []
+
+    def leave(near_ref, far_ref):
+        copies.append(pltpu.make_async_copy(near_ref, far_ref, sems.at[len(copies)]))
+        copies[-1].start()
+
+    band_two_back(filter_two, t2r)
+    leave(t2r, t2r_far)
+    band_two(filter_two, t2)
+    leave(t2, t2_far)
+    w3t[...] = (filter_three[...].astype(F32).T * 0.5).astype(BF)
+    leave(w3t, w3t_far)
+    band_one(filter_one, perm, t1)
+    leave(t1, t1_far)
+    at = with_column_shifts(either(swap_chip, swap_core, 64, 512), shift, x1, 0)
+    at = with_column_shifts(vol_own[...], shift, x1, at)
+    at = with_column_shifts(either(swap_core, swap_chip, 0, 448), shift, x1, at)
+    leave(x1.at[:, 768:2048], x1_far)
+    for j in range(10):
+        scale = jnp.where(inside(4 * me - 3 + j, 4 * blocks), 0.125, 0.0)
+        half, t, act = layer_one(t1, x1, 2 * j, scale)
+        if 3 <= j < 7:
+            slope = (1.0 + t) + half * (1.0 - t * t)
+            sl1[:, 256 * (j - 3) : 256 * (j - 3) + 256] = slope.astype(BF)
+        pp[:, 128 * j : 128 * j + 128] = act
+        if j == 6:
+            leave(sl1, sl1_far)
+    leave(pp, pp_far)
+    for copy in copies:
+        copy.wait()
 
 
 def body(
-    vol_own,
-    grad_own,
     swap_core,
     swap_chip,
     swap_chip2,
     swap_core2,
-    filter_one,
+    grad_own,
     filter_three,
+    t1_far,
     t2_far,
+    w3t_far,
     t2r_far,
-    perm,
+    x1_far,
+    pp_far,
+    sl1_far,
     shift,
     pair,
     odd,
@@ -151,11 +255,12 @@
     t2r,
     x1,
     pp,
+    sl1,
+    xo,
     x2,
     q,
     x3,
     d2c,
-    sl1,
     sl2,
     d2,
     d1,
@@ -164,61 +269,33 @@
 ):
     me, blocks = position()
     first_core = me % 2 == 0
+    either = either_of(first_core)
+    pairs = (
+        (t1_far, t1),
+        (pp_far, pp.at[:, 512:1792]),
+        (t2_far, t2),
+        (w3t_far, w3t),
+        (t2r_far, t2r),
+        (sl1_far, sl1),
+        (x1_far, x1),
+    )
     copies = [
         pltpu.make_async_copy(far_ref, near_ref, sems.at[i])
-        for i, (far_ref, near_ref) in enumerate(((t2_far, t2), (t2r_far, t2r)))
+        for i, (far_ref, near_ref) in enumerate(pairs)
     ]
     for copy in copies:
         copy.start()
 
-    lane = lax.broadcasted_iota(jnp.int32, (32, 640), 1) % 16
-    rows = filter_one[...].astype(F32).reshape(108, 32).astype(BF)
-    base = lax.dot_general(rows, perm[...], TN, preferred_element_type=F32)
-    for h in range(16):
-        moved = pltpu.roll(base, (h - 1) % 640, 1) if h != 1 else base
-        if h == 0:
-            moved = jnp.where(lane == 15, 0.0, moved)
-        if h == 15:
-            moved = jnp.where(lane == 0, 0.0, moved)
-        t1[32 * h : 32 * h + 32, :] = moved[:, :576].astype(BF)
-    w3t[...] = (filter_three[...].astype(F32).T * 0.5).astype(BF)
-
-    def either(a, b, lo, hi):
-        return jnp.where(first_core, a[lo:hi, :], b[lo:hi, :])
-
-    at = 0
-    for rows in (
-        either(swap_chip2, swap_core2, 0, 448),
-        either(swap_chip, swap_core, 0, 512),
-        vol_own[...],
-        either(swap_core, swap_chip, 0, 512),
-        either(swap_core2, swap_chip2, 0, 448),
-    ):
-        moved = dot(rows, shift[...]).astype(BF)
-        count = rows.shape[0] // 64
-        for p in range(count):
-            lanes = slice(128 * (at + p), 128 * (at + p) + 128)
-            x1[0:64, lanes] = moved[64 * p : 64 * p + 64, :128]
-            x1[64:128, lanes] = rows[64 * p : 64 * p + 64, :]
-            x1[128:192, lanes] = moved[64 * p : 64 * p + 64, 128:]
-        at += count
-
-    for j in range(18):
-        rhs = jnp.concatenate(
-            [x1[:, (2 * j + kd) * 128 : (2 * j + kd) * 128 + 256] for kd in range(3)], axis=0
-        )
-        half = dot(t1[...], rhs)
-        t = jnp.tanh(half)
-        if 7 <= j < 11:
-            slope = (1.0 + t) + half * (1.0 - t * t)
-            sl1[:, (j - 7) * 256 : (j - 7) * 256 + 256] = slope.astype(BF)
-        act = half + half * t
-        act = act[:, :128] + act[:, 128:]
-        act = act.reshape(8, 2, 32, 128)
-        act = (act[:, 0] + act[:, 1]).reshape(256, 128)
-        act = act + pltpu.roll(act, 127, 1)
+    at = with_column_shifts(either(swap_chip2, swap_core2, 0, 448), shift, xo, 0)
+    at = with_column_shifts(either(swap_chip, swap_core, 0, 192), shift, xo, at)
+    at = with_column_shifts(either(swap_core, swap_chip, 320, 512), shift, xo, at)
+    at = with_column_shifts(either(swap_core2, swap_chip2, 0, 448), shift, xo, at)
+    copies[0].wait()
+    for j in (0, 1, 2, 3, 14, 15, 16, 17):
         scale = jnp.where(inside(4 * me - 7 + j, 4 * blocks), 0.125, 0.0)
-        pp[:, j * 128 : j * 128 + 128] = (act * scale).astype(BF)
+        act = layer_one(t1, xo, 2 * j if j < 4 else 10 + 2 * (j - 14), scale)[2]
+        pp[:, 128 * j : 128 * j + 128] = act
+    copies[1].wait()
 
     for first in range(17):
         got = dot(pp[:, first * 128 : first * 128 + 256], pair[...]).astype(BF)
@@ -231,7 +308,7 @@
                         :, 128 * kw : 128 * kw + 128
                     ]
 
-    copies[0].wait()
+    copies[2].wait()
     for c in range(4):
         lanes = slice(c * 256, c * 256 + 256)
         for g in range(2):
@@ -279,6 +356,7 @@
         axis=0,
     )
     grown = dot(rows.astype(F32).T.astype(BF), grow_g[...])
+    copies[3].wait()
     half = dot(w3t[...], x3[...])
     t = jnp.tanh(half)
     d3 = (grown * ((1.0 + t) + half * (1.0 - t * t))).astype(BF)
@@ -341,8 +419,9 @@
                         d2c[512 * k : 512 * k + 512, 128 * m : 128 * m + 128] = got[
                             :, 128 * kw : 128 * kw + 128
                         ]
-    copies[1].wait()
+    copies[4].wait()
     back = dot(t2r[...], d2c[...]).astype(BF)
+    copies[5].wait()
     back = dot(back, grow1[...])
     for h in range(16):
         rows = slice(32 * h, 32 * h + 32)
@@ -372,7 +451,8 @@
                 lane16 < 64, low[:16], high[16:]
             ).astype(BF)
 
-    lhs = jnp.concatenate([x1[:, 128 * (14 + kd) : 128 * (14 + kd) + 1024] for kd in range(3)], axis=0)
+    copies[6].wait()
+    lhs = jnp.concatenate([x1[:, 128 * kd : 128 * kd + 1024] for kd in range(3)], axis=0)
     got = lax.dot_general(lhs, d1[...], NT, preferred_element_type=F32)
     row = lax.broadcasted_iota(jnp.int32, (576, 128), 0) % 16
     col = lax.broadcasted_iota(jnp.int32, (576, 128), 1) // 32
@@ -397,11 +477,11 @@
     sent[...] = out[pl.ds(half_rows - mine, half_rows), :]
 
 
-def finish(scales, mine, other, one, two, three):
+def finish(scales, mine, other, one_far, two_far, three_far, one, two, three, sems):
     first_core = position()[0] % 2 == 0
+    half_rows = mine.shape[0]
 
     def rows(at, count):
-        half_rows = mine.shape[0]
         parts = []
         while count:
             use = min(count, half_rows - at % half_rows)
@@ -411,15 +491,29 @@
             at, count = (at + use, count - use)
         return parts[0] if len(parts) == 1 else jnp.concatenate(parts, axis=0)
 
+    copies = []
+
+    def leave(near_ref, far_ref):
+        copies.append(pltpu.make_async_copy(near_ref, far_ref, sems.at[len(copies)]))
+        copies[-1].start()
+
     for k in range(27):
-        three[k] = rows(64 * k, 64) * scales[2]
         got = rows(G_TWO + 16 * k, 16) * scales[1]
         two[k, 0:16, :] = got[:, :64]
         two[k, 16:32, :] = got[:, 64:]
+    leave(two, two_far)
     got = rows(G_ONE, 48) * scales[0]
     for it in range(9):
         for kh, k in enumerate(taps_of(it)):
             one[k] = got[4 * it : 4 * it + 4, 32 * kh : 32 * kh + 32]
+    leave(one, one_far)
+    for third in range(3):
+        for k in range(9 * third, 9 * third + 9):
+            three[k] = rows(64 * k, 64) * scales[2]
+        here = slice(9 * third, 9 * third + 9)
+        leave(three.at[here], three_far.at[here])
+    for copy in copies:
+        copy.wait()
 
 
 VMEM = pl.BlockSpec(memory_space=pltpu.VMEM)
@@ -430,48 +524,58 @@
 
 
 FAR = pl.BlockSpec(memory_space=pl.ANY)
-BANDED = ((320, 1440), (256, 4608))
-
-
-def run_build(filter_two):
+HANDED = (
+    (512, 576),
+    (320, 1440),
+    (128, 1728),
+    (256, 4608),
+    (192, 1280),
+    (256, 1280),
+    (512, 1024),
+)
+
+
+def run_near(volume, swap_core, swap_chip, filter_one, filter_two, filter_three):
+    tables = [jnp.asarray(t, BF) for t in one_hot_tables()[:2]]
+    args = [volume, swap_core, swap_chip, filter_one, filter_two, filter_three, *tables]
     return pl.pallas_call(
-        build,
-        out_shape=[jax.ShapeDtypeStruct(shape, BF) for shape in BANDED],
-        in_specs=[VMEM],
-        out_specs=[FAR] * 2,
-        scratch_shapes=[near(*shape) for shape in BANDED] + [pltpu.SemaphoreType.DMA((2,))],
-        compiler_params=pltpu.CompilerParams(vmem_limit_bytes=16 * 1024 * 1024),
-        cost_estimate=pl.CostEstimate(flops=10**9, bytes_accessed=6 * 10**6, transcendentals=0),
-        name="build",
-    )(filter_two)
-
-
-def local_grads(volume, grad, swaps, filter_one, filter_three, banded, rows):
-    tables = [jnp.asarray(t, BF) for t in one_hot_tables()]
-    args = [volume, grad, *swaps, filter_one, filter_three, *banded, *tables]
-    far = (8, 9)
+        near_part,
+        out_shape=[jax.ShapeDtypeStruct(shape, BF) for shape in HANDED],
+        in_specs=[VMEM] * len(args),
+        out_specs=[FAR] * len(HANDED),
+        scratch_shapes=[near(*shape) for shape in HANDED[:4] + HANDED[5:]]
+        + [near(192, 22 * 128), pltpu.SemaphoreType.DMA((len(HANDED),))],
+        compiler_params=pltpu.CompilerParams(vmem_limit_bytes=20 * 1024 * 1024),
+        cost_estimate=pl.CostEstimate(
+            flops=3 * 10**9, bytes_accessed=8 * 10**6, transcendentals=0
+        ),
+        name="near_part",
+    )(*args)
+
+
+def local_grads(swaps, grad, filter_three, handed, rows):
+    tables = [jnp.asarray(t, BF) for t in one_hot_tables()[1:]]
+    args = [*swaps, grad, filter_three, *handed, *tables]
+    far = range(6, 6 + len(HANDED))
     return pl.pallas_call(
         body,
         out_shape=[jax.ShapeDtypeStruct((rows // 2, 128), BF)] * 2,
         in_specs=[FAR if i in far else VMEM for i in range(len(args))],
         out_specs=[VMEM] * 2,
-        scratch_shapes=[
-            near(512, 576),
-            near(320, 1440),
-            near(128, 1728),
-            near(256, 4608),
-            near(192, 38 * 128),
+        scratch_shapes=[near(*shape) for shape in HANDED[:5]]
+        + [
             near(256, 18 * 128),
+            near(512, 1024),
+            near(192, 20 * 128),
             near(2304, 1024),
             near(512, 512),
             near(1728, 768),
             near(4608, 256),
-            near(512, 1024),
             near(512, 512),
             near(512, 512),
             near(512, 1024),
             near(rows, 128),
-            pltpu.SemaphoreType.DMA((2,)),
+            pltpu.SemaphoreType.DMA((len(HANDED),)),
         ],
         compiler_params=pltpu.CompilerParams(vmem_limit_bytes=LIMIT * 1024 * 1024),
         cost_estimate=pl.CostEstimate(flops=10**10, bytes_accessed=10**7, transcendentals=0),
@@ -480,15 +584,17 @@
 
 
 def run_finish(mine, other, cells):
-    scales = 1.0 / jnp.sqrt(jnp.array([cells, cells / 8.0, cells / 64.0], F32))
+    scales = [float(1.0 / np.sqrt(cells / size)) for size in (1.0, 8.0, 64.0)]
     shapes = [(27, 4, 32), (27, 32, 64), (27, 64, 128)]
     outs = pl.pallas_call(
-        finish,
+        functools.partial(finish, scales),
         out_shape=[jax.ShapeDtypeStruct(shape, F32) for shape in shapes],
-        in_specs=[pl.BlockSpec(memory_space=pltpu.SMEM), VMEM, VMEM],
-        out_specs=[VMEM] * 3,
+        in_specs=[VMEM] * 2,
+        out_specs=[FAR] * 3,
+        scratch_shapes=[pltpu.VMEM(shape, F32) for shape in shapes]
+        + [pltpu.SemaphoreType.DMA((5,))],
         name="finish",
-    )(scales, mine, other)
+    )(mine, other)
     return tuple(o.reshape(3, 3, 3, *o.shape[1:]) for o in outs)
 
 
@@ -529,19 +635,12 @@
     swap_chip = swap(own, 1)
     relay = second(swap_core)
     swap_chip2 = swap(relay, 1)
-    f2_later = lax.optimization_barrier((f2, relay))[0]
-    banded = run_build(f2_later)
-    swap_chip, *banded = lax.optimization_barrier((swap_chip, *banded))
-    swap_core2 = swap(second(swap_chip, 1), 0)
+    chip_later = lax.optimization_barrier((swap_chip, relay))[0]
+    swap_core2 = swap(second(chip_later, 1), 0)
     chips = spaces // 2
+    handed = run_near(own, swap_core, swap_chip, f1, f2, f3)
     keep, send = local_grads(
-        own,
-        grad,
-        (swap_core, swap_chip, swap_chip2, swap_core2),
-        f1,
-        f3,
-        banded,
-        spaces * SLOT,
+        (swap_core, swap_chip, swap_chip2, swap_core2), grad, f3, handed, spaces * SLOT
     )
     half = (keep.astype(F32) + swap(send, 0).astype(F32)).astype(BF)
     part = total_of(over_chips(half.reshape(chips, SLOT, 128)))

time: 82.8 us -> 92.1 us (1.11)
  Pallas kernels: 18.9 us -> 23.8 us
  local copies, waits for them, and re-layouts: 1.84 us -> 6.24 us
  waiting for transfers between devices: 4.07 us -> 2.68 us
    pallas_call x2, Pallas kernels: 3.46 us -> 8.49 us  [the longest x1 6.17 us: run_near(): pl.pallas_call(near_part, out_shape=[jax.ShapeDtypeStruct(shape, BF) for...]
    unnamed x34 -> x38, local copies, waits for them, and re-layouts: 1.74 us -> 6.15 us
    ppermute x6, waiting for transfers between devices: 4.07 us -> 2.68 us  [swap(): return lax.ppermute(values, 'space', pairs + [(j, i) for i, j in pairs])]
  transfers between devices with their start and end apart: 6 -> 6, of which waited for: 4 -> 3; matrix products, arithmetic and copies ran while one was open for 1% -> 2% of each run, Pallas kernels for 1% -> 7%
where the time goes in v6:
time: 92.1 us; the launch traced here: 91.5 us
  blocking collectives  42.7 us (46%)
  Pallas kernels  23.8 us (26%)
  starting transfers between devices  13.4 us (15%)
  local copies, waits for them, and re-layouts  6.24 us (7%)
  waiting for transfers between devices  2.68 us (3%)
  other arithmetic  1.59 us (2%)
  between operations  1.08 us (1%)
    all_to_all x2, blocking collectives, over_chips(): lax.all_to_all(pieces, 'space', 0, 0, axis_index_groups=groups, tiled=True)  26.4 us
    all_to_all x1, blocking collectives, over_sample(): return lax.all_to_all(pieces, 'sample', 0, 0, tiled=True)  16.3 us
    pallas_call x1, Pallas kernels, local_grads(): pl.pallas_call(body, out_shape=[jax.ShapeDtypeStruct((rows // 2, 128), BF...  15.3 us
    ppermute x6, starting transfers between devices, swap(): return lax.ppermute(values, 'space', pairs + [(j, i) for i, j in pairs])  13.4 us
    pallas_call x1, Pallas kernels, run_near(): pl.pallas_call(near_part, out_shape=[jax.ShapeDtypeStruct(shape, BF) for...  6.17 us
    unnamed x38, local copies, waits for them, and re-layouts  6.15 us
    ppermute x6, waiting for transfers between devices, swap(): return lax.ppermute(values, 'space', pairs + [(j, i) for i, j in pairs])  2.68 us
    pallas_call x1, Pallas kernels, run_finish(): pl.pallas_call(functools.partial(finish, scales), out_shape=[jax.ShapeDty...  2.32 us
  transfers between devices with their start and end apart: 6, of which 3 were waited for; matrix products, arithmetic and copies ran while one was open for 2% of the time, Pallas kernels for 7%

profile of v6, /device:TPU:1, one launch (start us, length us, event | category | flops | bytes accessed | tf_op | source)
XLA Modules:
  0.0 91.5 jit_solution(5146535352752033633)
XLA Ops:
  0.6 3.3 %collective-permute-start = (bf16[512,128]{1,0:T(8,128)(2,1)}, bf16[512,128]{1,0:T(8,128)(2,1)S(1)}, u32[]{:S(2)}, u32[]{:S(2)}) collective-permute-start(bf16[512,128]{1,0:T(8,128)(2,1)} %bitcast.16), channel_id=1, source_target_pairs={{0,1},{2,3},{4,5},{6,7},{8,9},{10,11},{12,13},{14,15},{16,17},{18,... | collective-permute-start | bytes 393224 | tf_op jit(solution)/shard_map/ppermute | solution.py:618
  4.0 1.9 %collective-permute-start.1 = (bf16[512,128]{1,0:T(8,128)(2,1)}, bf16[512,128]{1,0:T(8,128)(2,1)S(1)}, u32[]{:S(2)}, u32[]{:S(2)}) collective-permute-start(bf16[512,128]{1,0:T(8,128)(2,1)} %bitcast.17), channel_id=1, source_target_pairs={{1,2},{3,4},{5,6},{7,8},{9,10},{11,12},{13,14},{15,16},{17,18},{19... | collective-permute-start | bytes 393224 | tf_op jit(solution)/shard_map/ppermute | solution.py:618
  5.9 0.0 collective-permute-done.swap_core
  5.9 0.7 pad_maximum_fusion.1
  6.6 3.6 %collective-permute-start.2 = (bf16[480,128]{1,0:T(8,128)(2,1)S(1)}, bf16[480,128]{1,0:T(8,128)(2,1)S(1)}, u32[]{:S(2)}, u32[]{:S(2)}) collective-permute-start(bf16[480,128]{1,0:T(8,128)(2,1)S(1)} %pad_maximum_fusion.1), channel_id=1, source_target_pairs={{1,2},{3,4},{5,6},{7,8},{9,10},{11,12},{13,14},{15,16},{17,18},{19... | collective-permute-start | bytes 368648 | tf_op jit(solution)/shard_map/ppermute | solution.py:618
  10.3 0.2 collective-permute-done.1.swap_chip
  10.5 0.7 pad_maximum_fusion
  11.2 0.1 collective-permute-start.3
  11.3 0.0 copy-start.1
  11.3 1.0 %copy-done.1 = bf16[3,3,3,64,128]{4,3,2,1,0:T(8,128)(2,1)S(1)} copy-done((bf16[3,3,3,64,128]{4,3,2,1,0:T(8,128)(2,1)S(1)}, bf16[3,3,3,64,128]{4,3,2,1,0:T(8,128)(2,1)}, u32[]{:S(2)}) %copy-start.1) | copy-done | bytes 442392
  12.3 0.9 %copy-done.3 = bf16[3,3,3,32,64]{4,3,2,1,0:T(8,128)(2,1)S(1)} copy-done((bf16[3,3,3,32,64]{4,3,2,1,0:T(8,128)(2,1)S(1)}, bf16[3,3,3,32,64]{4,3,2,1,0:T(8,128)(2,1)}, u32[]{:S(2)}) %copy-start.3) | copy-done | bytes 110616
  13.2 0.9 copy-done.4
  14.1 0.7 copy-done.5
  14.9 0.9 copy-done.11
  15.8 0.8 copy-done.15
  16.6 0.0 copy-start.8
  16.6 0.0 copy-start.9
  16.7 0.0 copy-start.10
  16.7 0.0 copy-start.12
  16.7 0.0 copy-start.13
  16.7 0.0 copy-start.14
  16.7 0.0 copy-start.16
  16.7 6.2 %near_part.1 = (bf16[512,576]{1,0:T(8,128)(2,1)S(1)}, bf16[320,1440]{1,0:T(8,128)(2,1)S(1)}, bf16[128,1728]{1,0:T(8,128)(2,1)S(1)}, bf16[256,4608]{1,0:T(8,128)(...) custom-call(bf16[512,128]{1,0:T(8,128)(2,1)S(1)} %bitcast.18, ...), custom_call_target="tpu_custom_call" | custom-call | flops 3000000000 | bytes 8000000 | tf_op jit(solution)/shard_map/near_part/pallas_call | solution.py:541
  22.9 0.0 collective-permute-done.3.swap_core2
  22.9 0.0 collective-permute-done.2.swap_chip2
  22.9 0.0 copy-done
  22.9 0.0 copy-done.2
  22.9 0.0 copy-done.6
  22.9 0.0 copy-done.7
  23.0 0.0 copy-done.8
  23.0 0.0 copy-done.9
  23.0 0.0 copy-done.10
  23.0 0.0 copy-done.12
  23.0 0.0 copy-done.13
  23.0 0.0 copy-done.14
  23.0 0.0 copy-done.16
  23.0 15.3 %local_grads.1 = (bf16[1280,128]{1,0:T(8,128)(2,1)S(1)}, bf16[1280,128]{1,0:T(8,128)(2,1)S(1)}) custom-call(bf16[512,128]{1,0:T(8,128)(2,1)S(1)} %collective-permute-done.swap_core, bf16[512,128]{1,0:T(8,128)(2,1)S(1)} %collective-permute-done.1.swap_chip, bf16[480,128]{1,0:T(8,128)(2,1)S(1)} %collective-permute-done.2.swap_chip2, ...), custom_call_target="tpu_custom_call" | custom-call | flops 10000000000 | bytes 10000000 | tf_op jit(solution)/shard_map/local_grads/pallas_call | solution.py:560
  38.3 0.6 collective-permute-start.4
  38.9 1.3 %collective-permute-done.4 = bf16[1280,128]{1,0:T(8,128)(2,1)S(1)} collective-permute-done((bf16[1280,128]{1,0:T(8,128)(2,1)S(1)}, bf16[1280,128]{1,0:T(8,128)(2,1)S(1)}, u32[]{:S(2)}, u32[]{:S(2)}) %collective-permute-start.4) | collective-permute-done | bytes 327712 | tf_op jit(solution)/shard_map/ppermute | solution.py:618
  40.2 0.1 add_convert_fusion
  40.3 15.5 %all_to_all.15 = bf16[16,80,128]{2,1,0:T(8,128)(2,1)S(1)} all-to-all(bf16[16,80,128]{2,1,0:T(8,128)(2,1)S(1)} %bitcast.22), channel_id=1, replica_groups={{0,2,4,6,8,10,12,14,16,18,20,22,24,26,28,30},{1,3,5,7,9,11,13,15,17,19,..., dimensions={0} | all-to-all | bytes 655360 | tf_op jit(solution)/shard_map/all_to_all | solution.py:608
  55.7 0.1 reduce_sum.24
  55.8 16.3 %all_to_all.16 = bf16[8,80,128]{2,1,0:T(8,128)(2,1)S(1)} all-to-all(bf16[8,80,128]{2,1,0:T(8,128)(2,1)S(1)} %broadcast_in_dim.4), channel_id=1, replica_groups=mesh['sample'=8,'space'=32] {'sample'}, dimensions={0} | all-to-all | bytes 327680 | tf_op jit(solution)/shard_map/all_to_all | solution.py:602
  72.2 10.9 %all_to_all.17 = bf16[16,80,128]{2,1,0:T(8,128)(2,1)S(1)} all-to-all(bf16[16,80,128]{2,1,0:T(8,128)(2,1)S(1)} %broadcast_in_dim.5), channel_id=1, replica_groups={{0,2,4,6,8,10,12,14,16,18,20,22,24,26,28,30},{1,3,5,7,9,11,13,15,17,19,..., dimensions={0} | all-to-all | bytes 655360 | tf_op jit(solution)/shard_map/all_to_all | solution.py:608
  83.1 3.9 %collective-permute-start.5 = (bf16[1280,128]{1,0:T(8,128)(2,1)S(1)}, bf16[1280,128]{1,0:T(8,128)(2,1)S(1)}, u32[]{:S(2)}, u32[]{:S(2)}) collective-permute-start(bf16[1280,128]{1,0:T(8,128)(2,1)S(1)} %bitcast.20), channel_id=1, source_target_pairs={{0,1},{2,3},{4,5},{6,7},{8,9},{10,11},{12,13},{14,15},{16,17},{18,... | collective-permute-start | bytes 983048 | tf_op jit(solution)/shard_map/ppermute | solution.py:618
  87.0 1.3 %collective-permute-done.5.other = bf16[1280,128]{1,0:T(8,128)(2,1)S(1)} collective-permute-done((bf16[1280,128]{1,0:T(8,128)(2,1)S(1)}, bf16[1280,128]{1,0:T(8,128)(2,1)S(1)}, u32[]{:S(2)}, u32[]{:S(2)}) %collective-permute-start.5) | collective-permute-done | bytes 327712 | tf_op jit(solution)/shard_map/ppermute | solution.py:618
  88.3 0.7 copy-done.18
  89.0 2.3 %finish.1 = (f32[27,4,32]{2,1,0:T(4,128)}, f32[27,32,64]{2,1,0:T(8,128)}, f32[27,64,128]{2,1,0:T(8,128)}) custom-call(bf16[1280,128]{1,0:T(8,128)(2,1)} %bitcast.21, bf16[1280,128]{1,0:T(8,128)(2,1)} %copy-done.18), custom_call_target="tpu_custom_call" | custom-call | tf_op jit(solution)/shard_map/finish/pallas_call | solution.py:589
  (17 shorter events, 0.1 us)
Async XLA Ops:
  0.6 5.3 %collective-permute-start = (bf16[512,128]{1,0:T(8,128)(2,1)}, bf16[512,128]{1,0:T(8,128)(2,1)S(1)}, u32[]{:S(2)}, u32[]{:S(2)}) collective-permute-start(bf16[512,128]{1,0:T(8,128)(2,1)} %bitcast.16), channel_id=1, source_target_pairs={{0,1},{2,3},{4,5},{6,7},{8,9},{10,11},{12,13},{14,15},{16,17},{18,... | collective-permute-start | bytes 393224 | tf_op jit(solution)/shard_map/ppermute | solution.py:618
  4.0 6.5 %collective-permute-start.1 = (bf16[512,128]{1,0:T(8,128)(2,1)}, bf16[512,128]{1,0:T(8,128)(2,1)S(1)}, u32[]{:S(2)}, u32[]{:S(2)}) collective-permute-start(bf16[512,128]{1,0:T(8,128)(2,1)} %bitcast.17), channel_id=1, source_target_pairs={{1,2},{3,4},{5,6},{7,8},{9,10},{11,12},{13,14},{15,16},{17,18},{19... | collective-permute-start | bytes 393224 | tf_op jit(solution)/shard_map/ppermute | solution.py:618
  6.6 16.3 %collective-permute-start.2 = (bf16[480,128]{1,0:T(8,128)(2,1)S(1)}, bf16[480,128]{1,0:T(8,128)(2,1)S(1)}, u32[]{:S(2)}, u32[]{:S(2)}) collective-permute-start(bf16[480,128]{1,0:T(8,128)(2,1)S(1)} %pad_maximum_fusion.1), channel_id=1, source_target_pairs={{1,2},{3,4},{5,6},{7,8},{9,10},{11,12},{13,14},{15,16},{17,18},{19... | collective-permute-start | bytes 368648 | tf_op jit(solution)/shard_map/ppermute | solution.py:618
  11.2 11.7 %collective-permute-start.3 = (bf16[480,128]{1,0:T(8,128)(2,1)S(1)}, bf16[480,128]{1,0:T(8,128)(2,1)S(1)}, u32[]{:S(2)}, u32[]{:S(2)}) collective-permute-start(bf16[480,128]{1,0:T(8,128)(2,1)S(1)} %pad_maximum_fusion), channel_id=1, source_target_pairs={{0,1},{2,3},{4,5},{6,7},{8,9},{10,11},{12,13},{14,15},{16,17},{18,... | collective-permute-start | bytes 368648 | tf_op jit(solution)/shard_map/ppermute | solution.py:618
  11.3 1.0 %copy-start.1 = (bf16[3,3,3,64,128]{4,3,2,1,0:T(8,128)(2,1)S(1)}, bf16[3,3,3,64,128]{4,3,2,1,0:T(8,128)(2,1)}, u32[]{:S(2)}) copy-start(bf16[3,3,3,64,128]{4,3,2,1,0:T(8,128)(2,1)} %param.20) | copy-start | bytes 1327108
  12.3 0.9 %copy-start.3 = (bf16[3,3,3,32,64]{4,3,2,1,0:T(8,128)(2,1)S(1)}, bf16[3,3,3,32,64]{4,3,2,1,0:T(8,128)(2,1)}, u32[]{:S(2)}) copy-start(bf16[3,3,3,32,64]{4,3,2,1,0:T(8,128)(2,1)} %param.19) | copy-start | bytes 331780
  13.2 0.9 copy-start.4
  14.1 0.7 copy-start.5
  14.9 0.9 copy-start.11
  15.8 0.8 copy-start.15
  16.6 6.3 %copy-start = (bf16[1,1,2,16,128]{4,3,2,1,0:T(8,128)(2,1)S(1)}, bf16[1,1,2,16,128]{4,3,2,1,0:T(8,128)(2,1)}, u32[]{:S(2)}) copy-start(bf16[1,1,2,16,128]{4,3,2,1,0:T(8,128)(2,1)} %param.17) | copy-start | bytes 24580
  16.6 6.3 %copy-start.2 = (bf16[3,3,3,64,128]{4,3,2,1,0:T(8,128)(2,1)S(1)}, bf16[3,3,3,64,128]{4,3,2,1,0:T(8,128)(2,1)}, u32[]{:S(2)}) copy-start(bf16[3,3,3,64,128]{4,3,2,1,0:T(8,128)(2,1)} %param.20) | copy-start | bytes 1327108
  16.6 6.3 %copy-start.6 = (bf16[128,1152]{1,0:T(8,128)(2,1)S(1)}, bf16[128,1152]{1,0:T(8,128)(2,1)}, u32[]{:S(2)}) copy-start(bf16[128,1152]{1,0:T(8,128)(2,1)} %constant.53.clone.spread) | copy-start | bytes 884740
  16.6 6.3 %copy-start.7 = (bf16[256,512]{1,0:T(8,128)(2,1)S(1)}, bf16[256,512]{1,0:T(8,128)(2,1)}, u32[]{:S(2)}) copy-start(bf16[256,512]{1,0:T(8,128)(2,1)} %constant.56.clone.grow1) | copy-start | bytes 786436
  16.6 6.3 %copy-start.8 = (bf16[256,384]{1,0:T(8,128)(2,1)S(1)}, bf16[256,384]{1,0:T(8,128)(2,1)}, u32[]{:S(2)}) copy-start(bf16[256,384]{1,0:T(8,128)(2,1)} %constant.50.clone.odd) | copy-start | bytes 589828
  16.6 6.3 %copy-start.9 = (bf16[256,384]{1,0:T(8,128)(2,1)S(1)}, bf16[256,384]{1,0:T(8,128)(2,1)}, u32[]{:S(2)}) copy-start(bf16[256,384]{1,0:T(8,128)(2,1)} %constant.49.clone.pair) | copy-start | bytes 589828
  16.7 6.3 %copy-start.10 = (bf16[96,768]{1,0:T(8,128)(2,1)S(1)}, bf16[96,768]{1,0:T(8,128)(2,1)}, u32[]{:S(2)}) copy-start(bf16[96,768]{1,0:T(8,128)(2,1)} %constant.54.clone.grow_g) | copy-start | bytes 442372
  16.7 6.3 %copy-start.12 = (bf16[128,512]{1,0:T(8,128)(2,1)S(1)}, bf16[128,512]{1,0:T(8,128)(2,1)}, u32[]{:S(2)}) copy-start(bf16[128,512]{1,0:T(8,128)(2,1)} %constant.55.clone.grow2) | copy-start | bytes 393220
  16.7 6.3 %copy-start.13 = (bf16[512,128]{1,0:T(8,128)(2,1)S(1)}, bf16[512,128]{1,0:T(8,128)(2,1)}, u32[]{:S(2)}) copy-start(bf16[512,128]{1,0:T(8,128)(2,1)} %constant.52.clone.squeeze) | copy-start | bytes 393220
  16.7 6.3 %copy-start.14 = (bf16[128,384]{1,0:T(8,128)(2,1)S(1)}, bf16[128,384]{1,0:T(8,128)(2,1)}, u32[]{:S(2)}) copy-start(bf16[128,384]{1,0:T(8,128)(2,1)} %constant.51.clone.even) | copy-start | bytes 294916
  16.7 6.3 %copy-start.16 = (bf16[128,256]{1,0:T(8,128)(2,1)S(1)}, bf16[128,256]{1,0:T(8,128)(2,1)}, u32[]{:S(2)}) copy-start(bf16[128,256]{1,0:T(8,128)(2,1)} %constant.48.clone.shift) | copy-start | bytes 196612
  38.3 1.8 %collective-permute-start.4 = (bf16[1280,128]{1,0:T(8,128)(2,1)S(1)}, bf16[1280,128]{1,0:T(8,128)(2,1)S(1)}, u32[]{:S(2)}, u32[]{:S(2)}) collective-permute-start(bf16[1280,128]{1,0:T(8,128)(2,1)S(1)} %get-tuple-element.25), channel_id=1, source_target_pairs={{0,1},{2,3},{4,5},{6,7},{8,9},{10,11},{12,13},{14,15},{16,17},{18,... | collective-permute-start | bytes 983048 | tf_op jit(solution)/shard_map/ppermute | solution.py:618
  83.1 5.2 %copy-start.17 = (bf16[16,80,128]{2,1,0:T(8,128)(2,1)}, bf16[16,80,128]{2,1,0:T(8,128)(2,1)S(1)}, u32[]{:S(2)}) copy-start(bf16[16,80,128]{2,1,0:T(8,128)(2,1)S(1)} %all_to_all.17) | copy-start | bytes 983044
  83.1 5.2 %collective-permute-start.5 = (bf16[1280,128]{1,0:T(8,128)(2,1)S(1)}, bf16[1280,128]{1,0:T(8,128)(2,1)S(1)}, u32[]{:S(2)}, u32[]{:S(2)}) collective-permute-start(bf16[1280,128]{1,0:T(8,128)(2,1)S(1)} %bitcast.20), channel_id=1, source_target_pairs={{0,1},{2,3},{4,5},{6,7},{8,9},{10,11},{12,13},{14,15},{16,17},{18,... | collective-permute-start | bytes 983048 | tf_op jit(solution)/shard_map/ppermute | solution.py:618
  88.3 0.7 copy-start.18

commit v7 on v5

--- a/solution.py
+++ b/solution.py
@@ -1,3 +1,5 @@
+import functools
+
 import jax
 import jax.numpy as jnp
 import numpy as np
@@ -92,9 +94,7 @@
     return [kd * 9 + (2 - kh) * 3 + kw for kh in range(3)]
 
 
-def build(filter_two, t2, t2r, s2, s2r, sems):
-    copy2r = pltpu.make_async_copy(s2r, t2r, sems.at[0])
-    copy2 = pltpu.make_async_copy(s2, t2, sems.at[1])
+def build(filter_two, t2, t2r):
     for it in range(9):
         v2 = [filter_two[k].astype(F32) for k in taps_back(it)]
         zero = jnp.zeros((32, 64), F32)
@@ -107,8 +107,7 @@
             for m in range(4):
                 hp = 2 * m + 1 - s
                 if 0 <= hp < 8:
-                    s2r[32 * hp : 32 * hp + 32, it * 512 + 128 * m : it * 512 + 128 * m + 128] = tile
-    copy2r.start()
+                    t2r[32 * hp : 32 * hp + 32, it * 512 + 128 * m : it * 512 + 128 * m + 128] = tile
     taps = []
     for kh in range(3):
         rows = jnp.concatenate([filter_two[taps_of(it)[kh]] for it in range(9)], axis=0)
@@ -116,10 +115,7 @@
     zero = jnp.zeros((64, 288), F32)
     for s in range(5):
         parts = [taps[p - s + 1] if 0 <= p - s + 1 < 3 else zero for p in range(5)]
-        s2[64 * s : 64 * s + 64, :] = jnp.concatenate(parts, axis=1).astype(BF)
-    copy2.start()
-    copy2r.wait()
-    copy2.wait()
+        t2[64 * s : 64 * s + 64, :] = jnp.concatenate(parts, axis=1).astype(BF)
 
 
 def body(
@@ -131,8 +127,8 @@
     swap_core2,
     filter_one,
     filter_three,
-    t2_far,
-    t2r_far,
+    t2,
+    t2r,
     perm,
     shift,
     pair,
@@ -146,9 +142,7 @@
     kept,
     sent,
     t1,
-    t2,
     w3t,
-    t2r,
     x1,
     pp,
     x2,
@@ -160,17 +154,9 @@
     d2,
     d1,
     out,
-    sems,
 ):
     me, blocks = position()
     first_core = me % 2 == 0
-    copies = [
-        pltpu.make_async_copy(far_ref, near_ref, sems.at[i])
-        for i, (far_ref, near_ref) in enumerate(((t2_far, t2), (t2r_far, t2r)))
-    ]
-    for copy in copies:
-        copy.start()
-
     lane = lax.broadcasted_iota(jnp.int32, (32, 640), 1) % 16
     rows = filter_one[...].astype(F32).reshape(108, 32).astype(BF)
     base = lax.dot_general(rows, perm[...], TN, preferred_element_type=F32)
@@ -231,7 +217,6 @@
                         :, 128 * kw : 128 * kw + 128
                     ]
 
-    copies[0].wait()
     for c in range(4):
         lanes = slice(c * 256, c * 256 + 256)
         for g in range(2):
@@ -341,7 +326,6 @@
                         d2c[512 * k : 512 * k + 512, 128 * m : 128 * m + 128] = got[
                             :, 128 * kw : 128 * kw + 128
                         ]
-    copies[1].wait()
     back = dot(t2r[...], d2c[...]).astype(BF)
     back = dot(back, grow1[...])
     for h in range(16):
@@ -397,11 +381,11 @@
     sent[...] = out[pl.ds(half_rows - mine, half_rows), :]
 
 
-def finish(scales, mine, other, one, two, three):
+def finish(scales, mine, other, one_far, two_far, three_far, one, two, three, sems):
     first_core = position()[0] % 2 == 0
+    half_rows = mine.shape[0]
 
     def rows(at, count):
-        half_rows = mine.shape[0]
         parts = []
         while count:
             use = min(count, half_rows - at % half_rows)
@@ -411,15 +395,29 @@
             at, count = (at + use, count - use)
         return parts[0] if len(parts) == 1 else jnp.concatenate(parts, axis=0)
 
+    copies = []
+
+    def leave(near_ref, far_ref):
+        copies.append(pltpu.make_async_copy(near_ref, far_ref, sems.at[len(copies)]))
+        copies[-1].start()
+
     for k in range(27):
-        three[k] = rows(64 * k, 64) * scales[2]
         got = rows(G_TWO + 16 * k, 16) * scales[1]
         two[k, 0:16, :] = got[:, :64]
         two[k, 16:32, :] = got[:, 64:]
+    leave(two, two_far)
     got = rows(G_ONE, 48) * scales[0]
     for it in range(9):
         for kh, k in enumerate(taps_of(it)):
             one[k] = got[4 * it : 4 * it + 4, 32 * kh : 32 * kh + 32]
+    leave(one, one_far)
+    for third in range(3):
+        for k in range(9 * third, 9 * third + 9):
+            three[k] = rows(64 * k, 64) * scales[2]
+        here = slice(9 * third, 9 * third + 9)
+        leave(three.at[here], three_far.at[here])
+    for copy in copies:
+        copy.wait()
 
 
 VMEM = pl.BlockSpec(memory_space=pltpu.VMEM)
@@ -438,8 +436,7 @@
         build,
         out_shape=[jax.ShapeDtypeStruct(shape, BF) for shape in BANDED],
         in_specs=[VMEM],
-        out_specs=[FAR] * 2,
-        scratch_shapes=[near(*shape) for shape in BANDED] + [pltpu.SemaphoreType.DMA((2,))],
+        out_specs=[VMEM] * 2,
         compiler_params=pltpu.CompilerParams(vmem_limit_bytes=16 * 1024 * 1024),
         cost_estimate=pl.CostEstimate(flops=10**9, bytes_accessed=6 * 10**6, transcendentals=0),
         name="build",
@@ -449,17 +446,14 @@
 def local_grads(volume, grad, swaps, filter_one, filter_three, banded, rows):
     tables = [jnp.asarray(t, BF) for t in one_hot_tables()]
     args = [volume, grad, *swaps, filter_one, filter_three, *banded, *tables]
-    far = (8, 9)
     return pl.pallas_call(
         body,
         out_shape=[jax.ShapeDtypeStruct((rows // 2, 128), BF)] * 2,
-        in_specs=[FAR if i in far else VMEM for i in range(len(args))],
+        in_specs=[VMEM] * len(args),
         out_specs=[VMEM] * 2,
         scratch_shapes=[
             near(512, 576),
-            near(320, 1440),
             near(128, 1728),
-            near(256, 4608),
             near(192, 38 * 128),
             near(256, 18 * 128),
             near(2304, 1024),
@@ -471,7 +465,6 @@
             near(512, 512),
             near(512, 1024),
             near(rows, 128),
-            pltpu.SemaphoreType.DMA((2,)),
         ],
         compiler_params=pltpu.CompilerParams(vmem_limit_bytes=LIMIT * 1024 * 1024),
         cost_estimate=pl.CostEstimate(flops=10**10, bytes_accessed=10**7, transcendentals=0),
@@ -480,15 +473,18 @@
 
 
 def run_finish(mine, other, cells):
-    scales = 1.0 / jnp.sqrt(jnp.array([cells, cells / 8.0, cells / 64.0], F32))
+    scales = [float(1.0 / np.sqrt(cells / size)) for size in (1.0, 8.0, 64.0)]
     shapes = [(27, 4, 32), (27, 32, 64), (27, 64, 128)]
     outs = pl.pallas_call(
-        finish,
+        functools.partial(finish, scales),
         out_shape=[jax.ShapeDtypeStruct(shape, F32) for shape in shapes],
-        in_specs=[pl.BlockSpec(memory_space=pltpu.SMEM), VMEM, VMEM],
-        out_specs=[VMEM] * 3,
+        in_specs=[VMEM] * 2,
+        out_specs=[FAR] * 3,
+        scratch_shapes=[pltpu.VMEM(shape, F32) for shape in shapes]
+        + [pltpu.SemaphoreType.DMA((5,))],
+        compiler_params=pltpu.CompilerParams(vmem_limit_bytes=8 * 1024 * 1024),
         name="finish",
-    )(scales, mine, other)
+    )(mine, other)
     return tuple(o.reshape(3, 3, 3, *o.shape[1:]) for o in outs)
 
 

time: 82.8 us -> 79.7 us (0.963)
  Pallas kernels: 18.9 us -> 16 us
    pallas_call x1, Pallas kernels: 15.4 us -> 14.2 us  [local_grads(): pl.pallas_call(body, out_shape=[jax.ShapeDtypeStruct((rows // 2, 128), BF...]
    pallas_call x1, Pallas kernels: 2.29 us -> 1.25 us  [run_finish(): pl.pallas_call(functools.partial(finish, scales), out_shape=[jax.ShapeDty...]
    unnamed x34 -> x30, local copies, waits for them, and re-layouts: 1.74 us -> 1.01 us
where the time goes in v7:
time: 79.7 us; the launch traced here: 79.4 us
  blocking collectives  43.1 us (54%)
  Pallas kernels  16 us (20%)
  starting transfers between devices  13.1 us (16%)
  waiting for transfers between devices  4.07 us (5%)
  local copies, waits for them, and re-layouts  1.11 us (1%)
  between operations  1.09 us (1%)
  other arithmetic  0.89 us (1%)
    all_to_all x2, blocking collectives, over_chips(): lax.all_to_all(pieces, 'space', 0, 0, axis_index_groups=groups, tiled=True)  26.8 us
    all_to_all x1, blocking collectives, over_sample(): return lax.all_to_all(pieces, 'sample', 0, 0, tiled=True)  16.4 us
    pallas_call x1, Pallas kernels, local_grads(): pl.pallas_call(body, out_shape=[jax.ShapeDtypeStruct((rows // 2, 128), BF...  14.2 us
    ppermute x6, starting transfers between devices, swap(): return lax.ppermute(values, 'space', pairs + [(j, i) for i, j in pairs])  13.1 us
    ppermute x6, waiting for transfers between devices, swap(): return lax.ppermute(values, 'space', pairs + [(j, i) for i, j in pairs])  4.07 us
  transfers between devices with their start and end apart: 6, of which 4 were waited for; matrix products, arithmetic and copies ran while one was open for 1% of the time, Pallas kernels for 1%

profile of v7, /device:TPU:1, one launch (start us, length us, event | category | flops | bytes accessed | tf_op | source)
XLA Modules:
  0.0 79.4 jit_solution(6536647906125816488)
XLA Ops:
  0.6 0.0 copy-start
  0.6 0.0 copy-start.1
  0.7 0.0 copy-start.4
  0.7 3.3 %collective-permute-start = (bf16[512,128]{1,0:T(8,128)(2,1)}, bf16[512,128]{1,0:T(8,128)(2,1)S(1)}, u32[]{:S(2)}, u32[]{:S(2)}) collective-permute-start(bf16[512,128]{1,0:T(8,128)(2,1)} %bitcast.17), channel_id=1, source_target_pairs={{0,1},{2,3},{4,5},{6,7},{8,9},{10,11},{12,13},{14,15},{16,17},{18,... | collective-permute-start | bytes 393224 | tf_op jit(solution)/shard_map/ppermute | solution.py:508
  4.0 1.9 %collective-permute-start.1 = (bf16[512,128]{1,0:T(8,128)(2,1)}, bf16[512,128]{1,0:T(8,128)(2,1)S(1)}, u32[]{:S(2)}, u32[]{:S(2)}) collective-permute-start(bf16[512,128]{1,0:T(8,128)(2,1)} %bitcast.18), channel_id=1, source_target_pairs={{1,2},{3,4},{5,6},{7,8},{9,10},{11,12},{13,14},{15,16},{17,18},{19... | collective-permute-start | bytes 393224 | tf_op jit(solution)/shard_map/ppermute | solution.py:508
  5.9 0.0 collective-permute-done.swap_core
  6.0 0.7 pad_maximum_fusion.1
  6.7 3.6 %collective-permute-start.2 = (bf16[480,128]{1,0:T(8,128)(2,1)S(1)}, bf16[480,128]{1,0:T(8,128)(2,1)S(1)}, u32[]{:S(2)}, u32[]{:S(2)}) collective-permute-start(bf16[480,128]{1,0:T(8,128)(2,1)S(1)} %pad_maximum_fusion.1), channel_id=1, source_target_pairs={{1,2},{3,4},{5,6},{7,8},{9,10},{11,12},{13,14},{15,16},{17,18},{19... | collective-permute-start | bytes 368648 | tf_op jit(solution)/shard_map/ppermute | solution.py:508
  10.3 0.0 copy-start.2
  10.3 0.9 %copy-done.2 = bf16[3,3,3,32,64]{4,3,2,1,0:T(8,128)(2,1)S(1)} copy-done((bf16[3,3,3,32,64]{4,3,2,1,0:T(8,128)(2,1)S(1)}, bf16[3,3,3,32,64]{4,3,2,1,0:T(8,128)(2,1)}, u32[]{:S(2)}) %copy-start.2) | copy-done | bytes 110616
  11.3 0.0 copy-start.3
  11.3 0.0 copy-start.8
  11.3 0.0 copy-start.9
  11.3 0.0 copy-start.10
  11.3 0.0 copy-start.11
  11.3 0.0 copy-start.12
  11.3 0.0 copy-start.13
  11.3 0.0 copy-start.14
  11.4 0.5 build.1
  11.9 0.0 collective-permute-done.1.swap_chip
  11.9 0.0 copy-done
  12.0 0.1 collective-permute-start.3
  12.1 0.8 %collective-permute-done.2.swap_chip2 = bf16[480,128]{1,0:T(8,128)(2,1)S(1)} collective-permute-done((bf16[480,128]{1,0:T(8,128)(2,1)S(1)}, bf16[480,128]{1,0:T(8,128)(2,1)S(1)}, u32[]{:S(2)}, u32[]{:S(2)}) %collective-permute-start.2) | collective-permute-done | bytes 122912 | tf_op jit(solution)/shard_map/ppermute | solution.py:508
  12.9 0.5 collective-permute-done.3.swap_core2
  13.4 0.0 copy-done.1
  13.4 0.0 copy-done.4
  13.4 0.0 copy-done.3
  13.4 0.0 copy-done.5
  13.4 0.0 copy-done.6
  13.4 0.0 copy-done.7
  13.4 0.0 copy-done.8
  13.4 0.0 copy-done.9
  13.4 0.0 copy-done.10
  13.5 0.0 copy-done.11
  13.5 0.0 copy-done.12
  13.5 0.0 copy-done.13
  13.5 0.0 copy-done.14
  13.5 14.2 %local_grads.1 = (bf16[1280,128]{1,0:T(8,128)(2,1)S(1)}, bf16[1280,128]{1,0:T(8,128)(2,1)S(1)}) custom-call(bf16[512,128]{1,0:T(8,128)(2,1)S(1)} %bitcast.19, bf16[32,128]{1,0:T(8,128)(2,1)S(1)} %bitcast.14, bf16[512,128]{1,0:T(8,128)(2,1)S(1)} %collective-permute-done.swap_core, bf16[512,128]{1,0:T(8,128)(2,1)S(1)} %collective-permute-done.1.swap_chip, ...), custom_call_target="tpu_custom_call" | custom-call | flops 10000000000 | bytes 10000000 | tf_op jit(solution)/shard_map/local_grads/pallas_call | solution.py:449
  27.7 0.2 collective-permute-start.4
  27.9 1.5 %collective-permute-done.4 = bf16[1280,128]{1,0:T(8,128)(2,1)S(1)} collective-permute-done((bf16[1280,128]{1,0:T(8,128)(2,1)S(1)}, bf16[1280,128]{1,0:T(8,128)(2,1)S(1)}, u32[]{:S(2)}, u32[]{:S(2)}) %collective-permute-start.4) | collective-permute-done | bytes 327712 | tf_op jit(solution)/shard_map/ppermute | solution.py:508
  29.4 0.1 add_convert_fusion
  29.5 16.2 %all_to_all.15 = bf16[16,80,128]{2,1,0:T(8,128)(2,1)S(1)} all-to-all(bf16[16,80,128]{2,1,0:T(8,128)(2,1)S(1)} %bitcast.21), channel_id=1, replica_groups={{0,2,4,6,8,10,12,14,16,18,20,22,24,26,28,30},{1,3,5,7,9,11,13,15,17,19,..., dimensions={0} | all-to-all | bytes 655360 | tf_op jit(solution)/shard_map/all_to_all | solution.py:498
  45.7 0.1 reduce_sum.24
  45.8 16.4 %all_to_all.16 = bf16[8,80,128]{2,1,0:T(8,128)(2,1)S(1)} all-to-all(bf16[8,80,128]{2,1,0:T(8,128)(2,1)S(1)} %broadcast_in_dim.4), channel_id=1, replica_groups=mesh['sample'=8,'space'=32] {'sample'}, dimensions={0} | all-to-all | bytes 327680 | tf_op jit(solution)/shard_map/all_to_all | solution.py:492
  62.2 10.6 %all_to_all.17 = bf16[16,80,128]{2,1,0:T(8,128)(2,1)S(1)} all-to-all(bf16[16,80,128]{2,1,0:T(8,128)(2,1)S(1)} %broadcast_in_dim.5), channel_id=1, replica_groups={{0,2,4,6,8,10,12,14,16,18,20,22,24,26,28,30},{1,3,5,7,9,11,13,15,17,19,..., dimensions={0} | all-to-all | bytes 655360 | tf_op jit(solution)/shard_map/all_to_all | solution.py:498
  72.8 3.9 %collective-permute-start.5 = (bf16[1280,128]{1,0:T(8,128)(2,1)S(1)}, bf16[1280,128]{1,0:T(8,128)(2,1)S(1)}, u32[]{:S(2)}, u32[]{:S(2)}) collective-permute-start(bf16[1280,128]{1,0:T(8,128)(2,1)S(1)} %bitcast.10), channel_id=1, source_target_pairs={{0,1},{2,3},{4,5},{6,7},{8,9},{10,11},{12,13},{14,15},{16,17},{18,... | collective-permute-start | bytes 983048 | tf_op jit(solution)/shard_map/ppermute | solution.py:508
  76.7 1.3 %collective-permute-done.5.other = bf16[1280,128]{1,0:T(8,128)(2,1)S(1)} collective-permute-done((bf16[1280,128]{1,0:T(8,128)(2,1)S(1)}, bf16[1280,128]{1,0:T(8,128)(2,1)S(1)}, u32[]{:S(2)}, u32[]{:S(2)}) %collective-permute-start.5) | collective-permute-done | bytes 327712 | tf_op jit(solution)/shard_map/ppermute | solution.py:508
  78.0 1.3 %finish.1 = (f32[27,4,32]{2,1,0:T(4,128)}, f32[27,32,64]{2,1,0:T(8,128)}, f32[27,64,128]{2,1,0:T(8,128)}) custom-call(bf16[1280,128]{1,0:T(8,128)(2,1)S(1)} %bitcast.11, bf16[1280,128]{1,0:T(8,128)(2,1)S(1)} %collective-permute-done.5.other), custom_call_target="tpu_custom_call" | custom-call | tf_op jit(solution)/shard_map/finish/pallas_call | solution.py:478
  (9 shorter events, 0.1 us)
Async XLA Ops:
  0.6 11.3 %copy-start = (bf16[1,1,2,16,128]{4,3,2,1,0:T(8,128)(2,1)S(1)}, bf16[1,1,2,16,128]{4,3,2,1,0:T(8,128)(2,1)}, u32[]{:S(2)}) copy-start(bf16[1,1,2,16,128]{4,3,2,1,0:T(8,128)(2,1)} %param.16) | copy-start | bytes 24580
  0.6 12.7 %copy-start.1 = (bf16[3,3,3,64,128]{4,3,2,1,0:T(8,128)(2,1)S(1)}, bf16[3,3,3,64,128]{4,3,2,1,0:T(8,128)(2,1)}, u32[]{:S(2)}) copy-start(bf16[3,3,3,64,128]{4,3,2,1,0:T(8,128)(2,1)} %param.19) | copy-start | bytes 1327108
  0.7 12.7 %copy-start.4 = (bf16[3,3,3,4,32]{4,3,2,1,0:T(4,128)(2,1)S(1)}, bf16[3,3,3,4,32]{4,3,2,1,0:T(4,128)(2,1)}, u32[]{:S(2)}) copy-start(bf16[3,3,3,4,32]{4,3,2,1,0:T(4,128)(2,1)} %param.17) | copy-start | bytes 20740
  0.7 5.3 %collective-permute-start = (bf16[512,128]{1,0:T(8,128)(2,1)}, bf16[512,128]{1,0:T(8,128)(2,1)S(1)}, u32[]{:S(2)}, u32[]{:S(2)}) collective-permute-start(bf16[512,128]{1,0:T(8,128)(2,1)} %bitcast.17), channel_id=1, source_target_pairs={{0,1},{2,3},{4,5},{6,7},{8,9},{10,11},{12,13},{14,15},{16,17},{18,... | collective-permute-start | bytes 393224 | tf_op jit(solution)/shard_map/ppermute | solution.py:508
  4.0 7.9 %collective-permute-start.1 = (bf16[512,128]{1,0:T(8,128)(2,1)}, bf16[512,128]{1,0:T(8,128)(2,1)S(1)}, u32[]{:S(2)}, u32[]{:S(2)}) collective-permute-start(bf16[512,128]{1,0:T(8,128)(2,1)} %bitcast.18), channel_id=1, source_target_pairs={{1,2},{3,4},{5,6},{7,8},{9,10},{11,12},{13,14},{15,16},{17,18},{19... | collective-permute-start | bytes 393224 | tf_op jit(solution)/shard_map/ppermute | solution.py:508
  6.7 6.2 %collective-permute-start.2 = (bf16[480,128]{1,0:T(8,128)(2,1)S(1)}, bf16[480,128]{1,0:T(8,128)(2,1)S(1)}, u32[]{:S(2)}, u32[]{:S(2)}) collective-permute-start(bf16[480,128]{1,0:T(8,128)(2,1)S(1)} %pad_maximum_fusion.1), channel_id=1, source_target_pairs={{1,2},{3,4},{5,6},{7,8},{9,10},{11,12},{13,14},{15,16},{17,18},{19... | collective-permute-start | bytes 368648 | tf_op jit(solution)/shard_map/ppermute | solution.py:508
  10.3 0.9 %copy-start.2 = (bf16[3,3,3,32,64]{4,3,2,1,0:T(8,128)(2,1)S(1)}, bf16[3,3,3,32,64]{4,3,2,1,0:T(8,128)(2,1)}, u32[]{:S(2)}) copy-start(bf16[3,3,3,32,64]{4,3,2,1,0:T(8,128)(2,1)} %param.18) | copy-start | bytes 331780
  11.3 2.1 %copy-start.3 = (bf16[1,8,4,16,128]{4,3,2,1,0:T(8,128)(2,1)S(1)}, bf16[1,8,4,16,128]{4,3,2,1,0:T(8,128)(2,1)}, u32[]{:S(2)}) copy-start(bf16[1,8,4,16,128]{4,3,2,1,0:T(8,128)(2,1)} %param.15) | copy-start | bytes 393220
  11.3 2.1 %copy-start.5 = (bf16[128,1152]{1,0:T(8,128)(2,1)S(1)}, bf16[128,1152]{1,0:T(8,128)(2,1)}, u32[]{:S(2)}) copy-start(bf16[128,1152]{1,0:T(8,128)(2,1)} %constant.53.clone.spread) | copy-start | bytes 884740
  11.3 2.1 %copy-start.6 = (bf16[256,512]{1,0:T(8,128)(2,1)S(1)}, bf16[256,512]{1,0:T(8,128)(2,1)}, u32[]{:S(2)}) copy-start(bf16[256,512]{1,0:T(8,128)(2,1)} %constant.56.clone.grow1) | copy-start | bytes 786436
  11.3 2.2 %copy-start.7 = (bf16[256,384]{1,0:T(8,128)(2,1)S(1)}, bf16[256,384]{1,0:T(8,128)(2,1)}, u32[]{:S(2)}) copy-start(bf16[256,384]{1,0:T(8,128)(2,1)} %constant.50.clone.odd) | copy-start | bytes 589828
  11.3 2.2 %copy-start.8 = (bf16[256,384]{1,0:T(8,128)(2,1)S(1)}, bf16[256,384]{1,0:T(8,128)(2,1)}, u32[]{:S(2)}) copy-start(bf16[256,384]{1,0:T(8,128)(2,1)} %constant.49.clone.pair) | copy-start | bytes 589828
  11.3 2.2 %copy-start.9 = (bf16[96,768]{1,0:T(8,128)(2,1)S(1)}, bf16[96,768]{1,0:T(8,128)(2,1)}, u32[]{:S(2)}) copy-start(bf16[96,768]{1,0:T(8,128)(2,1)} %constant.54.clone.grow_g) | copy-start | bytes 442372
  11.3 2.2 %copy-start.10 = (bf16[108,640]{1,0:T(8,128)(2,1)S(1)}, bf16[108,640]{1,0:T(8,128)(2,1)}, u32[]{:S(2)}) copy-start(bf16[108,640]{1,0:T(8,128)(2,1)} %constant.47.clone.perm) | copy-start | bytes 414724
  11.3 2.1 %copy-start.11 = (bf16[128,512]{1,0:T(8,128)(2,1)S(1)}, bf16[128,512]{1,0:T(8,128)(2,1)}, u32[]{:S(2)}) copy-start(bf16[128,512]{1,0:T(8,128)(2,1)} %constant.55.clone.grow2) | copy-start | bytes 393220
  11.3 2.1 %copy-start.12 = (bf16[512,128]{1,0:T(8,128)(2,1)S(1)}, bf16[512,128]{1,0:T(8,128)(2,1)}, u32[]{:S(2)}) copy-start(bf16[512,128]{1,0:T(8,128)(2,1)} %constant.52.clone.squeeze) | copy-start | bytes 393220
  11.3 2.1 %copy-start.13 = (bf16[128,384]{1,0:T(8,128)(2,1)S(1)}, bf16[128,384]{1,0:T(8,128)(2,1)}, u32[]{:S(2)}) copy-start(bf16[128,384]{1,0:T(8,128)(2,1)} %constant.51.clone.even) | copy-start | bytes 294916
  11.3 2.1 %copy-start.14 = (bf16[128,256]{1,0:T(8,128)(2,1)S(1)}, bf16[128,256]{1,0:T(8,128)(2,1)}, u32[]{:S(2)}) copy-start(bf16[128,256]{1,0:T(8,128)(2,1)} %constant.48.clone.shift) | copy-start | bytes 196612
  12.0 1.4 %collective-permute-start.3 = (bf16[480,128]{1,0:T(8,128)(2,1)S(1)}, bf16[480,128]{1,0:T(8,128)(2,1)S(1)}, u32[]{:S(2)}, u32[]{:S(2)}) collective-permute-start(bf16[480,128]{1,0:T(8,128)(2,1)S(1)} %pad_maximum_fusion), channel_id=1, source_target_pairs={{0,1},{2,3},{4,5},{6,7},{8,9},{10,11},{12,13},{14,15},{16,17},{18,... | collective-permute-start | bytes 368648 | tf_op jit(solution)/shard_map/ppermute | solution.py:508
  27.7 1.7 %collective-permute-start.4 = (bf16[1280,128]{1,0:T(8,128)(2,1)S(1)}, bf16[1280,128]{1,0:T(8,128)(2,1)S(1)}, u32[]{:S(2)}, u32[]{:S(2)}) collective-permute-start(bf16[1280,128]{1,0:T(8,128)(2,1)S(1)} %get-tuple-element.21), channel_id=1, source_target_pairs={{0,1},{2,3},{4,5},{6,7},{8,9},{10,11},{12,13},{14,15},{16,17},{18,... | collective-permute-start | bytes 983048 | tf_op jit(solution)/shard_map/ppermute | solution.py:508
  72.8 5.2 %collective-permute-start.5 = (bf16[1280,128]{1,0:T(8,128)(2,1)S(1)}, bf16[1280,128]{1,0:T(8,128)(2,1)S(1)}, u32[]{:S(2)}, u32[]{:S(2)}) collective-permute-start(bf16[1280,128]{1,0:T(8,128)(2,1)S(1)} %bitcast.10), channel_id=1, source_target_pairs={{0,1},{2,3},{4,5},{6,7},{8,9},{10,11},{12,13},{14,15},{16,17},{18,... | collective-permute-start | bytes 983048 | tf_op jit(solution)/shard_map/ppermute | solution.py:508

commit v8 on v7

--- a/solution.py
+++ b/solution.py
@@ -10,7 +10,7 @@
 
 BF = jnp.bfloat16
 F32 = jnp.float32
-SLOT = 80
+SLOT = 72
 LIMIT = 44
 G_TWO = 1728
 G_ONE = 2160
@@ -36,17 +36,10 @@
             shift[w - 1, w] = 1.0
         if w + 1 < 128:
             shift[w + 1, 128 + w] = 1.0
-    pair = table(256, 384)
-    odd = table(256, 384)
-    even = table(128, 384)
+    pair = table(256, 128)
     for a in range(2):
-        for kw in range(3):
-            for w in range(64):
-                src = w + kw - 1
-                if 0 <= src < 64:
-                    pair[128 * a + 2 * src, 128 * kw + 64 * a + w] = 1.0
-                    odd[64 + 64 * a + src, 128 * kw + 64 * a + w] = 1.0
-                    even[64 * a + src, 128 * kw + 64 * a + w] = 1.0
+        for w in range(64):
+            pair[128 * a + 2 * w, 64 * a + w] = 1.0
     squeeze = table(512, 128)
     spread = table(128, 1152)
     grow_g = table(96, 768)
@@ -69,7 +62,7 @@
     for e in range(4):
         for w in range(128):
             grow1[64 * e + w // 2, 128 * e + w] = 1.0 / 16
-    return [perm, shift, pair, odd, even, squeeze, spread, grow_g, grow2, grow1]
+    return [perm, shift, pair, squeeze, spread, grow_g, grow2, grow1]
 
 
 def dot(a, b):
@@ -132,8 +125,6 @@
     perm,
     shift,
     pair,
-    odd,
-    even,
     squeeze,
     spread,
     grow_g,
@@ -206,16 +197,21 @@
         scale = jnp.where(inside(4 * me - 7 + j, 4 * blocks), 0.125, 0.0)
         pp[:, j * 128 : j * 128 + 128] = (act * scale).astype(BF)
 
+    col64 = lax.broadcasted_iota(jnp.int32, (256, 128), 1) % 64
+    first_col, last_col = (col64 == 0, col64 == 63)
     for first in range(17):
-        got = dot(pp[:, first * 128 : first * 128 + 256], pair[...]).astype(BF)
+        got = dot(pp[:, first * 128 : first * 128 + 256], pair[...])
+        moved = (
+            jnp.where(first_col, 0.0, pltpu.roll(got, 1, 1)).astype(BF),
+            got.astype(BF),
+            jnp.where(last_col, 0.0, pltpu.roll(got, 127, 1)).astype(BF),
+        )
         for kd in range(3):
             m = (first - kd) // 2
             if (first - kd) % 2 == 0 and 0 <= m < 8:
                 for kw in range(3):
                     k = 3 * kd + kw
-                    x2[256 * k : 256 * k + 256, m * 128 : m * 128 + 128] = got[
-                        :, 128 * kw : 128 * kw + 128
-                    ]
+                    x2[256 * k : 256 * k + 256, m * 128 : m * 128 + 128] = moved[kw]
 
     for c in range(4):
         lanes = slice(c * 256, c * 256 + 256)
@@ -311,21 +307,26 @@
             source = back[64 * n : 64 * n + 64, 128 * (h // 2) : 128 * (h // 2) + 128]
             d2[rows, lanes] = (source * sl2[rows, lanes].astype(F32)).astype(BF)
 
-    for start in range(1, 6):
-        u = start // 2
-        if start % 2:
-            got = dot(d2[:, 128 * u : 128 * u + 256], odd[...])
-        else:
-            got = dot(d2[:, 128 * u : 128 * u + 128], even[...])
-        got = got.astype(BF)
-        for kd in range(3):
-            for m in range(2):
-                if 1 + kd + 2 * m == start:
-                    for kw in range(3):
-                        k = 3 * kd + kw
-                        d2c[512 * k : 512 * k + 512, 128 * m : 128 * m + 128] = got[
-                            :, 128 * kw : 128 * kw + 128
-                        ]
+    for part in range(2):
+        rows = slice(256 * part, 256 * part + 256)
+        for start in range(1, 6):
+            u = start // 2
+            got = d2[rows, 128 * u : 128 * u + 128].astype(F32)
+            if start % 2:
+                after = d2[rows, 128 * u + 128 : 128 * u + 256].astype(F32)
+                lane = lax.broadcasted_iota(jnp.int32, (256, 128), 1)
+                got = jnp.where(lane < 64, pltpu.roll(got, 64, 1), pltpu.roll(after, 64, 1))
+            moved = (
+                jnp.where(first_col, 0.0, pltpu.roll(got, 1, 1)).astype(BF),
+                got.astype(BF),
+                jnp.where(last_col, 0.0, pltpu.roll(got, 127, 1)).astype(BF),
+            )
+            for kd in range(3):
+                for m in range(2):
+                    if 1 + kd + 2 * m == start:
+                        for kw in range(3):
+                            lo = 512 * (3 * kd + kw) + 256 * part
+                            d2c[lo : lo + 256, 128 * m : 128 * m + 128] = moved[kw]
     back = dot(t2r[...], d2c[...]).astype(BF)
     back = dot(back, grow1[...])
     for h in range(16):

time: 79.7 us -> 77.8 us (0.976)
  Pallas kernels: 16 us -> 15.1 us
    pallas_call x1, Pallas kernels: 14.2 us -> 13.3 us  [local_grads(): pl.pallas_call(body, out_shape=[jax.ShapeDtypeStruct((rows // 2, 128), BF...]
where the time goes in v8:
time: 77.8 us; the launch traced here: 77.5 us
  blocking collectives  42.6 us (55%)
  Pallas kernels  15.1 us (19%)
  starting transfers between devices  13 us (17%)
  waiting for transfers between devices  3.99 us (5%)
  local copies, waits for them, and re-layouts  1.09 us (1%)
  between operations  0.9 us (1%)
  other arithmetic  0.87 us (1%)
    all_to_all x2, blocking collectives, over_chips(): lax.all_to_all(pieces, 'space', 0, 0, axis_index_groups=groups, tiled=True)  26.4 us
    all_to_all x1, blocking collectives, over_sample(): return lax.all_to_all(pieces, 'sample', 0, 0, tiled=True)  16.2 us
    pallas_call x1, Pallas kernels, local_grads(): pl.pallas_call(body, out_shape=[jax.ShapeDtypeStruct((rows // 2, 128), BF...  13.3 us
    ppermute x6, starting transfers between devices, swap(): return lax.ppermute(values, 'space', pairs + [(j, i) for i, j in pairs])  13 us
    ppermute x6, waiting for transfers between devices, swap(): return lax.ppermute(values, 'space', pairs + [(j, i) for i, j in pairs])  3.99 us
  transfers between devices with their start and end apart: 6, of which 4 were waited for; matrix products, arithmetic and copies ran while one was open for 1% of the time, Pallas kernels for 1%

profile of v8, /device:TPU:1, one launch (start us, length us, event | category | flops | bytes accessed | tf_op | source)
XLA Modules:
  0.0 77.5 jit_solution(552089146710096225)
XLA Ops:
  0.6 0.0 copy-start
  0.6 0.0 copy-start.1
  0.7 0.0 copy-start.4
  0.7 3.3 %collective-permute-start = (bf16[512,128]{1,0:T(8,128)(2,1)}, bf16[512,128]{1,0:T(8,128)(2,1)S(1)}, u32[]{:S(2)}, u32[]{:S(2)}) collective-permute-start(bf16[512,128]{1,0:T(8,128)(2,1)} %bitcast.17), channel_id=1, source_target_pairs={{0,1},{2,3},{4,5},{6,7},{8,9},{10,11},{12,13},{14,15},{16,17},{18,... | collective-permute-start | bytes 393224 | tf_op jit(solution)/shard_map/ppermute | solution.py:509
  4.0 1.9 %collective-permute-start.1 = (bf16[512,128]{1,0:T(8,128)(2,1)}, bf16[512,128]{1,0:T(8,128)(2,1)S(1)}, u32[]{:S(2)}, u32[]{:S(2)}) collective-permute-start(bf16[512,128]{1,0:T(8,128)(2,1)} %bitcast.18), channel_id=1, source_target_pairs={{1,2},{3,4},{5,6},{7,8},{9,10},{11,12},{13,14},{15,16},{17,18},{19... | collective-permute-start | bytes 393224 | tf_op jit(solution)/shard_map/ppermute | solution.py:509
  5.9 0.0 collective-permute-done.swap_core
  6.0 0.7 pad_maximum_fusion.1
  6.7 3.6 %collective-permute-start.2 = (bf16[480,128]{1,0:T(8,128)(2,1)S(1)}, bf16[480,128]{1,0:T(8,128)(2,1)S(1)}, u32[]{:S(2)}, u32[]{:S(2)}) collective-permute-start(bf16[480,128]{1,0:T(8,128)(2,1)S(1)} %pad_maximum_fusion.1), channel_id=1, source_target_pairs={{1,2},{3,4},{5,6},{7,8},{9,10},{11,12},{13,14},{15,16},{17,18},{19... | collective-permute-start | bytes 368648 | tf_op jit(solution)/shard_map/ppermute | solution.py:509
  10.3 0.0 copy-start.2
  10.3 0.9 %copy-done.2 = bf16[3,3,3,32,64]{4,3,2,1,0:T(8,128)(2,1)S(1)} copy-done((bf16[3,3,3,32,64]{4,3,2,1,0:T(8,128)(2,1)S(1)}, bf16[3,3,3,32,64]{4,3,2,1,0:T(8,128)(2,1)}, u32[]{:S(2)}) %copy-start.2) | copy-done | bytes 110616
  11.3 0.0 copy-start.3
  11.3 0.0 copy-start.5
  11.3 0.0 copy-start.6
  11.3 0.0 copy-start.7
  11.3 0.0 copy-start.8
  11.3 0.0 copy-start.9
  11.3 0.0 copy-start.10
  11.3 0.0 copy-start.11
  11.3 0.0 copy-start.12
  11.3 0.5 build.1
  11.9 0.0 collective-permute-done.1.swap_chip
  11.9 0.0 copy-done
  11.9 0.1 collective-permute-start.3
  12.0 0.8 %collective-permute-done.2.swap_chip2 = bf16[480,128]{1,0:T(8,128)(2,1)S(1)} collective-permute-done((bf16[480,128]{1,0:T(8,128)(2,1)S(1)}, bf16[480,128]{1,0:T(8,128)(2,1)S(1)}, u32[]{:S(2)}, u32[]{:S(2)}) %collective-permute-start.2) | collective-permute-done | bytes 122912 | tf_op jit(solution)/shard_map/ppermute | solution.py:509
  12.9 0.5 collective-permute-done.3.swap_core2
  13.4 0.0 copy-done.1
  13.4 0.0 copy-done.4
  13.4 0.0 copy-done.3
  13.4 0.0 copy-done.5
  13.4 0.0 copy-done.6
  13.4 0.0 copy-done.7
  13.4 0.0 copy-done.8
  13.4 0.0 copy-done.9
  13.4 0.0 copy-done.10
  13.4 0.0 copy-done.11
  13.4 0.0 copy-done.12
  13.4 13.3 %local_grads.1 = (bf16[1152,128]{1,0:T(8,128)(2,1)S(1)}, bf16[1152,128]{1,0:T(8,128)(2,1)S(1)}) custom-call(bf16[512,128]{1,0:T(8,128)(2,1)S(1)} %bitcast.19, bf16[32,128]{1,0:T(8,128)(2,1)S(1)} %bitcast.14, bf16[512,128]{1,0:T(8,128)(2,1)S(1)} %collective-permute-done.swap_core, bf16[512,128]{1,0:T(8,128)(2,1)S(1)} %collective-permute-done.1.swap_chip, ...), custom_call_target="tpu_custom_call" | custom-call | flops 10000000000 | bytes 10000000 | tf_op jit(solution)/shard_map/local_grads/pallas_call | solution.py:450
  26.7 0.2 collective-permute-start.4
  27.0 1.5 %collective-permute-done.4 = bf16[1152,128]{1,0:T(8,128)(2,1)S(1)} collective-permute-done((bf16[1152,128]{1,0:T(8,128)(2,1)S(1)}, bf16[1152,128]{1,0:T(8,128)(2,1)S(1)}, u32[]{:S(2)}, u32[]{:S(2)}) %collective-permute-start.4) | collective-permute-done | bytes 294944 | tf_op jit(solution)/shard_map/ppermute | solution.py:509
  28.4 0.1 add_convert_fusion
  28.5 15.8 %all_to_all.15 = bf16[16,72,128]{2,1,0:T(8,128)(2,1)S(1)} all-to-all(bf16[16,72,128]{2,1,0:T(8,128)(2,1)S(1)} %bitcast.21), channel_id=1, replica_groups={{0,2,4,6,8,10,12,14,16,18,20,22,24,26,28,30},{1,3,5,7,9,11,13,15,17,19,..., dimensions={0} | all-to-all | bytes 589824 | tf_op jit(solution)/shard_map/all_to_all | solution.py:499
  44.4 16.2 %all_to_all.16 = bf16[8,72,128]{2,1,0:T(8,128)(2,1)S(1)} all-to-all(bf16[8,72,128]{2,1,0:T(8,128)(2,1)S(1)} %broadcast_in_dim.4), channel_id=1, replica_groups=mesh['sample'=8,'space'=32] {'sample'}, dimensions={0} | all-to-all | bytes 294912 | tf_op jit(solution)/shard_map/all_to_all | solution.py:493
  60.7 10.5 %all_to_all.17 = bf16[16,72,128]{2,1,0:T(8,128)(2,1)S(1)} all-to-all(bf16[16,72,128]{2,1,0:T(8,128)(2,1)S(1)} %broadcast_in_dim.5), channel_id=1, replica_groups={{0,2,4,6,8,10,12,14,16,18,20,22,24,26,28,30},{1,3,5,7,9,11,13,15,17,19,..., dimensions={0} | all-to-all | bytes 589824 | tf_op jit(solution)/shard_map/all_to_all | solution.py:499
  71.2 3.8 %collective-permute-start.5 = (bf16[1152,128]{1,0:T(8,128)(2,1)S(1)}, bf16[1152,128]{1,0:T(8,128)(2,1)S(1)}, u32[]{:S(2)}, u32[]{:S(2)}) collective-permute-start(bf16[1152,128]{1,0:T(8,128)(2,1)S(1)} %bitcast.10), channel_id=1, source_target_pairs={{0,1},{2,3},{4,5},{6,7},{8,9},{10,11},{12,13},{14,15},{16,17},{18,... | collective-permute-start | bytes 884744 | tf_op jit(solution)/shard_map/ppermute | solution.py:509
  75.0 1.2 %collective-permute-done.5.other = bf16[1152,128]{1,0:T(8,128)(2,1)S(1)} collective-permute-done((bf16[1152,128]{1,0:T(8,128)(2,1)S(1)}, bf16[1152,128]{1,0:T(8,128)(2,1)S(1)}, u32[]{:S(2)}, u32[]{:S(2)}) %collective-permute-start.5) | collective-permute-done | bytes 294944 | tf_op jit(solution)/shard_map/ppermute | solution.py:509
  76.2 1.3 %finish.1 = (f32[27,4,32]{2,1,0:T(4,128)}, f32[27,32,64]{2,1,0:T(8,128)}, f32[27,64,128]{2,1,0:T(8,128)}) custom-call(bf16[1152,128]{1,0:T(8,128)(2,1)S(1)} %bitcast.11, bf16[1152,128]{1,0:T(8,128)(2,1)S(1)} %collective-permute-done.5.other), custom_call_target="tpu_custom_call" | custom-call | tf_op jit(solution)/shard_map/finish/pallas_call | solution.py:479
  (7 shorter events, 0.2 us)
Async XLA Ops:
  0.6 11.3 %copy-start = (bf16[1,1,2,16,128]{4,3,2,1,0:T(8,128)(2,1)S(1)}, bf16[1,1,2,16,128]{4,3,2,1,0:T(8,128)(2,1)}, u32[]{:S(2)}) copy-start(bf16[1,1,2,16,128]{4,3,2,1,0:T(8,128)(2,1)} %param.14) | copy-start | bytes 24580
  0.6 12.7 %copy-start.1 = (bf16[3,3,3,64,128]{4,3,2,1,0:T(8,128)(2,1)S(1)}, bf16[3,3,3,64,128]{4,3,2,1,0:T(8,128)(2,1)}, u32[]{:S(2)}) copy-start(bf16[3,3,3,64,128]{4,3,2,1,0:T(8,128)(2,1)} %param.17) | copy-start | bytes 1327108
  0.7 12.7 %copy-start.4 = (bf16[3,3,3,4,32]{4,3,2,1,0:T(4,128)(2,1)S(1)}, bf16[3,3,3,4,32]{4,3,2,1,0:T(4,128)(2,1)}, u32[]{:S(2)}) copy-start(bf16[3,3,3,4,32]{4,3,2,1,0:T(4,128)(2,1)} %param.15) | copy-start | bytes 20740
  0.7 5.3 %collective-permute-start = (bf16[512,128]{1,0:T(8,128)(2,1)}, bf16[512,128]{1,0:T(8,128)(2,1)S(1)}, u32[]{:S(2)}, u32[]{:S(2)}) collective-permute-start(bf16[512,128]{1,0:T(8,128)(2,1)} %bitcast.17), channel_id=1, source_target_pairs={{0,1},{2,3},{4,5},{6,7},{8,9},{10,11},{12,13},{14,15},{16,17},{18,... | collective-permute-start | bytes 393224 | tf_op jit(solution)/shard_map/ppermute | solution.py:509
  4.0 7.9 %collective-permute-start.1 = (bf16[512,128]{1,0:T(8,128)(2,1)}, bf16[512,128]{1,0:T(8,128)(2,1)S(1)}, u32[]{:S(2)}, u32[]{:S(2)}) collective-permute-start(bf16[512,128]{1,0:T(8,128)(2,1)} %bitcast.18), channel_id=1, source_target_pairs={{1,2},{3,4},{5,6},{7,8},{9,10},{11,12},{13,14},{15,16},{17,18},{19... | collective-permute-start | bytes 393224 | tf_op jit(solution)/shard_map/ppermute | solution.py:509
  6.7 6.2 %collective-permute-start.2 = (bf16[480,128]{1,0:T(8,128)(2,1)S(1)}, bf16[480,128]{1,0:T(8,128)(2,1)S(1)}, u32[]{:S(2)}, u32[]{:S(2)}) collective-permute-start(bf16[480,128]{1,0:T(8,128)(2,1)S(1)} %pad_maximum_fusion.1), channel_id=1, source_target_pairs={{1,2},{3,4},{5,6},{7,8},{9,10},{11,12},{13,14},{15,16},{17,18},{19... | collective-permute-start | bytes 368648 | tf_op jit(solution)/shard_map/ppermute | solution.py:509
  10.3 0.9 %copy-start.2 = (bf16[3,3,3,32,64]{4,3,2,1,0:T(8,128)(2,1)S(1)}, bf16[3,3,3,32,64]{4,3,2,1,0:T(8,128)(2,1)}, u32[]{:S(2)}) copy-start(bf16[3,3,3,32,64]{4,3,2,1,0:T(8,128)(2,1)} %param.16) | copy-start | bytes 331780
  11.3 2.1 %copy-start.3 = (bf16[1,8,4,16,128]{4,3,2,1,0:T(8,128)(2,1)S(1)}, bf16[1,8,4,16,128]{4,3,2,1,0:T(8,128)(2,1)}, u32[]{:S(2)}) copy-start(bf16[1,8,4,16,128]{4,3,2,1,0:T(8,128)(2,1)} %param.13) | copy-start | bytes 393220
  11.3 2.1 %copy-start.5 = (bf16[128,1152]{1,0:T(8,128)(2,1)S(1)}, bf16[128,1152]{1,0:T(8,128)(2,1)}, u32[]{:S(2)}) copy-start(bf16[128,1152]{1,0:T(8,128)(2,1)} %constant.47.clone.spread) | copy-start | bytes 884740
  11.3 2.1 %copy-start.6 = (bf16[256,512]{1,0:T(8,128)(2,1)S(1)}, bf16[256,512]{1,0:T(8,128)(2,1)}, u32[]{:S(2)}) copy-start(bf16[256,512]{1,0:T(8,128)(2,1)} %constant.50.clone.grow1) | copy-start | bytes 786436
  11.3 2.1 %copy-start.7 = (bf16[96,768]{1,0:T(8,128)(2,1)S(1)}, bf16[96,768]{1,0:T(8,128)(2,1)}, u32[]{:S(2)}) copy-start(bf16[96,768]{1,0:T(8,128)(2,1)} %constant.48.clone.grow_g) | copy-start | bytes 442372
  11.3 2.1 %copy-start.8 = (bf16[108,640]{1,0:T(8,128)(2,1)S(1)}, bf16[108,640]{1,0:T(8,128)(2,1)}, u32[]{:S(2)}) copy-start(bf16[108,640]{1,0:T(8,128)(2,1)} %constant.43.clone.perm) | copy-start | bytes 414724
  11.3 2.1 %copy-start.9 = (bf16[128,512]{1,0:T(8,128)(2,1)S(1)}, bf16[128,512]{1,0:T(8,128)(2,1)}, u32[]{:S(2)}) copy-start(bf16[128,512]{1,0:T(8,128)(2,1)} %constant.49.clone.grow2) | copy-start | bytes 393220
  11.3 2.1 %copy-start.10 = (bf16[512,128]{1,0:T(8,128)(2,1)S(1)}, bf16[512,128]{1,0:T(8,128)(2,1)}, u32[]{:S(2)}) copy-start(bf16[512,128]{1,0:T(8,128)(2,1)} %constant.46.clone.squeeze) | copy-start | bytes 393220
  11.3 2.1 %copy-start.11 = (bf16[256,128]{1,0:T(8,128)(2,1)S(1)}, bf16[256,128]{1,0:T(8,128)(2,1)}, u32[]{:S(2)}) copy-start(bf16[256,128]{1,0:T(8,128)(2,1)} %constant.45.clone.pair) | copy-start | bytes 196612
  11.3 2.1 %copy-start.12 = (bf16[128,256]{1,0:T(8,128)(2,1)S(1)}, bf16[128,256]{1,0:T(8,128)(2,1)}, u32[]{:S(2)}) copy-start(bf16[128,256]{1,0:T(8,128)(2,1)} %constant.44.clone.shift) | copy-start | bytes 196612
  11.9 1.4 %collective-permute-start.3 = (bf16[480,128]{1,0:T(8,128)(2,1)S(1)}, bf16[480,128]{1,0:T(8,128)(2,1)S(1)}, u32[]{:S(2)}, u32[]{:S(2)}) collective-permute-start(bf16[480,128]{1,0:T(8,128)(2,1)S(1)} %pad_maximum_fusion), channel_id=1, source_target_pairs={{0,1},{2,3},{4,5},{6,7},{8,9},{10,11},{12,13},{14,15},{16,17},{18,... | collective-permute-start | bytes 368648 | tf_op jit(solution)/shard_map/ppermute | solution.py:509
  26.7 1.7 %collective-permute-start.4 = (bf16[1152,128]{1,0:T(8,128)(2,1)S(1)}, bf16[1152,128]{1,0:T(8,128)(2,1)S(1)}, u32[]{:S(2)}, u32[]{:S(2)}) collective-permute-start(bf16[1152,128]{1,0:T(8,128)(2,1)S(1)} %get-tuple-element.21), channel_id=1, source_target_pairs={{0,1},{2,3},{4,5},{6,7},{8,9},{10,11},{12,13},{14,15},{16,17},{18,... | collective-permute-start | bytes 884744 | tf_op jit(solution)/shard_map/ppermute | solution.py:509
  71.2 5.0 %collective-permute-start.5 = (bf16[1152,128]{1,0:T(8,128)(2,1)S(1)}, bf16[1152,128]{1,0:T(8,128)(2,1)S(1)}, u32[]{:S(2)}, u32[]{:S(2)}) collective-permute-start(bf16[1152,128]{1,0:T(8,128)(2,1)S(1)} %bitcast.10), channel_id=1, source_target_pairs={{0,1},{2,3},{4,5},{6,7},{8,9},{10,11},{12,13},{14,15},{16,17},{18,... | collective-permute-start | bytes 884744 | tf_op jit(solution)/shard_map/ppermute | solution.py:509

commit v9 on v8

--- a/solution.py
+++ b/solution.py
@@ -23,19 +23,6 @@
 
 
 def one_hot_tables():
-    perm = table(108, 640)
-    for kd in range(3):
-        for kh in range(3):
-            for kw in range(3):
-                for c in range(4):
-                    row = ((kd * 3 + kh) * 3 + kw) * 4 + c
-                    perm[row, ((kd * 3 + kw) * 4 + c) * 16 + kh] = 0.5
-    shift = table(128, 256)
-    for w in range(128):
-        if w >= 1:
-            shift[w - 1, w] = 1.0
-        if w + 1 < 128:
-            shift[w + 1, 128 + w] = 1.0
     pair = table(256, 128)
     for a in range(2):
         for w in range(64):
@@ -62,7 +49,7 @@
     for e in range(4):
         for w in range(128):
             grow1[64 * e + w // 2, 128 * e + w] = 1.0 / 16
-    return [perm, shift, pair, squeeze, spread, grow_g, grow2, grow1]
+    return [pair, squeeze, spread, grow_g, grow2, grow1]
 
 
 def dot(a, b):
@@ -87,7 +74,41 @@
     return [kd * 9 + (2 - kh) * 3 + kw for kh in range(3)]
 
 
-def build(filter_two, t2, t2r):
+def band_one(filter_one, t1):
+    lane = lax.broadcasted_iota(jnp.int32, (32, 640), 1) % 16
+    rows = filter_one[...].astype(F32).reshape(108, 32).astype(BF)
+    at = lax.broadcasted_iota(jnp.int32, (108, 640), 1)
+    kd = (at >= 192).astype(jnp.int32) + (at >= 384).astype(jnp.int32)
+    rest = at - 192 * kd
+    kw = (rest >= 64).astype(jnp.int32) + (rest >= 128).astype(jnp.int32)
+    c = (rest - 64 * kw) // 16
+    kh = rest % 16
+    place = 36 * kd + 12 * kh + 4 * kw + c
+    here = lax.broadcasted_iota(jnp.int32, (108, 640), 0) == place
+    here = jnp.logical_and(here, jnp.logical_and(kh < 3, at < 576))
+    perm = jnp.where(here, 0.5, 0.0).astype(BF)
+    base = lax.dot_general(rows, perm, TN, preferred_element_type=F32)
+    for h in range(16):
+        moved = pltpu.roll(base, (h - 1) % 640, 1) if h != 1 else base
+        if h == 0:
+            moved = jnp.where(lane == 15, 0.0, moved)
+        if h == 15:
+            moved = jnp.where(lane == 0, 0.0, moved)
+        t1[32 * h : 32 * h + 32, :] = moved[:, :576].astype(BF)
+
+
+def band_two(filter_two, t2):
+    taps = []
+    for kh in range(3):
+        rows = jnp.concatenate([filter_two[taps_of(it)[kh]] for it in range(9)], axis=0)
+        taps.append(rows.astype(F32).T * 0.5)
+    zero = jnp.zeros((64, 288), F32)
+    for s in range(5):
+        parts = [taps[p - s + 1] if 0 <= p - s + 1 < 3 else zero for p in range(5)]
+        t2[64 * s : 64 * s + 64, :] = jnp.concatenate(parts, axis=1).astype(BF)
+
+
+def band_two_back(filter_two, t2r):
     for it in range(9):
         v2 = [filter_two[k].astype(F32) for k in taps_back(it)]
         zero = jnp.zeros((32, 64), F32)
@@ -101,29 +122,86 @@
                 hp = 2 * m + 1 - s
                 if 0 <= hp < 8:
                     t2r[32 * hp : 32 * hp + 32, it * 512 + 128 * m : it * 512 + 128 * m + 128] = tile
-    taps = []
-    for kh in range(3):
-        rows = jnp.concatenate([filter_two[taps_of(it)[kh]] for it in range(9)], axis=0)
-        taps.append(rows.astype(F32).T * 0.5)
-    zero = jnp.zeros((64, 288), F32)
-    for s in range(5):
-        parts = [taps[p - s + 1] if 0 <= p - s + 1 < 3 else zero for p in range(5)]
-        t2[64 * s : 64 * s + 64, :] = jnp.concatenate(parts, axis=1).astype(BF)
+
+
+def with_column_shifts(rows, x1, at):
+    lane = lax.broadcasted_iota(jnp.int32, (64, 128), 1)
+    for p in range(rows.shape[0] // 64):
+        lanes = slice(128 * (at + p), 128 * (at + p) + 128)
+        plane = rows[64 * p : 64 * p + 64, :]
+        wide = plane.astype(F32)
+        x1[0:64, lanes] = jnp.where(lane == 0, 0.0, pltpu.roll(wide, 1, 1)).astype(BF)
+        x1[64:128, lanes] = plane
+        x1[128:192, lanes] = jnp.where(lane == 127, 0.0, pltpu.roll(wide, 127, 1)).astype(BF)
+    return at + rows.shape[0] // 64
+
+
+def layer_one(t1, x1, at, scale):
+    rhs = jnp.concatenate(
+        [x1[:, 128 * (at + kd) : 128 * (at + kd) + 256] for kd in range(3)], axis=0
+    )
+    half = dot(t1[...], rhs)
+    t = jnp.tanh(half)
+    act = half + half * t
+    act = act[:, :128] + act[:, 128:]
+    act = act.reshape(8, 2, 32, 128)
+    act = (act[:, 0] + act[:, 1]).reshape(256, 128)
+    act = act + pltpu.roll(act, 127, 1)
+    return half, t, (act * scale).astype(BF)
+
+
+def either_of(first_core):
+    def either(a, b, lo, hi):
+        return jnp.where(first_core, a[lo:hi, :], b[lo:hi, :])
+
+    return either
+
+
+def near_part(
+    vol_own,
+    swap_core,
+    swap_chip,
+    filter_one,
+    filter_two,
+    t1,
+    t2,
+    t2r,
+    x1_own,
+    pp,
+    sl1,
+    x1,
+):
+    me, blocks = position()
+    either = either_of(me % 2 == 0)
+    band_two_back(filter_two, t2r)
+    band_two(filter_two, t2)
+    band_one(filter_one, t1)
+    at = with_column_shifts(either(swap_chip, swap_core, 64, 512), x1, 0)
+    at = with_column_shifts(vol_own[...], x1, at)
+    at = with_column_shifts(either(swap_core, swap_chip, 0, 448), x1, at)
+    x1_own[...] = x1[:, 768:2048]
+    for j in range(10):
+        scale = jnp.where(inside(4 * me - 3 + j, 4 * blocks), 0.125, 0.0)
+        half, t, act = layer_one(t1, x1, 2 * j, scale)
+        if 3 <= j < 7:
+            slope = (1.0 + t) + half * (1.0 - t * t)
+            sl1[:, 256 * (j - 3) : 256 * (j - 3) + 256] = slope.astype(BF)
+        pp[:, 128 * j : 128 * j + 128] = act
 
 
 def body(
-    vol_own,
-    grad_own,
     swap_core,
     swap_chip,
     swap_chip2,
     swap_core2,
-    filter_one,
+    grad_own,
     filter_three,
+    t1,
     t2,
     t2r,
-    perm,
-    shift,
+    x1,
+    pp_near,
+    sl1,
     pair,
     squeeze,
     spread,
@@ -132,75 +210,43 @@
     grow1,
     kept,
     sent,
-    t1,
     w3t,
-    x1,
     pp,
+    xo,
     x2,
     q,
     x3,
     d2c,
-    sl1,
     sl2,
     d2,
     d1,
     out,
 ):
     me, blocks = position()
-    first_core = me % 2 == 0
-    lane = lax.broadcasted_iota(jnp.int32, (32, 640), 1) % 16
-    rows = filter_one[...].astype(F32).reshape(108, 32).astype(BF)
-    base = lax.dot_general(rows, perm[...], TN, preferred_element_type=F32)
-    for h in range(16):
-        moved = pltpu.roll(base, (h - 1) % 640, 1) if h != 1 else base
-        if h == 0:
-            moved = jnp.where(lane == 15, 0.0, moved)
-        if h == 15:
-            moved = jnp.where(lane == 0, 0.0, moved)
-        t1[32 * h : 32 * h + 32, :] = moved[:, :576].astype(BF)
+    either = either_of(me % 2 == 0)
     w3t[...] = (filter_three[...].astype(F32).T * 0.5).astype(BF)
 
-    def either(a, b, lo, hi):
-        return jnp.where(first_core, a[lo:hi, :], b[lo:hi, :])
-
-    at = 0
-    for rows in (
-        either(swap_chip2, swap_core2, 0, 448),
-        either(swap_chip, swap_core, 0, 512),
-        vol_own[...],
-        either(swap_core, swap_chip, 0, 512),
-        either(swap_core2, swap_chip2, 0, 448),
-    ):
-        moved = dot(rows, shift[...]).astype(BF)
-        count = rows.shape[0] // 64
-        for p in range(count):
-            lanes = slice(128 * (at + p), 128 * (at + p) + 128)
-            x1[0:64, lanes] = moved[64 * p : 64 * p + 64, :128]
-            x1[64:128, lanes] = rows[64 * p : 64 * p + 64, :]
-            x1[128:192, lanes] = moved[64 * p : 64 * p + 64, 128:]
-        at += count
-
-    for j in range(18):
-        rhs = jnp.concatenate(
-            [x1[:, (2 * j + kd) * 128 : (2 * j + kd) * 128 + 256] for kd in range(3)], axis=0
-        )
-        half = dot(t1[...], rhs)
-        t = jnp.tanh(half)
-        if 7 <= j < 11:
-            slope = (1.0 + t) + half * (1.0 - t * t)
-            sl1[:, (j - 7) * 256 : (j - 7) * 256 + 256] = slope.astype(BF)
-        act = half + half * t
-        act = act[:, :128] + act[:, 128:]
-        act = act.reshape(8, 2, 32, 128)
-        act = (act[:, 0] + act[:, 1]).reshape(256, 128)
-        act = act + pltpu.roll(act, 127, 1)
+    at = with_column_shifts(either(swap_chip2, swap_core2, 0, 448), xo, 0)
+    at = with_column_shifts(either(swap_chip, swap_core, 0, 192), xo, at)
+    at = with_column_shifts(either(swap_core, swap_chip, 320, 512), xo, at)
+    at = with_column_shifts(either(swap_core2, swap_chip2, 0, 448), xo, at)
+    for j in (0, 1, 2, 3, 14, 15, 16, 17):
         scale = jnp.where(inside(4 * me - 7 + j, 4 * blocks), 0.125, 0.0)
-        pp[:, j * 128 : j * 128 + 128] = (act * scale).astype(BF)
+        act = layer_one(t1, xo, 2 * j if j < 4 else 10 + 2 * (j - 14), scale)[2]
+        lo = 128 * (j if j < 4 else j - 10)
+        pp[:, lo : lo + 128] = act
+
+    def pooled_plane(j):
+        if 4 <= j < 14:
+            return pp_near[:, 128 * (j - 4) : 128 * (j - 4) + 128]
+        lo = 128 * (j if j < 4 else j - 10)
+        return pp[:, lo : lo + 128]
 
     col64 = lax.broadcasted_iota(jnp.int32, (256, 128), 1) % 64
     first_col, last_col = (col64 == 0, col64 == 63)
     for first in range(17):
-        got = dot(pp[:, first * 128 : first * 128 + 256], pair[...])
+        both = jnp.concatenate([pooled_plane(first), pooled_plane(first + 1)], axis=1)
+        got = dot(both, pair[...])
         moved = (
             jnp.where(first_col, 0.0, pltpu.roll(got, 1, 1)).astype(BF),
             got.astype(BF),
@@ -357,7 +403,7 @@
                 lane16 < 64, low[:16], high[16:]
             ).astype(BF)
 
-    lhs = jnp.concatenate([x1[:, 128 * (14 + kd) : 128 * (14 + kd) + 1024] for kd in range(3)], axis=0)
+    lhs = jnp.concatenate([x1[:, 128 * kd : 128 * kd + 1024] for kd in range(3)], axis=0)
     got = lax.dot_general(lhs, d1[...], NT, preferred_element_type=F32)
     row = lax.broadcasted_iota(jnp.int32, (576, 128), 0) % 16
     col = lax.broadcasted_iota(jnp.int32, (576, 128), 1) // 32
@@ -429,39 +475,41 @@
 
 
 FAR = pl.BlockSpec(memory_space=pl.ANY)
-BANDED = ((320, 1440), (256, 4608))
-
-
-def run_build(filter_two):
+HANDED = ((512, 576), (320, 1440), (256, 4608), (192, 1280), (256, 1280), (512, 1024))
+
+
+def run_near(volume, swap_core, swap_chip, filter_one, filter_two):
+    args = [volume, swap_core, swap_chip, filter_one, filter_two]
     return pl.pallas_call(
-        build,
-        out_shape=[jax.ShapeDtypeStruct(shape, BF) for shape in BANDED],
-        in_specs=[VMEM],
-        out_specs=[VMEM] * 2,
-        compiler_params=pltpu.CompilerParams(vmem_limit_bytes=16 * 1024 * 1024),
-        cost_estimate=pl.CostEstimate(flops=10**9, bytes_accessed=6 * 10**6, transcendentals=0),
-        name="build",
-    )(filter_two)
-
-
-def local_grads(volume, grad, swaps, filter_one, filter_three, banded, rows):
+        near_part,
+        out_shape=[jax.ShapeDtypeStruct(shape, BF) for shape in HANDED],
+        in_specs=[VMEM] * len(args),
+        out_specs=[VMEM] * len(HANDED),
+        scratch_shapes=[near(192, 22 * 128)],
+        compiler_params=pltpu.CompilerParams(vmem_limit_bytes=20 * 1024 * 1024),
+        cost_estimate=pl.CostEstimate(
+            flops=3 * 10**9, bytes_accessed=8 * 10**6, transcendentals=0
+        ),
+        name="near_part",
+    )(*args)
+
+
+def local_grads(swaps, grad, filter_three, handed, rows):
     tables = [jnp.asarray(t, BF) for t in one_hot_tables()]
-    args = [volume, grad, *swaps, filter_one, filter_three, *banded, *tables]
+    args = [*swaps, grad, filter_three, *handed, *tables]
     return pl.pallas_call(
         body,
         out_shape=[jax.ShapeDtypeStruct((rows // 2, 128), BF)] * 2,
         in_specs=[VMEM] * len(args),
         out_specs=[VMEM] * 2,
         scratch_shapes=[
-            near(512, 576),
             near(128, 1728),
-            near(192, 38 * 128),
-            near(256, 18 * 128),
+            near(256, 8 * 128),
+            near(192, 20 * 128),
             near(2304, 1024),
             near(512, 512),
             near(1728, 768),
             near(4608, 256),
-            near(512, 1024),
             near(512, 512),
             near(512, 512),
             near(512, 1024),
@@ -526,19 +574,12 @@
     swap_chip = swap(own, 1)
     relay = second(swap_core)
     swap_chip2 = swap(relay, 1)
-    f2_later = lax.optimization_barrier((f2, relay))[0]
-    banded = run_build(f2_later)
-    swap_chip, *banded = lax.optimization_barrier((swap_chip, *banded))
-    swap_core2 = swap(second(swap_chip, 1), 0)
+    chip_later = lax.optimization_barrier((swap_chip, relay))[0]
+    swap_core2 = swap(second(chip_later, 1), 0)
     chips = spaces // 2
+    handed = run_near(own, swap_core, swap_chip, f1, f2)
     keep, send = local_grads(
-        own,
-        grad,
-        (swap_core, swap_chip, swap_chip2, swap_core2),
-        f1,
-        f3,
-        banded,
-        spaces * SLOT,
+        (swap_core, swap_chip, swap_chip2, swap_core2), grad, f3, handed, spaces * SLOT
     )
     half = (keep.astype(F32) + swap(send, 0).astype(F32)).astype(BF)
     part = total_of(over_chips(half.reshape(chips, SLOT, 128)))

time: 77.8 us -> 79.3 us (1.019)
  local copies, waits for them, and re-layouts: 1.09 us -> 2.71 us
  waiting for transfers between devices: 3.99 us -> 2.59 us
    pallas_call x1, Pallas kernels: 0.53 us -> 3.09 us  [run_near(): pl.pallas_call(near_part, out_shape=[jax.ShapeDtypeStruct(shape, BF) for...]
    pallas_call x1, Pallas kernels: 13.3 us -> 11.3 us  [local_grads(): pl.pallas_call(body, out_shape=[jax.ShapeDtypeStruct((rows // 2, 128), BF...]
    unnamed x26 -> x22, local copies, waits for them, and re-layouts: 0.99 us -> 2.62 us
    ppermute x6, waiting for transfers between devices: 3.99 us -> 2.59 us  [swap(): return lax.ppermute(values, 'space', pairs + [(j, i) for i, j in pairs])]
  transfers between devices with their start and end apart: 6 -> 6, of which waited for: 4 -> 3; matrix products, arithmetic and copies ran while one was open for 1% -> 2% of each run, Pallas kernels for 1% -> 4%
where the time goes in v9:
time: 79.3 us; the launch traced here: 78.9 us
  blocking collectives  41.9 us (53%)
  Pallas kernels  15.6 us (20%)
  starting transfers between devices  13.5 us (17%)
  local copies, waits for them, and re-layouts  2.71 us (3%)
  waiting for transfers between devices  2.59 us (3%)
  other arithmetic  1.57 us (2%)
  between operations  1.02 us (1%)
    all_to_all x2, blocking collectives, over_chips(): lax.all_to_all(pieces, 'space', 0, 0, axis_index_groups=groups, tiled=True)  25.8 us
    all_to_all x1, blocking collectives, over_sample(): return lax.all_to_all(pieces, 'sample', 0, 0, tiled=True)  16.1 us
    ppermute x6, starting transfers between devices, swap(): return lax.ppermute(values, 'space', pairs + [(j, i) for i, j in pairs])  13.5 us
    pallas_call x1, Pallas kernels, local_grads(): pl.pallas_call(body, out_shape=[jax.ShapeDtypeStruct((rows // 2, 128), BF...  11.3 us
    pallas_call x1, Pallas kernels, run_near(): pl.pallas_call(near_part, out_shape=[jax.ShapeDtypeStruct(shape, BF) for...  3.09 us
    unnamed x22, local copies, waits for them, and re-layouts  2.62 us
    ppermute x6, waiting for transfers between devices, swap(): return lax.ppermute(values, 'space', pairs + [(j, i) for i, j in pairs])  2.59 us
  transfers between devices with their start and end apart: 6, of which 3 were waited for; matrix products, arithmetic and copies ran while one was open for 2% of the time, Pallas kernels for 4%

profile of v9, /device:TPU:1, one launch (start us, length us, event | category | flops | bytes accessed | tf_op | source)
XLA Modules:
  0.0 78.9 jit_solution(11821123213903765714)
XLA Ops:
  0.6 3.3 %collective-permute-start = (bf16[512,128]{1,0:T(8,128)(2,1)}, bf16[512,128]{1,0:T(8,128)(2,1)S(1)}, u32[]{:S(2)}, u32[]{:S(2)}) collective-permute-start(bf16[512,128]{1,0:T(8,128)(2,1)} %bitcast.17), channel_id=1, source_target_pairs={{0,1},{2,3},{4,5},{6,7},{8,9},{10,11},{12,13},{14,15},{16,17},{18,... | collective-permute-start | bytes 393224 | tf_op jit(solution)/shard_map/ppermute | solution.py:557
  4.0 1.9 %collective-permute-start.1 = (bf16[512,128]{1,0:T(8,128)(2,1)}, bf16[512,128]{1,0:T(8,128)(2,1)S(1)}, u32[]{:S(2)}, u32[]{:S(2)}) collective-permute-start(bf16[512,128]{1,0:T(8,128)(2,1)} %bitcast.18), channel_id=1, source_target_pairs={{1,2},{3,4},{5,6},{7,8},{9,10},{11,12},{13,14},{15,16},{17,18},{19... | collective-permute-start | bytes 393224 | tf_op jit(solution)/shard_map/ppermute | solution.py:557
  5.9 0.0 collective-permute-done.swap_core
  5.9 0.7 pad_maximum_fusion.1
  6.6 3.6 %collective-permute-start.2 = (bf16[480,128]{1,0:T(8,128)(2,1)S(1)}, bf16[480,128]{1,0:T(8,128)(2,1)S(1)}, u32[]{:S(2)}, u32[]{:S(2)}) collective-permute-start(bf16[480,128]{1,0:T(8,128)(2,1)S(1)} %pad_maximum_fusion.1), channel_id=1, source_target_pairs={{1,2},{3,4},{5,6},{7,8},{9,10},{11,12},{13,14},{15,16},{17,18},{19... | collective-permute-start | bytes 368648 | tf_op jit(solution)/shard_map/ppermute | solution.py:557
  10.3 0.2 collective-permute-done.1.swap_chip
  10.5 0.7 pad_maximum_fusion
  11.2 0.1 collective-permute-start.3
  11.3 0.0 copy-start.2
  11.3 0.9 %copy-done.2 = bf16[3,3,3,32,64]{4,3,2,1,0:T(8,128)(2,1)S(1)} copy-done((bf16[3,3,3,32,64]{4,3,2,1,0:T(8,128)(2,1)S(1)}, bf16[3,3,3,32,64]{4,3,2,1,0:T(8,128)(2,1)}, u32[]{:S(2)}) %copy-start.2) | copy-done | bytes 110616
  12.2 0.0 copy-start.3
  12.2 0.9 %copy-done.3 = bf16[1,8,4,16,128]{4,3,2,1,0:T(8,128)(2,1)S(1)} copy-done((bf16[1,8,4,16,128]{4,3,2,1,0:T(8,128)(2,1)S(1)}, bf16[1,8,4,16,128]{4,3,2,1,0:T(8,128)(2,1)}, u32[]{:S(2)}) %copy-start.3) | copy-done | bytes 131096
  13.1 0.0 copy-start.4
  13.1 0.7 copy-done.4
  13.9 0.0 copy-start
  13.9 0.0 copy-start.1
  13.9 0.0 copy-start.5
  13.9 0.0 copy-start.6
  13.9 0.0 copy-start.7
  13.9 0.0 copy-start.8
  13.9 0.0 copy-start.9
  13.9 0.0 copy-start.10
  13.9 3.1 %near_part.1 = (bf16[512,576]{1,0:T(8,128)(2,1)S(1)}, bf16[320,1440]{1,0:T(8,128)(2,1)S(1)}, bf16[256,4608]{1,0:T(8,128)(2,1)S(1)}, bf16[192,1280]{1,0:T(8,128)(...) custom-call(bf16[512,128]{1,0:T(8,128)(2,1)S(1)} %bitcast.19, ...), custom_call_target="tpu_custom_call" | custom-call | flops 3000000000 | bytes 8000000 | tf_op jit(solution)/shard_map/near_part/pallas_call | solution.py:483
  17.0 0.0 collective-permute-done.3.swap_core2
  17.0 0.0 collective-permute-done.2.swap_chip2
  17.0 0.0 copy-done
  17.0 0.0 copy-done.1
  17.1 0.0 copy-done.5
  17.1 0.0 copy-done.6
  17.1 0.0 copy-done.7
  17.1 0.0 copy-done.8
  17.1 0.0 copy-done.9
  17.1 0.0 copy-done.10
  17.1 11.3 %local_grads.1 = (bf16[1152,128]{1,0:T(8,128)(2,1)S(1)}, bf16[1152,128]{1,0:T(8,128)(2,1)S(1)}) custom-call(bf16[512,128]{1,0:T(8,128)(2,1)S(1)} %collective-permute-done.swap_core, bf16[512,128]{1,0:T(8,128)(2,1)S(1)} %collective-permute-done.1.swap_chip, bf16[480,128]{1,0:T(8,128)(2,1)S(1)} %collective-permute-done.2.swap_chip2, ...), custom_call_target="tpu_custom_call" | custom-call | flops 10000000000 | bytes 10000000 | tf_op jit(solution)/shard_map/local_grads/pallas_call | solution.py:500
  28.4 0.6 collective-permute-start.4
  28.9 1.2 %collective-permute-done.4 = bf16[1152,128]{1,0:T(8,128)(2,1)S(1)} collective-permute-done((bf16[1152,128]{1,0:T(8,128)(2,1)S(1)}, bf16[1152,128]{1,0:T(8,128)(2,1)S(1)}, u32[]{:S(2)}, u32[]{:S(2)}) %collective-permute-start.4) | collective-permute-done | bytes 294944 | tf_op jit(solution)/shard_map/ppermute | solution.py:557
  30.1 0.1 add_convert_fusion
  30.2 15.1 %all_to_all.15 = bf16[16,72,128]{2,1,0:T(8,128)(2,1)S(1)} all-to-all(bf16[16,72,128]{2,1,0:T(8,128)(2,1)S(1)} %bitcast.21), channel_id=1, replica_groups={{0,2,4,6,8,10,12,14,16,18,20,22,24,26,28,30},{1,3,5,7,9,11,13,15,17,19,..., dimensions={0} | all-to-all | bytes 589824 | tf_op jit(solution)/shard_map/all_to_all | solution.py:547
  45.4 16.1 %all_to_all.16 = bf16[8,72,128]{2,1,0:T(8,128)(2,1)S(1)} all-to-all(bf16[8,72,128]{2,1,0:T(8,128)(2,1)S(1)} %broadcast_in_dim.4), channel_id=1, replica_groups=mesh['sample'=8,'space'=32] {'sample'}, dimensions={0} | all-to-all | bytes 294912 | tf_op jit(solution)/shard_map/all_to_all | solution.py:541
  61.6 10.6 %all_to_all.17 = bf16[16,72,128]{2,1,0:T(8,128)(2,1)S(1)} all-to-all(bf16[16,72,128]{2,1,0:T(8,128)(2,1)S(1)} %broadcast_in_dim.5), channel_id=1, replica_groups={{0,2,4,6,8,10,12,14,16,18,20,22,24,26,28,30},{1,3,5,7,9,11,13,15,17,19,..., dimensions={0} | all-to-all | bytes 589824 | tf_op jit(solution)/shard_map/all_to_all | solution.py:547
  72.3 4.0 %collective-permute-start.5 = (bf16[1152,128]{1,0:T(8,128)(2,1)S(1)}, bf16[1152,128]{1,0:T(8,128)(2,1)S(1)}, u32[]{:S(2)}, u32[]{:S(2)}) collective-permute-start(bf16[1152,128]{1,0:T(8,128)(2,1)S(1)} %bitcast.10), channel_id=1, source_target_pairs={{0,1},{2,3},{4,5},{6,7},{8,9},{10,11},{12,13},{14,15},{16,17},{18,... | collective-permute-start | bytes 884744 | tf_op jit(solution)/shard_map/ppermute | solution.py:557
  76.3 1.2 %collective-permute-done.5.other = bf16[1152,128]{1,0:T(8,128)(2,1)S(1)} collective-permute-done((bf16[1152,128]{1,0:T(8,128)(2,1)S(1)}, bf16[1152,128]{1,0:T(8,128)(2,1)S(1)}, u32[]{:S(2)}, u32[]{:S(2)}) %collective-permute-start.5) | collective-permute-done | bytes 294944 | tf_op jit(solution)/shard_map/ppermute | solution.py:557
  77.5 1.3 %finish.1 = (f32[27,4,32]{2,1,0:T(4,128)}, f32[27,32,64]{2,1,0:T(8,128)}, f32[27,64,128]{2,1,0:T(8,128)}) custom-call(bf16[1152,128]{1,0:T(8,128)(2,1)S(1)} %bitcast.11, bf16[1152,128]{1,0:T(8,128)(2,1)S(1)} %collective-permute-done.5.other), custom_call_target="tpu_custom_call" | custom-call | tf_op jit(solution)/shard_map/finish/pallas_call | solution.py:527
  (6 shorter events, 0.2 us)
Async XLA Ops:
  0.6 5.3 %collective-permute-start = (bf16[512,128]{1,0:T(8,128)(2,1)}, bf16[512,128]{1,0:T(8,128)(2,1)S(1)}, u32[]{:S(2)}, u32[]{:S(2)}) collective-permute-start(bf16[512,128]{1,0:T(8,128)(2,1)} %bitcast.17), channel_id=1, source_target_pairs={{0,1},{2,3},{4,5},{6,7},{8,9},{10,11},{12,13},{14,15},{16,17},{18,... | collective-permute-start | bytes 393224 | tf_op jit(solution)/shard_map/ppermute | solution.py:557
  4.0 6.5 %collective-permute-start.1 = (bf16[512,128]{1,0:T(8,128)(2,1)}, bf16[512,128]{1,0:T(8,128)(2,1)S(1)}, u32[]{:S(2)}, u32[]{:S(2)}) collective-permute-start(bf16[512,128]{1,0:T(8,128)(2,1)} %bitcast.18), channel_id=1, source_target_pairs={{1,2},{3,4},{5,6},{7,8},{9,10},{11,12},{13,14},{15,16},{17,18},{19... | collective-permute-start | bytes 393224 | tf_op jit(solution)/shard_map/ppermute | solution.py:557
  6.6 10.4 %collective-permute-start.2 = (bf16[480,128]{1,0:T(8,128)(2,1)S(1)}, bf16[480,128]{1,0:T(8,128)(2,1)S(1)}, u32[]{:S(2)}, u32[]{:S(2)}) collective-permute-start(bf16[480,128]{1,0:T(8,128)(2,1)S(1)} %pad_maximum_fusion.1), channel_id=1, source_target_pairs={{1,2},{3,4},{5,6},{7,8},{9,10},{11,12},{13,14},{15,16},{17,18},{19... | collective-permute-start | bytes 368648 | tf_op jit(solution)/shard_map/ppermute | solution.py:557
  11.2 5.8 %collective-permute-start.3 = (bf16[480,128]{1,0:T(8,128)(2,1)S(1)}, bf16[480,128]{1,0:T(8,128)(2,1)S(1)}, u32[]{:S(2)}, u32[]{:S(2)}) collective-permute-start(bf16[480,128]{1,0:T(8,128)(2,1)S(1)} %pad_maximum_fusion), channel_id=1, source_target_pairs={{0,1},{2,3},{4,5},{6,7},{8,9},{10,11},{12,13},{14,15},{16,17},{18,... | collective-permute-start | bytes 368648 | tf_op jit(solution)/shard_map/ppermute | solution.py:557
  11.3 0.9 %copy-start.2 = (bf16[3,3,3,32,64]{4,3,2,1,0:T(8,128)(2,1)S(1)}, bf16[3,3,3,32,64]{4,3,2,1,0:T(8,128)(2,1)}, u32[]{:S(2)}) copy-start(bf16[3,3,3,32,64]{4,3,2,1,0:T(8,128)(2,1)} %param.14) | copy-start | bytes 331780
  12.2 0.9 %copy-start.3 = (bf16[1,8,4,16,128]{4,3,2,1,0:T(8,128)(2,1)S(1)}, bf16[1,8,4,16,128]{4,3,2,1,0:T(8,128)(2,1)}, u32[]{:S(2)}) copy-start(bf16[1,8,4,16,128]{4,3,2,1,0:T(8,128)(2,1)} %param.11) | copy-start | bytes 393220
  13.1 0.7 copy-start.4
  13.9 3.2 %copy-start = (bf16[1,1,2,16,128]{4,3,2,1,0:T(8,128)(2,1)S(1)}, bf16[1,1,2,16,128]{4,3,2,1,0:T(8,128)(2,1)}, u32[]{:S(2)}) copy-start(bf16[1,1,2,16,128]{4,3,2,1,0:T(8,128)(2,1)} %param.12) | copy-start | bytes 24580
  13.9 3.2 %copy-start.1 = (bf16[3,3,3,64,128]{4,3,2,1,0:T(8,128)(2,1)S(1)}, bf16[3,3,3,64,128]{4,3,2,1,0:T(8,128)(2,1)}, u32[]{:S(2)}) copy-start(bf16[3,3,3,64,128]{4,3,2,1,0:T(8,128)(2,1)} %param.15) | copy-start | bytes 1327108
  13.9 3.2 %copy-start.5 = (bf16[128,1152]{1,0:T(8,128)(2,1)S(1)}, bf16[128,1152]{1,0:T(8,128)(2,1)}, u32[]{:S(2)}) copy-start(bf16[128,1152]{1,0:T(8,128)(2,1)} %constant.41.clone.spread) | copy-start | bytes 884740
  13.9 3.2 %copy-start.6 = (bf16[256,512]{1,0:T(8,128)(2,1)S(1)}, bf16[256,512]{1,0:T(8,128)(2,1)}, u32[]{:S(2)}) copy-start(bf16[256,512]{1,0:T(8,128)(2,1)} %constant.44.clone.grow1) | copy-start | bytes 786436
  13.9 3.2 %copy-start.7 = (bf16[96,768]{1,0:T(8,128)(2,1)S(1)}, bf16[96,768]{1,0:T(8,128)(2,1)}, u32[]{:S(2)}) copy-start(bf16[96,768]{1,0:T(8,128)(2,1)} %constant.42.clone.grow_g) | copy-start | bytes 442372
  13.9 3.2 %copy-start.8 = (bf16[128,512]{1,0:T(8,128)(2,1)S(1)}, bf16[128,512]{1,0:T(8,128)(2,1)}, u32[]{:S(2)}) copy-start(bf16[128,512]{1,0:T(8,128)(2,1)} %constant.43.clone.grow2) | copy-start | bytes 393220
  13.9 3.2 %copy-start.9 = (bf16[512,128]{1,0:T(8,128)(2,1)S(1)}, bf16[512,128]{1,0:T(8,128)(2,1)}, u32[]{:S(2)}) copy-start(bf16[512,128]{1,0:T(8,128)(2,1)} %constant.40.clone.squeeze) | copy-start | bytes 393220
  13.9 3.2 %copy-start.10 = (bf16[256,128]{1,0:T(8,128)(2,1)S(1)}, bf16[256,128]{1,0:T(8,128)(2,1)}, u32[]{:S(2)}) copy-start(bf16[256,128]{1,0:T(8,128)(2,1)} %constant.39.clone.pair) | copy-start | bytes 196612
  28.4 1.8 %collective-permute-start.4 = (bf16[1152,128]{1,0:T(8,128)(2,1)S(1)}, bf16[1152,128]{1,0:T(8,128)(2,1)S(1)}, u32[]{:S(2)}, u32[]{:S(2)}) collective-permute-start(bf16[1152,128]{1,0:T(8,128)(2,1)S(1)} %get-tuple-element.23), channel_id=1, source_target_pairs={{0,1},{2,3},{4,5},{6,7},{8,9},{10,11},{12,13},{14,15},{16,17},{18,... | collective-permute-start | bytes 884744 | tf_op jit(solution)/shard_map/ppermute | solution.py:557
  72.3 5.2 %collective-permute-start.5 = (bf16[1152,128]{1,0:T(8,128)(2,1)S(1)}, bf16[1152,128]{1,0:T(8,128)(2,1)S(1)}, u32[]{:S(2)}, u32[]{:S(2)}) collective-permute-start(bf16[1152,128]{1,0:T(8,128)(2,1)S(1)} %bitcast.10), channel_id=1, source_target_pairs={{0,1},{2,3},{4,5},{6,7},{8,9},{10,11},{12,13},{14,15},{16,17},{18,... | collective-permute-start | bytes 884744 | tf_op jit(solution)/shard_map/ppermute | solution.py:557

commit v10 on v9

--- a/solution.py
+++ b/solution.py
@@ -475,6 +475,26 @@
 
 
 FAR = pl.BlockSpec(memory_space=pl.ANY)
+def relay_planes(block, grad, out):
+    first_core = position()[0] % 2 == 0
+    out[:448, :] = jnp.where(first_core, block[64:, :], block[:448, :])
+    out[448:, :] = grad[...]
+
+
+def run_relay(block, grad):
+    return pl.pallas_call(
+        relay_planes,
+        out_shape=jax.ShapeDtypeStruct((480, 128), BF),
+        in_specs=[VMEM] * 2,
+        out_specs=VMEM,
+        compiler_params=pltpu.CompilerParams(vmem_limit_bytes=4 * 1024 * 1024),
+        cost_estimate=pl.CostEstimate(
+            flops=4 * 10**9, bytes_accessed=12 * 10**6, transcendentals=0
+        ),
+        name="relay",
+    )(block, grad)
+
+
 HANDED = ((512, 576), (320, 1440), (256, 4608), (192, 1280), (256, 1280), (512, 1024))
 
 
@@ -566,8 +586,8 @@
     f3 = filter_three.reshape(1728, 128)
     core = lax.axis_index("space") % 2
 
-    def second(block, flip=0):
-        planes = lax.dynamic_slice(block, (64 * (core ^ flip), 0), (448, 128))
+    def second(block):
+        planes = lax.dynamic_slice(block, (64 * core, 0), (448, 128))
         return jnp.concatenate([planes, grad], axis=0)
 
     swap_core = swap(own, 0)
@@ -575,7 +595,7 @@
     relay = second(swap_core)
     swap_chip2 = swap(relay, 1)
     chip_later = lax.optimization_barrier((swap_chip, relay))[0]
-    swap_core2 = swap(second(chip_later, 1), 0)
+    swap_core2 = swap(run_relay(chip_later, grad), 0)
     chips = spaces // 2
     handed = run_near(own, swap_core, swap_chip, f1, f2)
     keep, send = local_grads(

time: 79.3 us -> 77.4 us (0.976)
  local copies, waits for them, and re-layouts: 2.71 us -> 1.59 us
    unnamed x22 -> x24, local copies, waits for them, and re-layouts: 2.62 us -> 1.51 us
  transfers between devices with their start and end apart: 6 -> 6, of which waited for: 3 -> 3; matrix products, arithmetic and copies ran while one was open for 2% -> 1% of each run, Pallas kernels for 4% -> 4%
where the time goes in v10:
time: 77.4 us; the launch traced here: 77 us
  blocking collectives  42.1 us (54%)
  Pallas kernels  15.7 us (20%)
  starting transfers between devices  12.9 us (17%)
  waiting for transfers between devices  2.9 us (4%)
  local copies, waits for them, and re-layouts  1.59 us (2%)
  between operations  1.04 us (1%)
  other arithmetic  0.9 us (1%)
    all_to_all x2, blocking collectives, over_chips(): lax.all_to_all(pieces, 'space', 0, 0, axis_index_groups=groups, tiled=True)  25.9 us
    all_to_all x1, blocking collectives, over_sample(): return lax.all_to_all(pieces, 'sample', 0, 0, tiled=True)  16.2 us
    ppermute x6, starting transfers between devices, swap(): return lax.ppermute(values, 'space', pairs + [(j, i) for i, j in pairs])  12.9 us
    pallas_call x1, Pallas kernels, local_grads(): pl.pallas_call(body, out_shape=[jax.ShapeDtypeStruct((rows // 2, 128), BF...  11.3 us
    pallas_call x1, Pallas kernels, run_near(): pl.pallas_call(near_part, out_shape=[jax.ShapeDtypeStruct(shape, BF) for...  3.09 us
    ppermute x6, waiting for transfers between devices, swap(): return lax.ppermute(values, 'space', pairs + [(j, i) for i, j in pairs])  2.9 us
  transfers between devices with their start and end apart: 6, of which 3 were waited for; matrix products, arithmetic and copies ran while one was open for 1% of the time, Pallas kernels for 4%

profile of v10, /device:TPU:1, one launch (start us, length us, event | category | flops | bytes accessed | tf_op | source)
XLA Modules:
  0.0 77.0 jit_solution(12528939035927200524)
XLA Ops:
  0.6 3.3 %collective-permute-start = (bf16[512,128]{1,0:T(8,128)(2,1)}, bf16[512,128]{1,0:T(8,128)(2,1)S(1)}, u32[]{:S(2)}, u32[]{:S(2)}) collective-permute-start(bf16[512,128]{1,0:T(8,128)(2,1)} %bitcast.17), channel_id=1, source_target_pairs={{0,1},{2,3},{4,5},{6,7},{8,9},{10,11},{12,13},{14,15},{16,17},{18,... | collective-permute-start | bytes 393224 | tf_op jit(solution)/shard_map/ppermute | solution.py:577
  4.0 1.9 %collective-permute-start.1 = (bf16[512,128]{1,0:T(8,128)(2,1)}, bf16[512,128]{1,0:T(8,128)(2,1)S(1)}, u32[]{:S(2)}, u32[]{:S(2)}) collective-permute-start(bf16[512,128]{1,0:T(8,128)(2,1)} %bitcast.18), channel_id=1, source_target_pairs={{1,2},{3,4},{5,6},{7,8},{9,10},{11,12},{13,14},{15,16},{17,18},{19... | collective-permute-start | bytes 393224 | tf_op jit(solution)/shard_map/ppermute | solution.py:577
  5.9 0.0 collective-permute-done.swap_core
  5.9 0.0 copy-start.3
  5.9 0.7 pad_maximum_fusion
  6.7 3.6 %collective-permute-start.2 = (bf16[480,128]{1,0:T(8,128)(2,1)S(1)}, bf16[480,128]{1,0:T(8,128)(2,1)S(1)}, u32[]{:S(2)}, u32[]{:S(2)}) collective-permute-start(bf16[480,128]{1,0:T(8,128)(2,1)S(1)} %pad_maximum_fusion), channel_id=1, source_target_pairs={{1,2},{3,4},{5,6},{7,8},{9,10},{11,12},{13,14},{15,16},{17,18},{19... | collective-permute-start | bytes 368648 | tf_op jit(solution)/shard_map/ppermute | solution.py:577
  10.3 0.1 collective-permute-done.1.block.swap_chip
  10.4 0.0 copy-start
  10.4 0.7 copy-done
  11.1 0.0 copy-start.4
  11.1 0.0 copy-start.5
  11.2 0.1 collective-permute-start.3
  11.3 0.0 copy-done.3
  11.3 0.8 copy-done.4
  12.0 0.0 copy-done.5
  12.1 0.0 copy-start.1
  12.1 0.0 copy-start.2
  12.1 0.0 copy-start.6
  12.1 0.0 copy-start.7
  12.1 0.0 copy-start.8
  12.1 0.0 copy-start.9
  12.1 0.0 copy-start.10
  12.1 0.0 copy-start.11
  12.1 3.1 %near_part.1 = (bf16[512,576]{1,0:T(8,128)(2,1)S(1)}, bf16[320,1440]{1,0:T(8,128)(2,1)S(1)}, bf16[256,4608]{1,0:T(8,128)(2,1)S(1)}, bf16[192,1280]{1,0:T(8,128)(...) custom-call(bf16[512,128]{1,0:T(8,128)(2,1)S(1)} %bitcast.19, ...), custom_call_target="tpu_custom_call" | custom-call | flops 3000000000 | bytes 8000000 | tf_op jit(solution)/shard_map/near_part/pallas_call | solution.py:503
  15.2 0.0 collective-permute-done.3.swap_core2
  15.2 0.0 collective-permute-done.2.swap_chip2
  15.2 0.0 copy-done.1
  15.3 0.0 copy-done.2
  15.3 0.0 copy-done.6
  15.3 0.0 copy-done.7
  15.3 0.0 copy-done.8
  15.3 0.0 copy-done.9
  15.3 0.0 copy-done.10
  15.3 0.0 copy-done.11
  15.3 11.3 %local_grads.1 = (bf16[1152,128]{1,0:T(8,128)(2,1)S(1)}, bf16[1152,128]{1,0:T(8,128)(2,1)S(1)}) custom-call(bf16[512,128]{1,0:T(8,128)(2,1)S(1)} %collective-permute-done.swap_core, bf16[512,128]{1,0:T(8,128)(2,1)S(1)} %collective-permute-done.1.block.swap_chip, bf16[480,128]{1,0:T(8,128)(2,1)S(1)} %collective-permute-done.2.swap_chip2, ...), custom_call_target="tpu_custom_call" | custom-call | flops 10000000000 | bytes 10000000 | tf_op jit(solution)/shard_map/local_grads/pallas_call | solution.py:520
  26.6 0.1 collective-permute-start.4
  26.7 1.6 %collective-permute-done.4 = bf16[1152,128]{1,0:T(8,128)(2,1)S(1)} collective-permute-done((bf16[1152,128]{1,0:T(8,128)(2,1)S(1)}, bf16[1152,128]{1,0:T(8,128)(2,1)S(1)}, u32[]{:S(2)}, u32[]{:S(2)}) %collective-permute-start.4) | collective-permute-done | bytes 294944 | tf_op jit(solution)/shard_map/ppermute | solution.py:577
  28.3 0.1 add_convert_fusion
  28.4 15.4 %all_to_all.15 = bf16[16,72,128]{2,1,0:T(8,128)(2,1)S(1)} all-to-all(bf16[16,72,128]{2,1,0:T(8,128)(2,1)S(1)} %bitcast.21), channel_id=1, replica_groups={{0,2,4,6,8,10,12,14,16,18,20,22,24,26,28,30},{1,3,5,7,9,11,13,15,17,19,..., dimensions={0} | all-to-all | bytes 589824 | tf_op jit(solution)/shard_map/all_to_all | solution.py:567
  43.8 16.2 %all_to_all.16 = bf16[8,72,128]{2,1,0:T(8,128)(2,1)S(1)} all-to-all(bf16[8,72,128]{2,1,0:T(8,128)(2,1)S(1)} %broadcast_in_dim.4), channel_id=1, replica_groups=mesh['sample'=8,'space'=32] {'sample'}, dimensions={0} | all-to-all | bytes 294912 | tf_op jit(solution)/shard_map/all_to_all | solution.py:561
  60.1 10.5 %all_to_all.17 = bf16[16,72,128]{2,1,0:T(8,128)(2,1)S(1)} all-to-all(bf16[16,72,128]{2,1,0:T(8,128)(2,1)S(1)} %broadcast_in_dim.5), channel_id=1, replica_groups={{0,2,4,6,8,10,12,14,16,18,20,22,24,26,28,30},{1,3,5,7,9,11,13,15,17,19,..., dimensions={0} | all-to-all | bytes 589824 | tf_op jit(solution)/shard_map/all_to_all | solution.py:567
  70.6 3.8 %collective-permute-start.5 = (bf16[1152,128]{1,0:T(8,128)(2,1)S(1)}, bf16[1152,128]{1,0:T(8,128)(2,1)S(1)}, u32[]{:S(2)}, u32[]{:S(2)}) collective-permute-start(bf16[1152,128]{1,0:T(8,128)(2,1)S(1)} %bitcast.10), channel_id=1, source_target_pairs={{0,1},{2,3},{4,5},{6,7},{8,9},{10,11},{12,13},{14,15},{16,17},{18,... | collective-permute-start | bytes 884744 | tf_op jit(solution)/shard_map/ppermute | solution.py:577
  74.4 1.2 %collective-permute-done.5.other = bf16[1152,128]{1,0:T(8,128)(2,1)S(1)} collective-permute-done((bf16[1152,128]{1,0:T(8,128)(2,1)S(1)}, bf16[1152,128]{1,0:T(8,128)(2,1)S(1)}, u32[]{:S(2)}, u32[]{:S(2)}) %collective-permute-start.5) | collective-permute-done | bytes 294944 | tf_op jit(solution)/shard_map/ppermute | solution.py:577
  75.6 1.3 %finish.1 = (f32[27,4,32]{2,1,0:T(4,128)}, f32[27,32,64]{2,1,0:T(8,128)}, f32[27,64,128]{2,1,0:T(8,128)}) custom-call(bf16[1152,128]{1,0:T(8,128)(2,1)S(1)} %bitcast.11, bf16[1152,128]{1,0:T(8,128)(2,1)S(1)} %collective-permute-done.5.other), custom_call_target="tpu_custom_call" | custom-call | tf_op jit(solution)/shard_map/finish/pallas_call | solution.py:547
  (6 shorter events, 0.2 us)
Async XLA Ops:
  0.6 5.3 %collective-permute-start = (bf16[512,128]{1,0:T(8,128)(2,1)}, bf16[512,128]{1,0:T(8,128)(2,1)S(1)}, u32[]{:S(2)}, u32[]{:S(2)}) collective-permute-start(bf16[512,128]{1,0:T(8,128)(2,1)} %bitcast.17), channel_id=1, source_target_pairs={{0,1},{2,3},{4,5},{6,7},{8,9},{10,11},{12,13},{14,15},{16,17},{18,... | collective-permute-start | bytes 393224 | tf_op jit(solution)/shard_map/ppermute | solution.py:577
  4.0 6.5 %collective-permute-start.1 = (bf16[512,128]{1,0:T(8,128)(2,1)}, bf16[512,128]{1,0:T(8,128)(2,1)S(1)}, u32[]{:S(2)}, u32[]{:S(2)}) collective-permute-start(bf16[512,128]{1,0:T(8,128)(2,1)} %bitcast.18), channel_id=1, source_target_pairs={{1,2},{3,4},{5,6},{7,8},{9,10},{11,12},{13,14},{15,16},{17,18},{19... | collective-permute-start | bytes 393224 | tf_op jit(solution)/shard_map/ppermute | solution.py:577
  5.9 5.4 %copy-start.3 = (bf16[3,3,3,32,64]{4,3,2,1,0:T(8,128)(2,1)S(1)}, bf16[3,3,3,32,64]{4,3,2,1,0:T(8,128)(2,1)}, u32[]{:S(2)}) copy-start(bf16[3,3,3,32,64]{4,3,2,1,0:T(8,128)(2,1)} %param.14) | copy-start | bytes 331780
  6.7 8.6 %collective-permute-start.2 = (bf16[480,128]{1,0:T(8,128)(2,1)S(1)}, bf16[480,128]{1,0:T(8,128)(2,1)S(1)}, u32[]{:S(2)}, u32[]{:S(2)}) collective-permute-start(bf16[480,128]{1,0:T(8,128)(2,1)S(1)} %pad_maximum_fusion), channel_id=1, source_target_pairs={{1,2},{3,4},{5,6},{7,8},{9,10},{11,12},{13,14},{15,16},{17,18},{19... | collective-permute-start | bytes 368648 | tf_op jit(solution)/shard_map/ppermute | solution.py:577
  10.4 0.7 copy-start
  11.1 0.9 %copy-start.4 = (bf16[1,8,4,16,128]{4,3,2,1,0:T(8,128)(2,1)S(1)}, bf16[1,8,4,16,128]{4,3,2,1,0:T(8,128)(2,1)}, u32[]{:S(2)}) copy-start(bf16[1,8,4,16,128]{4,3,2,1,0:T(8,128)(2,1)} %param.11) | copy-start | bytes 393220
  11.1 0.9 %copy-start.5 = (bf16[3,3,3,4,32]{4,3,2,1,0:T(4,128)(2,1)S(1)}, bf16[3,3,3,4,32]{4,3,2,1,0:T(4,128)(2,1)}, u32[]{:S(2)}) copy-start(bf16[3,3,3,4,32]{4,3,2,1,0:T(4,128)(2,1)} %param.13) | copy-start | bytes 20740
  11.2 4.0 %collective-permute-start.3 = (bf16[480,128]{1,0:T(8,128)(2,1)S(1)}, bf16[480,128]{1,0:T(8,128)(2,1)S(1)}, u32[]{:S(2)}, u32[]{:S(2)}) collective-permute-start(bf16[480,128]{1,0:T(8,128)(2,1)S(1)} %relay.1), channel_id=1, source_target_pairs={{0,1},{2,3},{4,5},{6,7},{8,9},{10,11},{12,13},{14,15},{16,17},{18,... | collective-permute-start | bytes 368648 | tf_op jit(solution)/shard_map/ppermute | solution.py:577
  12.1 3.2 %copy-start.1 = (bf16[1,1,2,16,128]{4,3,2,1,0:T(8,128)(2,1)S(1)}, bf16[1,1,2,16,128]{4,3,2,1,0:T(8,128)(2,1)}, u32[]{:S(2)}) copy-start(bf16[1,1,2,16,128]{4,3,2,1,0:T(8,128)(2,1)} %param.12) | copy-start | bytes 24580
  12.1 3.2 %copy-start.2 = (bf16[3,3,3,64,128]{4,3,2,1,0:T(8,128)(2,1)S(1)}, bf16[3,3,3,64,128]{4,3,2,1,0:T(8,128)(2,1)}, u32[]{:S(2)}) copy-start(bf16[3,3,3,64,128]{4,3,2,1,0:T(8,128)(2,1)} %param.15) | copy-start | bytes 1327108
  12.1 3.2 %copy-start.6 = (bf16[128,1152]{1,0:T(8,128)(2,1)S(1)}, bf16[128,1152]{1,0:T(8,128)(2,1)}, u32[]{:S(2)}) copy-start(bf16[128,1152]{1,0:T(8,128)(2,1)} %constant.40.clone.spread) | copy-start | bytes 884740
  12.1 3.2 %copy-start.7 = (bf16[256,512]{1,0:T(8,128)(2,1)S(1)}, bf16[256,512]{1,0:T(8,128)(2,1)}, u32[]{:S(2)}) copy-start(bf16[256,512]{1,0:T(8,128)(2,1)} %constant.43.clone.grow1) | copy-start | bytes 786436
  12.1 3.2 %copy-start.8 = (bf16[96,768]{1,0:T(8,128)(2,1)S(1)}, bf16[96,768]{1,0:T(8,128)(2,1)}, u32[]{:S(2)}) copy-start(bf16[96,768]{1,0:T(8,128)(2,1)} %constant.41.clone.grow_g) | copy-start | bytes 442372
  12.1 3.2 %copy-start.9 = (bf16[128,512]{1,0:T(8,128)(2,1)S(1)}, bf16[128,512]{1,0:T(8,128)(2,1)}, u32[]{:S(2)}) copy-start(bf16[128,512]{1,0:T(8,128)(2,1)} %constant.42.clone.grow2) | copy-start | bytes 393220
  12.1 3.2 %copy-start.10 = (bf16[512,128]{1,0:T(8,128)(2,1)S(1)}, bf16[512,128]{1,0:T(8,128)(2,1)}, u32[]{:S(2)}) copy-start(bf16[512,128]{1,0:T(8,128)(2,1)} %constant.39.clone.squeeze) | copy-start | bytes 393220
  12.1 3.2 %copy-start.11 = (bf16[256,128]{1,0:T(8,128)(2,1)S(1)}, bf16[256,128]{1,0:T(8,128)(2,1)}, u32[]{:S(2)}) copy-start(bf16[256,128]{1,0:T(8,128)(2,1)} %constant.38.clone.pair) | copy-start | bytes 196612
  26.6 1.7 %collective-permute-start.4 = (bf16[1152,128]{1,0:T(8,128)(2,1)S(1)}, bf16[1152,128]{1,0:T(8,128)(2,1)S(1)}, u32[]{:S(2)}, u32[]{:S(2)}) collective-permute-start(bf16[1152,128]{1,0:T(8,128)(2,1)S(1)} %get-tuple-element.23), channel_id=1, source_target_pairs={{0,1},{2,3},{4,5},{6,7},{8,9},{10,11},{12,13},{14,15},{16,17},{18,... | collective-permute-start | bytes 884744 | tf_op jit(solution)/shard_map/ppermute | solution.py:577
  70.6 5.0 %collective-permute-start.5 = (bf16[1152,128]{1,0:T(8,128)(2,1)S(1)}, bf16[1152,128]{1,0:T(8,128)(2,1)S(1)}, u32[]{:S(2)}, u32[]{:S(2)}) collective-permute-start(bf16[1152,128]{1,0:T(8,128)(2,1)S(1)} %bitcast.10), channel_id=1, source_target_pairs={{0,1},{2,3},{4,5},{6,7},{8,9},{10,11},{12,13},{14,15},{16,17},{18,... | collective-permute-start | bytes 884744 | tf_op jit(solution)/shard_map/ppermute | solution.py:577

commit v11 on v10

--- a/solution.py
+++ b/solution.py
@@ -475,15 +475,15 @@
 
 
 FAR = pl.BlockSpec(memory_space=pl.ANY)
-def relay_planes(block, grad, out):
-    first_core = position()[0] % 2 == 0
-    out[:448, :] = jnp.where(first_core, block[64:, :], block[:448, :])
+def relay_planes(last_seven, block, grad, out):
+    flag = position()[0] % 2 == last_seven
+    out[:448, :] = jnp.where(flag, block[64:, :], block[:448, :])
     out[448:, :] = grad[...]
 
 
-def run_relay(block, grad):
+def run_relay(last_seven, block, grad):
     return pl.pallas_call(
-        relay_planes,
+        functools.partial(relay_planes, last_seven),
         out_shape=jax.ShapeDtypeStruct((480, 128), BF),
         in_specs=[VMEM] * 2,
         out_specs=VMEM,
@@ -584,18 +584,12 @@
     f1 = filter_one.reshape(27, 4, 32)
     f2 = filter_two.reshape(27, 32, 64)
     f3 = filter_three.reshape(1728, 128)
-    core = lax.axis_index("space") % 2
-
-    def second(block):
-        planes = lax.dynamic_slice(block, (64 * core, 0), (448, 128))
-        return jnp.concatenate([planes, grad], axis=0)
-
     swap_core = swap(own, 0)
     swap_chip = swap(own, 1)
-    relay = second(swap_core)
+    relay = run_relay(1, swap_core, grad)
     swap_chip2 = swap(relay, 1)
     chip_later = lax.optimization_barrier((swap_chip, relay))[0]
-    swap_core2 = swap(run_relay(chip_later, grad), 0)
+    swap_core2 = swap(run_relay(0, chip_later, grad), 0)
     chips = spaces // 2
     handed = run_near(own, swap_core, swap_chip, f1, f2)
     keep, send = local_grads(

time: 77.4 us -> 76 us (0.982)
  starting transfers between devices: 12.9 us -> 13.7 us
    ppermute x6, starting transfers between devices: 12.9 us -> 13.7 us  [swap(): return lax.ppermute(values, 'space', pairs + [(j, i) for i, j in pairs])]
  transfers between devices with their start and end apart: 6 -> 6, of which waited for: 3 -> 2; matrix products, arithmetic and copies ran while one was open for 1% -> 0% of each run, Pallas kernels for 4% -> 4%
where the time goes in v11:
time: 76 us; the launch traced here: 75.6 us
  blocking collectives  41.9 us (55%)
  Pallas kernels  15.6 us (21%)
  starting transfers between devices  13.7 us (18%)
  waiting for transfers between devices  2.43 us (3%)
  between operations  1.07 us (1%)
  local copies, waits for them, and re-layouts  0.83 us (1%)
    all_to_all x2, blocking collectives, over_chips(): lax.all_to_all(pieces, 'space', 0, 0, axis_index_groups=groups, tiled=True)  25.8 us
    all_to_all x1, blocking collectives, over_sample(): return lax.all_to_all(pieces, 'sample', 0, 0, tiled=True)  16.1 us
    ppermute x6, starting transfers between devices, swap(): return lax.ppermute(values, 'space', pairs + [(j, i) for i, j in pairs])  13.7 us
    pallas_call x1, Pallas kernels, local_grads(): pl.pallas_call(body, out_shape=[jax.ShapeDtypeStruct((rows // 2, 128), BF...  11.3 us
    pallas_call x1, Pallas kernels, run_near(): pl.pallas_call(near_part, out_shape=[jax.ShapeDtypeStruct(shape, BF) for...  3.02 us
    ppermute x6, waiting for transfers between devices, swap(): return lax.ppermute(values, 'space', pairs + [(j, i) for i, j in pairs])  2.43 us
  transfers between devices with their start and end apart: 6, of which 2 were waited for; matrix products, arithmetic and copies ran while one was open for 0% of the time, Pallas kernels for 4%

profile of v11, /device:TPU:1, one launch (start us, length us, event | category | flops | bytes accessed | tf_op | source)
XLA Modules:
  0.0 75.6 jit_solution(157888487686126021)
XLA Ops:
  0.6 3.3 %collective-permute-start = (bf16[512,128]{1,0:T(8,128)(2,1)}, bf16[512,128]{1,0:T(8,128)(2,1)S(1)}, u32[]{:S(2)}, u32[]{:S(2)}) collective-permute-start(bf16[512,128]{1,0:T(8,128)(2,1)} %bitcast.14), channel_id=1, source_target_pairs={{0,1},{2,3},{4,5},{6,7},{8,9},{10,11},{12,13},{14,15},{16,17},{18,... | collective-permute-start | bytes 393224 | tf_op jit(solution)/shard_map/ppermute | solution.py:577
  4.0 1.9 %collective-permute-start.1 = (bf16[512,128]{1,0:T(8,128)(2,1)}, bf16[512,128]{1,0:T(8,128)(2,1)S(1)}, u32[]{:S(2)}, u32[]{:S(2)}) collective-permute-start(bf16[512,128]{1,0:T(8,128)(2,1)} %bitcast.15), channel_id=1, source_target_pairs={{1,2},{3,4},{5,6},{7,8},{9,10},{11,12},{13,14},{15,16},{17,18},{19... | collective-permute-start | bytes 393224 | tf_op jit(solution)/shard_map/ppermute | solution.py:577
  5.9 0.0 collective-permute-done.block.swap_core
  5.9 0.0 copy-start.4
  5.9 0.7 copy-done.4
  6.6 0.0 copy-start.1
  6.6 0.0 copy-start.2
  6.6 0.0 copy-start.3
  6.7 3.8 %collective-permute-start.2 = (bf16[480,128]{1,0:T(8,128)(2,1)S(1)}, bf16[480,128]{1,0:T(8,128)(2,1)S(1)}, u32[]{:S(2)}, u32[]{:S(2)}) collective-permute-start(bf16[480,128]{1,0:T(8,128)(2,1)S(1)} %relay.2), channel_id=1, source_target_pairs={{1,2},{3,4},{5,6},{7,8},{9,10},{11,12},{13,14},{15,16},{17,18},{19... | collective-permute-start | bytes 368648 | tf_op jit(solution)/shard_map/ppermute | solution.py:577
  10.4 0.0 collective-permute-done.1.block.swap_chip
  10.5 0.1 collective-permute-start.3
  10.6 0.0 copy-done.1
  10.6 0.0 copy-done.2
  10.6 0.0 copy-done.3
  10.6 0.0 copy-start
  10.6 0.0 copy-start.5
  10.6 0.0 copy-start.6
  10.7 0.0 copy-start.7
  10.7 0.0 copy-start.8
  10.7 0.0 copy-start.9
  10.7 0.0 copy-start.10
  10.7 0.0 copy-start.11
  10.7 3.0 %near_part.1 = (bf16[512,576]{1,0:T(8,128)(2,1)S(1)}, bf16[320,1440]{1,0:T(8,128)(2,1)S(1)}, bf16[256,4608]{1,0:T(8,128)(2,1)S(1)}, bf16[192,1280]{1,0:T(8,128)(...) custom-call(bf16[512,128]{1,0:T(8,128)(2,1)S(1)} %bitcast.16, ...), custom_call_target="tpu_custom_call" | custom-call | flops 3000000000 | bytes 8000000 | tf_op jit(solution)/shard_map/near_part/pallas_call | solution.py:503
  13.7 0.0 collective-permute-done.3.swap_core2
  13.7 0.0 collective-permute-done.2.swap_chip2
  13.8 0.0 copy-done
  13.8 0.0 copy-done.5
  13.8 0.0 copy-done.6
  13.8 0.0 copy-done.7
  13.8 0.0 copy-done.8
  13.8 0.0 copy-done.9
  13.8 0.0 copy-done.10
  13.8 0.0 copy-done.11
  13.8 11.3 %local_grads.1 = (bf16[1152,128]{1,0:T(8,128)(2,1)S(1)}, bf16[1152,128]{1,0:T(8,128)(2,1)S(1)}) custom-call(bf16[512,128]{1,0:T(8,128)(2,1)S(1)} %collective-permute-done.block.swap_core, bf16[512,128]{1,0:T(8,128)(2,1)S(1)} %collective-permute-done.1.block.swap_chip, bf16[480,128]{1,0:T(8,128)(2,1)S(1)} %collective-permute-done.2.swap_chip2, ...), custom_call_target="tpu_custom_call" | custom-call | flops 10000000000 | bytes 10000000 | tf_op jit(solution)/shard_map/local_grads/pallas_call | solution.py:520
  25.1 0.6 collective-permute-start.4
  25.7 1.2 %collective-permute-done.4 = bf16[1152,128]{1,0:T(8,128)(2,1)S(1)} collective-permute-done((bf16[1152,128]{1,0:T(8,128)(2,1)S(1)}, bf16[1152,128]{1,0:T(8,128)(2,1)S(1)}, u32[]{:S(2)}, u32[]{:S(2)}) %collective-permute-start.4) | collective-permute-done | bytes 294944 | tf_op jit(solution)/shard_map/ppermute | solution.py:577
  26.9 0.1 add_convert_fusion
  27.0 15.1 %all_to_all.15 = bf16[16,72,128]{2,1,0:T(8,128)(2,1)S(1)} all-to-all(bf16[16,72,128]{2,1,0:T(8,128)(2,1)S(1)} %bitcast.21), channel_id=1, replica_groups={{0,2,4,6,8,10,12,14,16,18,20,22,24,26,28,30},{1,3,5,7,9,11,13,15,17,19,..., dimensions={0} | all-to-all | bytes 589824 | tf_op jit(solution)/shard_map/all_to_all | solution.py:567
  42.2 16.1 %all_to_all.16 = bf16[8,72,128]{2,1,0:T(8,128)(2,1)S(1)} all-to-all(bf16[8,72,128]{2,1,0:T(8,128)(2,1)S(1)} %broadcast_in_dim.4), channel_id=1, replica_groups=mesh['sample'=8,'space'=32] {'sample'}, dimensions={0} | all-to-all | bytes 294912 | tf_op jit(solution)/shard_map/all_to_all | solution.py:561
  58.4 10.6 %all_to_all.17 = bf16[16,72,128]{2,1,0:T(8,128)(2,1)S(1)} all-to-all(bf16[16,72,128]{2,1,0:T(8,128)(2,1)S(1)} %broadcast_in_dim.5), channel_id=1, replica_groups={{0,2,4,6,8,10,12,14,16,18,20,22,24,26,28,30},{1,3,5,7,9,11,13,15,17,19,..., dimensions={0} | all-to-all | bytes 589824 | tf_op jit(solution)/shard_map/all_to_all | solution.py:567
  69.0 4.0 %collective-permute-start.5 = (bf16[1152,128]{1,0:T(8,128)(2,1)S(1)}, bf16[1152,128]{1,0:T(8,128)(2,1)S(1)}, u32[]{:S(2)}, u32[]{:S(2)}) collective-permute-start(bf16[1152,128]{1,0:T(8,128)(2,1)S(1)} %bitcast.10), channel_id=1, source_target_pairs={{0,1},{2,3},{4,5},{6,7},{8,9},{10,11},{12,13},{14,15},{16,17},{18,... | collective-permute-start | bytes 884744 | tf_op jit(solution)/shard_map/ppermute | solution.py:577
  73.0 1.2 %collective-permute-done.5.other = bf16[1152,128]{1,0:T(8,128)(2,1)S(1)} collective-permute-done((bf16[1152,128]{1,0:T(8,128)(2,1)S(1)}, bf16[1152,128]{1,0:T(8,128)(2,1)S(1)}, u32[]{:S(2)}, u32[]{:S(2)}) %collective-permute-start.5) | collective-permute-done | bytes 294944 | tf_op jit(solution)/shard_map/ppermute | solution.py:577
  74.2 1.3 %finish.1 = (f32[27,4,32]{2,1,0:T(4,128)}, f32[27,32,64]{2,1,0:T(8,128)}, f32[27,64,128]{2,1,0:T(8,128)}) custom-call(bf16[1152,128]{1,0:T(8,128)(2,1)S(1)} %bitcast.11, bf16[1152,128]{1,0:T(8,128)(2,1)S(1)} %collective-permute-done.5.other), custom_call_target="tpu_custom_call" | custom-call | tf_op jit(solution)/shard_map/finish/pallas_call | solution.py:547
  (6 shorter events, 0.2 us)
Async XLA Ops:
  0.6 5.2 %collective-permute-start = (bf16[512,128]{1,0:T(8,128)(2,1)}, bf16[512,128]{1,0:T(8,128)(2,1)S(1)}, u32[]{:S(2)}, u32[]{:S(2)}) collective-permute-start(bf16[512,128]{1,0:T(8,128)(2,1)} %bitcast.14), channel_id=1, source_target_pairs={{0,1},{2,3},{4,5},{6,7},{8,9},{10,11},{12,13},{14,15},{16,17},{18,... | collective-permute-start | bytes 393224 | tf_op jit(solution)/shard_map/ppermute | solution.py:577
  4.0 6.5 %collective-permute-start.1 = (bf16[512,128]{1,0:T(8,128)(2,1)}, bf16[512,128]{1,0:T(8,128)(2,1)S(1)}, u32[]{:S(2)}, u32[]{:S(2)}) collective-permute-start(bf16[512,128]{1,0:T(8,128)(2,1)} %bitcast.15), channel_id=1, source_target_pairs={{1,2},{3,4},{5,6},{7,8},{9,10},{11,12},{13,14},{15,16},{17,18},{19... | collective-permute-start | bytes 393224 | tf_op jit(solution)/shard_map/ppermute | solution.py:577
  5.9 0.7 copy-start.4
  6.6 4.0 %copy-start.1 = (bf16[3,3,3,32,64]{4,3,2,1,0:T(8,128)(2,1)S(1)}, bf16[3,3,3,32,64]{4,3,2,1,0:T(8,128)(2,1)}, u32[]{:S(2)}) copy-start(bf16[3,3,3,32,64]{4,3,2,1,0:T(8,128)(2,1)} %param.14) | copy-start | bytes 331780
  6.6 4.0 %copy-start.2 = (bf16[1,8,4,16,128]{4,3,2,1,0:T(8,128)(2,1)S(1)}, bf16[1,8,4,16,128]{4,3,2,1,0:T(8,128)(2,1)}, u32[]{:S(2)}) copy-start(bf16[1,8,4,16,128]{4,3,2,1,0:T(8,128)(2,1)} %param.11) | copy-start | bytes 393220
  6.6 4.0 %copy-start.3 = (bf16[3,3,3,4,32]{4,3,2,1,0:T(4,128)(2,1)S(1)}, bf16[3,3,3,4,32]{4,3,2,1,0:T(4,128)(2,1)}, u32[]{:S(2)}) copy-start(bf16[3,3,3,4,32]{4,3,2,1,0:T(4,128)(2,1)} %param.13) | copy-start | bytes 20740
  6.7 7.1 %collective-permute-start.2 = (bf16[480,128]{1,0:T(8,128)(2,1)S(1)}, bf16[480,128]{1,0:T(8,128)(2,1)S(1)}, u32[]{:S(2)}, u32[]{:S(2)}) collective-permute-start(bf16[480,128]{1,0:T(8,128)(2,1)S(1)} %relay.2), channel_id=1, source_target_pairs={{1,2},{3,4},{5,6},{7,8},{9,10},{11,12},{13,14},{15,16},{17,18},{19... | collective-permute-start | bytes 368648 | tf_op jit(solution)/shard_map/ppermute | solution.py:577
  10.5 3.3 %collective-permute-start.3 = (bf16[480,128]{1,0:T(8,128)(2,1)S(1)}, bf16[480,128]{1,0:T(8,128)(2,1)S(1)}, u32[]{:S(2)}, u32[]{:S(2)}) collective-permute-start(bf16[480,128]{1,0:T(8,128)(2,1)S(1)} %relay.3), channel_id=1, source_target_pairs={{0,1},{2,3},{4,5},{6,7},{8,9},{10,11},{12,13},{14,15},{16,17},{18,... | collective-permute-start | bytes 368648 | tf_op jit(solution)/shard_map/ppermute | solution.py:577
  10.6 3.1 %copy-start = (bf16[3,3,3,64,128]{4,3,2,1,0:T(8,128)(2,1)S(1)}, bf16[3,3,3,64,128]{4,3,2,1,0:T(8,128)(2,1)}, u32[]{:S(2)}) copy-start(bf16[3,3,3,64,128]{4,3,2,1,0:T(8,128)(2,1)} %param.15) | copy-start | bytes 1327108
  10.6 3.1 %copy-start.5 = (bf16[1,1,2,16,128]{4,3,2,1,0:T(8,128)(2,1)S(1)}, bf16[1,1,2,16,128]{4,3,2,1,0:T(8,128)(2,1)}, u32[]{:S(2)}) copy-start(bf16[1,1,2,16,128]{4,3,2,1,0:T(8,128)(2,1)} %param.12) | copy-start | bytes 24580
  10.6 3.1 %copy-start.6 = (bf16[128,1152]{1,0:T(8,128)(2,1)S(1)}, bf16[128,1152]{1,0:T(8,128)(2,1)}, u32[]{:S(2)}) copy-start(bf16[128,1152]{1,0:T(8,128)(2,1)} %constant.18.clone.spread) | copy-start | bytes 884740
  10.7 3.1 %copy-start.7 = (bf16[256,512]{1,0:T(8,128)(2,1)S(1)}, bf16[256,512]{1,0:T(8,128)(2,1)}, u32[]{:S(2)}) copy-start(bf16[256,512]{1,0:T(8,128)(2,1)} %constant.21.clone.grow1) | copy-start | bytes 786436
  10.7 3.1 %copy-start.8 = (bf16[96,768]{1,0:T(8,128)(2,1)S(1)}, bf16[96,768]{1,0:T(8,128)(2,1)}, u32[]{:S(2)}) copy-start(bf16[96,768]{1,0:T(8,128)(2,1)} %constant.19.clone.grow_g) | copy-start | bytes 442372
  10.7 3.1 %copy-start.9 = (bf16[128,512]{1,0:T(8,128)(2,1)S(1)}, bf16[128,512]{1,0:T(8,128)(2,1)}, u32[]{:S(2)}) copy-start(bf16[128,512]{1,0:T(8,128)(2,1)} %constant.20.clone.grow2) | copy-start | bytes 393220
  10.7 3.1 %copy-start.10 = (bf16[512,128]{1,0:T(8,128)(2,1)S(1)}, bf16[512,128]{1,0:T(8,128)(2,1)}, u32[]{:S(2)}) copy-start(bf16[512,128]{1,0:T(8,128)(2,1)} %constant.17.clone.squeeze) | copy-start | bytes 393220
  10.7 3.1 %copy-start.11 = (bf16[256,128]{1,0:T(8,128)(2,1)S(1)}, bf16[256,128]{1,0:T(8,128)(2,1)}, u32[]{:S(2)}) copy-start(bf16[256,128]{1,0:T(8,128)(2,1)} %constant.16.clone.pair) | copy-start | bytes 196612
  25.1 1.8 %collective-permute-start.4 = (bf16[1152,128]{1,0:T(8,128)(2,1)S(1)}, bf16[1152,128]{1,0:T(8,128)(2,1)S(1)}, u32[]{:S(2)}, u32[]{:S(2)}) collective-permute-start(bf16[1152,128]{1,0:T(8,128)(2,1)S(1)} %get-tuple-element.23), channel_id=1, source_target_pairs={{0,1},{2,3},{4,5},{6,7},{8,9},{10,11},{12,13},{14,15},{16,17},{18,... | collective-permute-start | bytes 884744 | tf_op jit(solution)/shard_map/ppermute | solution.py:577
  69.0 5.2 %collective-permute-start.5 = (bf16[1152,128]{1,0:T(8,128)(2,1)S(1)}, bf16[1152,128]{1,0:T(8,128)(2,1)S(1)}, u32[]{:S(2)}, u32[]{:S(2)}) collective-permute-start(bf16[1152,128]{1,0:T(8,128)(2,1)S(1)} %bitcast.10), channel_id=1, source_target_pairs={{0,1},{2,3},{4,5},{6,7},{8,9},{10,11},{12,13},{14,15},{16,17},{18,... | collective-permute-start | bytes 884744 | tf_op jit(solution)/shard_map/ppermute | solution.py:577

commit v12 on v11

--- a/solution.py
+++ b/solution.py
@@ -163,16 +163,19 @@
     swap_chip,
     filter_one,
     filter_two,
+    filter_three,
     t1,
     t2,
     t2r,
     x1_own,
     pp,
     sl1,
+    w3t,
     x1,
 ):
     me, blocks = position()
     either = either_of(me % 2 == 0)
+    w3t[...] = (filter_three[...].astype(F32).T * 0.5).astype(BF)
     band_two_back(filter_two, t2r)
     band_two(filter_two, t2)
     band_one(filter_one, t1)
@@ -202,6 +205,7 @@
     x1,
     pp_near,
     sl1,
+    w3t,
     pair,
     squeeze,
     spread,
@@ -210,7 +214,6 @@
     grow1,
     kept,
     sent,
-    w3t,
     pp,
     xo,
     x2,
@@ -224,7 +227,6 @@
 ):
     me, blocks = position()
     either = either_of(me % 2 == 0)
-    w3t[...] = (filter_three[...].astype(F32).T * 0.5).astype(BF)
 
     at = with_column_shifts(either(swap_chip2, swap_core2, 0, 448), xo, 0)
     at = with_column_shifts(either(swap_chip, swap_core, 0, 192), xo, at)
@@ -495,11 +497,11 @@
     )(block, grad)
 
 
-HANDED = ((512, 576), (320, 1440), (256, 4608), (192, 1280), (256, 1280), (512, 1024))
-
-
-def run_near(volume, swap_core, swap_chip, filter_one, filter_two):
-    args = [volume, swap_core, swap_chip, filter_one, filter_two]
+HANDED = ((512, 576), (320, 1440), (256, 4608), (192, 1280), (256, 1280), (512, 1024), (128, 1728))
+
+
+def run_near(volume, swap_core, swap_chip, filter_one, filter_two, filter_three):
+    args = [volume, swap_core, swap_chip, filter_one, filter_two, filter_three]
     return pl.pallas_call(
         near_part,
         out_shape=[jax.ShapeDtypeStruct(shape, BF) for shape in HANDED],
@@ -523,7 +525,6 @@
         in_specs=[VMEM] * len(args),
         out_specs=[VMEM] * 2,
         scratch_shapes=[
-            near(128, 1728),
             near(256, 8 * 128),
             near(192, 20 * 128),
             near(2304, 1024),
@@ -591,7 +592,7 @@
     chip_later = lax.optimization_barrier((swap_chip, relay))[0]
     swap_core2 = swap(run_relay(0, chip_later, grad), 0)
     chips = spaces // 2
-    handed = run_near(own, swap_core, swap_chip, f1, f2)
+    handed = run_near(own, swap_core, swap_chip, f1, f2, f3)
     keep, send = local_grads(
         (swap_core, swap_chip, swap_chip2, swap_core2), grad, f3, handed, spaces * SLOT
     )

time: 76 us -> 76 us (level)
  no operation moved by 1% of the time
where the time goes in v12:
time: 76 us; the launch traced here: 75.7 us
  blocking collectives  41.9 us (55%)
  Pallas kernels  15.6 us (21%)
  starting transfers between devices  13.7 us (18%)
  waiting for transfers between devices  2.43 us (3%)
  between operations  1.06 us (1%)
  local copies, waits for them, and re-layouts  0.82 us (1%)
    all_to_all x2, blocking collectives, over_chips(): lax.all_to_all(pieces, 'space', 0, 0, axis_index_groups=groups, tiled=True)  25.8 us
    all_to_all x1, blocking collectives, over_sample(): return lax.all_to_all(pieces, 'sample', 0, 0, tiled=True)  16.1 us
    ppermute x6, starting transfers between devices, swap(): return lax.ppermute(values, 'space', pairs + [(j, i) for i, j in pairs])  13.7 us
    pallas_call x1, Pallas kernels, local_grads(): pl.pallas_call(body, out_shape=[jax.ShapeDtypeStruct((rows // 2, 128), BF...  11.3 us
    pallas_call x1, Pallas kernels, run_near(): pl.pallas_call(near_part, out_shape=[jax.ShapeDtypeStruct(shape, BF) for...  3.04 us
    ppermute x6, waiting for transfers between devices, swap(): return lax.ppermute(values, 'space', pairs + [(j, i) for i, j in pairs])  2.43 us
  transfers between devices with their start and end apart: 6, of which 2 were waited for; matrix products, arithmetic and copies ran while one was open for 0% of the time, Pallas kernels for 4%

profile of v12, /device:TPU:1, one launch (start us, length us, event | category | flops | bytes accessed | tf_op | source)
XLA Modules:
  0.0 75.7 jit_solution(16604830079312816666)
XLA Ops:
  0.6 3.3 %collective-permute-start = (bf16[512,128]{1,0:T(8,128)(2,1)}, bf16[512,128]{1,0:T(8,128)(2,1)S(1)}, u32[]{:S(2)}, u32[]{:S(2)}) collective-permute-start(bf16[512,128]{1,0:T(8,128)(2,1)} %bitcast.15), channel_id=1, source_target_pairs={{0,1},{2,3},{4,5},{6,7},{8,9},{10,11},{12,13},{14,15},{16,17},{18,... | collective-permute-start | bytes 393224 | tf_op jit(solution)/shard_map/ppermute | solution.py:578
  4.0 1.9 %collective-permute-start.1 = (bf16[512,128]{1,0:T(8,128)(2,1)}, bf16[512,128]{1,0:T(8,128)(2,1)S(1)}, u32[]{:S(2)}, u32[]{:S(2)}) collective-permute-start(bf16[512,128]{1,0:T(8,128)(2,1)} %bitcast.16), channel_id=1, source_target_pairs={{1,2},{3,4},{5,6},{7,8},{9,10},{11,12},{13,14},{15,16},{17,18},{19... | collective-permute-start | bytes 393224 | tf_op jit(solution)/shard_map/ppermute | solution.py:578
  5.9 0.0 collective-permute-done.block.swap_core
  5.9 0.0 copy-start.4
  5.9 0.7 copy-done.4
  6.6 0.0 copy-start
  6.6 0.0 copy-start.1
  6.6 0.0 copy-start.2
  6.7 0.0 copy-start.3
  6.7 3.8 %collective-permute-start.2 = (bf16[480,128]{1,0:T(8,128)(2,1)S(1)}, bf16[480,128]{1,0:T(8,128)(2,1)S(1)}, u32[]{:S(2)}, u32[]{:S(2)}) collective-permute-start(bf16[480,128]{1,0:T(8,128)(2,1)S(1)} %relay.2), channel_id=1, source_target_pairs={{1,2},{3,4},{5,6},{7,8},{9,10},{11,12},{13,14},{15,16},{17,18},{19... | collective-permute-start | bytes 368648 | tf_op jit(solution)/shard_map/ppermute | solution.py:578
  10.4 0.0 collective-permute-done.1.block.swap_chip
  10.5 0.1 collective-permute-start.3
  10.6 0.0 copy-done
  10.6 0.0 copy-done.1
  10.6 0.0 copy-done.2
  10.6 0.0 copy-done.3
  10.6 0.0 copy-start.5
  10.6 0.0 copy-start.6
  10.7 0.0 copy-start.7
  10.7 0.0 copy-start.8
  10.7 0.0 copy-start.9
  10.7 0.0 copy-start.10
  10.7 3.0 %near_part.1 = (bf16[512,576]{1,0:T(8,128)(2,1)S(1)}, bf16[320,1440]{1,0:T(8,128)(2,1)S(1)}, bf16[256,4608]{1,0:T(8,128)(2,1)S(1)}, bf16[192,1280]{1,0:T(8,128)(...) custom-call(bf16[512,128]{1,0:T(8,128)(2,1)S(1)} %bitcast.17, ...), custom_call_target="tpu_custom_call" | custom-call | flops 3000000000 | bytes 8000000 | tf_op jit(solution)/shard_map/near_part/pallas_call | solution.py:505
  13.8 0.0 collective-permute-done.3.swap_core2
  13.8 0.0 collective-permute-done.2.swap_chip2
  13.8 0.0 copy-done.5
  13.8 0.0 copy-done.6
  13.8 0.0 copy-done.7
  13.8 0.0 copy-done.8
  13.8 0.0 copy-done.9
  13.8 0.0 copy-done.10
  13.8 11.3 %local_grads.1 = (bf16[1152,128]{1,0:T(8,128)(2,1)S(1)}, bf16[1152,128]{1,0:T(8,128)(2,1)S(1)}) custom-call(bf16[512,128]{1,0:T(8,128)(2,1)S(1)} %collective-permute-done.block.swap_core, bf16[512,128]{1,0:T(8,128)(2,1)S(1)} %collective-permute-done.1.block.swap_chip, bf16[480,128]{1,0:T(8,128)(2,1)S(1)} %collective-permute-done.2.swap_chip2, ...), custom_call_target="tpu_custom_call" | custom-call | flops 10000000000 | bytes 10000000 | tf_op jit(solution)/shard_map/local_grads/pallas_call | solution.py:522
  25.1 0.5 collective-permute-start.4
  25.7 1.2 %collective-permute-done.4 = bf16[1152,128]{1,0:T(8,128)(2,1)S(1)} collective-permute-done((bf16[1152,128]{1,0:T(8,128)(2,1)S(1)}, bf16[1152,128]{1,0:T(8,128)(2,1)S(1)}, u32[]{:S(2)}, u32[]{:S(2)}) %collective-permute-start.4) | collective-permute-done | bytes 294944 | tf_op jit(solution)/shard_map/ppermute | solution.py:578
  26.9 0.1 add_convert_fusion
  27.0 15.1 %all_to_all.15 = bf16[16,72,128]{2,1,0:T(8,128)(2,1)S(1)} all-to-all(bf16[16,72,128]{2,1,0:T(8,128)(2,1)S(1)} %bitcast.22), channel_id=1, replica_groups={{0,2,4,6,8,10,12,14,16,18,20,22,24,26,28,30},{1,3,5,7,9,11,13,15,17,19,..., dimensions={0} | all-to-all | bytes 589824 | tf_op jit(solution)/shard_map/all_to_all | solution.py:568
  42.2 16.1 %all_to_all.16 = bf16[8,72,128]{2,1,0:T(8,128)(2,1)S(1)} all-to-all(bf16[8,72,128]{2,1,0:T(8,128)(2,1)S(1)} %broadcast_in_dim.4), channel_id=1, replica_groups=mesh['sample'=8,'space'=32] {'sample'}, dimensions={0} | all-to-all | bytes 294912 | tf_op jit(solution)/shard_map/all_to_all | solution.py:562
  58.4 10.6 %all_to_all.17 = bf16[16,72,128]{2,1,0:T(8,128)(2,1)S(1)} all-to-all(bf16[16,72,128]{2,1,0:T(8,128)(2,1)S(1)} %broadcast_in_dim.5), channel_id=1, replica_groups={{0,2,4,6,8,10,12,14,16,18,20,22,24,26,28,30},{1,3,5,7,9,11,13,15,17,19,..., dimensions={0} | all-to-all | bytes 589824 | tf_op jit(solution)/shard_map/all_to_all | solution.py:568
  69.0 4.0 %collective-permute-start.5 = (bf16[1152,128]{1,0:T(8,128)(2,1)S(1)}, bf16[1152,128]{1,0:T(8,128)(2,1)S(1)}, u32[]{:S(2)}, u32[]{:S(2)}) collective-permute-start(bf16[1152,128]{1,0:T(8,128)(2,1)S(1)} %bitcast.10), channel_id=1, source_target_pairs={{0,1},{2,3},{4,5},{6,7},{8,9},{10,11},{12,13},{14,15},{16,17},{18,... | collective-permute-start | bytes 884744 | tf_op jit(solution)/shard_map/ppermute | solution.py:578
  73.0 1.2 %collective-permute-done.5.other = bf16[1152,128]{1,0:T(8,128)(2,1)S(1)} collective-permute-done((bf16[1152,128]{1,0:T(8,128)(2,1)S(1)}, bf16[1152,128]{1,0:T(8,128)(2,1)S(1)}, u32[]{:S(2)}, u32[]{:S(2)}) %collective-permute-start.5) | collective-permute-done | bytes 294944 | tf_op jit(solution)/shard_map/ppermute | solution.py:578
  74.2 1.3 %finish.1 = (f32[27,4,32]{2,1,0:T(4,128)}, f32[27,32,64]{2,1,0:T(8,128)}, f32[27,64,128]{2,1,0:T(8,128)}) custom-call(bf16[1152,128]{1,0:T(8,128)(2,1)S(1)} %bitcast.11, bf16[1152,128]{1,0:T(8,128)(2,1)S(1)} %collective-permute-done.5.other), custom_call_target="tpu_custom_call" | custom-call | tf_op jit(solution)/shard_map/finish/pallas_call | solution.py:548
  (6 shorter events, 0.2 us)
Async XLA Ops:
  0.6 5.2 %collective-permute-start = (bf16[512,128]{1,0:T(8,128)(2,1)}, bf16[512,128]{1,0:T(8,128)(2,1)S(1)}, u32[]{:S(2)}, u32[]{:S(2)}) collective-permute-start(bf16[512,128]{1,0:T(8,128)(2,1)} %bitcast.15), channel_id=1, source_target_pairs={{0,1},{2,3},{4,5},{6,7},{8,9},{10,11},{12,13},{14,15},{16,17},{18,... | collective-permute-start | bytes 393224 | tf_op jit(solution)/shard_map/ppermute | solution.py:578
  4.0 6.5 %collective-permute-start.1 = (bf16[512,128]{1,0:T(8,128)(2,1)}, bf16[512,128]{1,0:T(8,128)(2,1)S(1)}, u32[]{:S(2)}, u32[]{:S(2)}) collective-permute-start(bf16[512,128]{1,0:T(8,128)(2,1)} %bitcast.16), channel_id=1, source_target_pairs={{1,2},{3,4},{5,6},{7,8},{9,10},{11,12},{13,14},{15,16},{17,18},{19... | collective-permute-start | bytes 393224 | tf_op jit(solution)/shard_map/ppermute | solution.py:578
  5.9 0.7 copy-start.4
  6.6 4.0 %copy-start = (bf16[3,3,3,64,128]{4,3,2,1,0:T(8,128)(2,1)S(1)}, bf16[3,3,3,64,128]{4,3,2,1,0:T(8,128)(2,1)}, u32[]{:S(2)}) copy-start(bf16[3,3,3,64,128]{4,3,2,1,0:T(8,128)(2,1)} %param.15) | copy-start | bytes 1327108
  6.6 4.0 %copy-start.1 = (bf16[3,3,3,32,64]{4,3,2,1,0:T(8,128)(2,1)S(1)}, bf16[3,3,3,32,64]{4,3,2,1,0:T(8,128)(2,1)}, u32[]{:S(2)}) copy-start(bf16[3,3,3,32,64]{4,3,2,1,0:T(8,128)(2,1)} %param.14) | copy-start | bytes 331780
  6.6 4.0 %copy-start.2 = (bf16[1,8,4,16,128]{4,3,2,1,0:T(8,128)(2,1)S(1)}, bf16[1,8,4,16,128]{4,3,2,1,0:T(8,128)(2,1)}, u32[]{:S(2)}) copy-start(bf16[1,8,4,16,128]{4,3,2,1,0:T(8,128)(2,1)} %param.11) | copy-start | bytes 393220
  6.7 4.0 %copy-start.3 = (bf16[3,3,3,4,32]{4,3,2,1,0:T(4,128)(2,1)S(1)}, bf16[3,3,3,4,32]{4,3,2,1,0:T(4,128)(2,1)}, u32[]{:S(2)}) copy-start(bf16[3,3,3,4,32]{4,3,2,1,0:T(4,128)(2,1)} %param.13) | copy-start | bytes 20740
  6.7 7.1 %collective-permute-start.2 = (bf16[480,128]{1,0:T(8,128)(2,1)S(1)}, bf16[480,128]{1,0:T(8,128)(2,1)S(1)}, u32[]{:S(2)}, u32[]{:S(2)}) collective-permute-start(bf16[480,128]{1,0:T(8,128)(2,1)S(1)} %relay.2), channel_id=1, source_target_pairs={{1,2},{3,4},{5,6},{7,8},{9,10},{11,12},{13,14},{15,16},{17,18},{19... | collective-permute-start | bytes 368648 | tf_op jit(solution)/shard_map/ppermute | solution.py:578
  10.5 3.3 %collective-permute-start.3 = (bf16[480,128]{1,0:T(8,128)(2,1)S(1)}, bf16[480,128]{1,0:T(8,128)(2,1)S(1)}, u32[]{:S(2)}, u32[]{:S(2)}) collective-permute-start(bf16[480,128]{1,0:T(8,128)(2,1)S(1)} %relay.3), channel_id=1, source_target_pairs={{0,1},{2,3},{4,5},{6,7},{8,9},{10,11},{12,13},{14,15},{16,17},{18,... | collective-permute-start | bytes 368648 | tf_op jit(solution)/shard_map/ppermute | solution.py:578
  10.6 3.1 %copy-start.5 = (bf16[128,1152]{1,0:T(8,128)(2,1)S(1)}, bf16[128,1152]{1,0:T(8,128)(2,1)}, u32[]{:S(2)}) copy-start(bf16[128,1152]{1,0:T(8,128)(2,1)} %constant.18.clone.spread) | copy-start | bytes 884740
  10.6 3.1 %copy-start.6 = (bf16[256,512]{1,0:T(8,128)(2,1)S(1)}, bf16[256,512]{1,0:T(8,128)(2,1)}, u32[]{:S(2)}) copy-start(bf16[256,512]{1,0:T(8,128)(2,1)} %constant.21.clone.grow1) | copy-start | bytes 786436
  10.7 3.1 %copy-start.7 = (bf16[96,768]{1,0:T(8,128)(2,1)S(1)}, bf16[96,768]{1,0:T(8,128)(2,1)}, u32[]{:S(2)}) copy-start(bf16[96,768]{1,0:T(8,128)(2,1)} %constant.19.clone.grow_g) | copy-start | bytes 442372
  10.7 3.1 %copy-start.8 = (bf16[128,512]{1,0:T(8,128)(2,1)S(1)}, bf16[128,512]{1,0:T(8,128)(2,1)}, u32[]{:S(2)}) copy-start(bf16[128,512]{1,0:T(8,128)(2,1)} %constant.20.clone.grow2) | copy-start | bytes 393220
  10.7 3.1 %copy-start.9 = (bf16[512,128]{1,0:T(8,128)(2,1)S(1)}, bf16[512,128]{1,0:T(8,128)(2,1)}, u32[]{:S(2)}) copy-start(bf16[512,128]{1,0:T(8,128)(2,1)} %constant.17.clone.squeeze) | copy-start | bytes 393220
  10.7 3.1 %copy-start.10 = (bf16[256,128]{1,0:T(8,128)(2,1)S(1)}, bf16[256,128]{1,0:T(8,128)(2,1)}, u32[]{:S(2)}) copy-start(bf16[256,128]{1,0:T(8,128)(2,1)} %constant.16.clone.pair) | copy-start | bytes 196612
  25.1 1.8 %collective-permute-start.4 = (bf16[1152,128]{1,0:T(8,128)(2,1)S(1)}, bf16[1152,128]{1,0:T(8,128)(2,1)S(1)}, u32[]{:S(2)}, u32[]{:S(2)}) collective-permute-start(bf16[1152,128]{1,0:T(8,128)(2,1)S(1)} %get-tuple-element.25), channel_id=1, source_target_pairs={{0,1},{2,3},{4,5},{6,7},{8,9},{10,11},{12,13},{14,15},{16,17},{18,... | collective-permute-start | bytes 884744 | tf_op jit(solution)/shard_map/ppermute | solution.py:578
  69.0 5.2 %collective-permute-start.5 = (bf16[1152,128]{1,0:T(8,128)(2,1)S(1)}, bf16[1152,128]{1,0:T(8,128)(2,1)S(1)}, u32[]{:S(2)}, u32[]{:S(2)}) collective-permute-start(bf16[1152,128]{1,0:T(8,128)(2,1)S(1)} %bitcast.10), channel_id=1, source_target_pairs={{0,1},{2,3},{4,5},{6,7},{8,9},{10,11},{12,13},{14,15},{16,17},{18,... | collective-permute-start | bytes 884744 | tf_op jit(solution)/shard_map/ppermute | solution.py:578
